TPU v7x, 32 devices: a whole 2x2x4 slice. The times are simulated.
32 devices in a mesh: gx: 4 (over y, x), gy: 8 (over z, core).
Axes of the slice: x: 2, y: 2, z: 4, core: 2. Of those that a mesh axis runs over, the one named last changes fastest.
Arguments:
- vorticity: float32 [3, 128, 256, 256], P(None, 'gx', 'gy'), may hold values from -6 to 6
- velocity_old: float32 [3, 128, 256, 256], P(None, 'gx', 'gy'), may hold values from -6 to 6
- green_hat: float32 [512, 512], P(None, 'gy'), may hold values from 0.45 to 10.5, as said below
Outputs:
- vorticity_new: float32 [3, 128, 256, 256], P(None, 'gx', 'gy')
- velocity: float32 [3, 128, 256, 256], P(None, 'gx', 'gy')
Inputs may be any that keep to these rules, and one draw needn't show every extreme that they name: green_hat[(512 - m) mod (512), (512 - k) mod (512)] equals green_hat[m, k].
All inputs are finite; a program needn't handle non-finite values.
Results may differ from a plain program's by a relative error of at most 0.000059.
Values sent between devices are 32-bit elements; how exact they have to be, the bound alone decides.
No kernel may reach another device: no remote copies, remote signals or barrier semaphores. Data moves between devices by JAX's collectives and lax.ppermute only.
A program may use at most 192 MiB of HBM per device.

v0:
```python
import math

import jax
import jax.numpy as jnp
from jax import lax
from jax.sharding import PartitionSpec as P

time_step = 0.2
viscosity = 0.1
highest = lax.Precision.HIGHEST


def extended(value, sides, width):
    for axis, dim in sides:
        size, length = (lax.axis_size(axis), value.shape[dim])
        up = [(i, (i + 1) % size) for i in range(size - 1)]
        down = [(j, i) for i, j in up]
        last = lax.slice_in_dim(value, length - width, length, axis=dim)
        initial = lax.slice_in_dim(value, 0, width, axis=dim)
        before = lax.ppermute(last, axis, up)
        after = lax.ppermute(initial, axis, down)
        value = jnp.concatenate([before, value, after], axis=dim)
    return value


def phases(count_left, count_right, length):
    left = jnp.arange(count_left, dtype=jnp.int32)[:, None]
    right = jnp.arange(count_right, dtype=jnp.int32)[None, :]
    turns = left * right % length
    return turns.astype(jnp.float32) * (2.0 * math.pi / length)


def depth_next(field):
    return jnp.concatenate([field[..., 1:], jnp.zeros_like(field[..., :1])], axis=-1)


def depth_prev(field):
    return jnp.concatenate([jnp.zeros_like(field[..., :1]), field[..., :-1]], axis=-1)


def forward_depth(real_part, deep_real, deep_imaginary):

    def apply(source, matrix):
        return jnp.einsum("cxyz,zgk->cygxk", source, matrix, precision=highest)

    spectrum_real = apply(real_part, deep_real)
    spectrum_imag = apply(real_part, deep_imaginary)
    joined = jnp.stack([spectrum_real, spectrum_imag])
    sizes = joined.shape
    return joined.reshape(sizes[0], sizes[1], sizes[2], sizes[3], sizes[4] * sizes[5])


def on_device(vorticity, velocity_old, green_hat):
    groups = lax.axis_size("gy")
    planes = vorticity.shape[1]
    band = vorticity.shape[2]
    depth = vorticity.shape[3]
    across = band * groups
    padded_rows = 2 * across
    padded_depth = 2 * depth
    block = padded_depth // groups
    stacked = jnp.concatenate([vorticity, velocity_old], axis=0)
    framed = extended(stacked, (("gx", 1), ("gy", 2)), 1)
    x_plus = framed[:, 2:, 1:-1]
    x_minus = framed[:, :-2, 1:-1]
    y_plus = framed[:, 1:-1, 2:]
    y_minus = framed[:, 1:-1, :-2]
    z_plus = depth_next(stacked)
    z_minus = depth_prev(stacked)
    grad_x = 0.5 * (x_plus[3:] - x_minus[3:])
    grad_y = 0.5 * (y_plus[3:] - y_minus[3:])
    grad_z = 0.5 * (z_plus[3:] - z_minus[3:])
    stretch = vorticity[0:1] * grad_x + vorticity[1:2] * grad_y + vorticity[2:3] * grad_z
    laplace = (
        x_plus[:3]
        + x_minus[:3]
        + y_plus[:3]
        + y_minus[:3]
        + z_plus[:3]
        + z_minus[:3]
        - 6.0 * vorticity
    )
    vorticity_new = vorticity + time_step * (stretch + viscosity * laplace)
    angle_deep = phases(depth, padded_depth, padded_depth)
    deep_real = jnp.cos(angle_deep).reshape(depth, groups, block)
    deep_imaginary = (-jnp.sin(angle_deep)).reshape(depth, groups, block)
    angle_across = phases(padded_rows, across, padded_rows)
    across_real = jnp.cos(angle_across)
    across_imaginary = -jnp.sin(angle_across)
    angle_return = phases(across, padded_rows, padded_rows)
    return_real = jnp.cos(angle_return) / padded_rows
    return_imaginary = jnp.sin(angle_return) / padded_rows
    angle_shallow = phases(padded_depth, depth, padded_depth)
    shallow_real = (jnp.cos(angle_shallow) / padded_depth).reshape(groups, block, depth)
    shallow_imaginary = (jnp.sin(angle_shallow) / padded_depth).reshape(groups, block, depth)
    spectrum = forward_depth(vorticity_new, deep_real, deep_imaginary)
    kernel = jnp.tile(green_hat, (1, planes))
    received = lax.all_to_all(spectrum, "gy", split_axis=3, concat_axis=2, tiled=True)
    sizes = received.shape
    values = received.reshape(sizes[0], sizes[1], sizes[2], sizes[4])
    real_in = values[0]
    imag_in = values[1]

    def apply(matrix, source):
        return jnp.einsum("my,cyn->cmn", matrix, source, precision=highest)

    freq_real = (apply(across_real, real_in) - apply(across_imaginary, imag_in)) * kernel
    freq_imag = (apply(across_real, imag_in) + apply(across_imaginary, real_in)) * kernel
    rows_real = apply(return_real, freq_real) - apply(return_imaginary, freq_imag)
    rows_imag = apply(return_real, freq_imag) + apply(return_imaginary, freq_real)
    result = jnp.stack([rows_real, rows_imag])
    returned = lax.all_to_all(
        result.reshape(2, result.shape[1], result.shape[2], 1, result.shape[3]),
        "gy",
        split_axis=2,
        concat_axis=3,
        tiled=True,
    )
    shaped = returned.reshape(2, 3, band, groups, planes, block)

    def inverse(source, matrix):
        return jnp.einsum("cygxk,gkz->cxyz", source, matrix, precision=highest)

    stream_real = inverse(shaped[0], shallow_real) - inverse(shaped[1], shallow_imaginary)
    framed_stream = extended(stream_real, (("gx", 1), ("gy", 2)), 1)
    stream_dx = 0.5 * (framed_stream[:, 2:, 1:-1] - framed_stream[:, :-2, 1:-1])
    stream_dy = 0.5 * (framed_stream[:, 1:-1, 2:] - framed_stream[:, 1:-1, :-2])
    stream_dz = 0.5 * (depth_next(stream_real) - depth_prev(stream_real))
    velocity = jnp.stack(
        [stream_dy[2] - stream_dz[1], stream_dz[0] - stream_dx[2], stream_dx[1] - stream_dy[0]]
    )
    return (vorticity_new, velocity)


def solution(mesh):
    placed = (P(None, "gx", "gy", None), P(None, "gx", "gy", None), P(None, "gy"))
    return jax.shard_map(
        on_device,
        mesh=mesh,
        in_specs=placed,
        out_specs=(P(None, "gx", "gy", None), P(None, "gx", "gy", None)),
        check_vma=False,
    )
```

profile of v0, /device:TPU:10, one launch (start us, length us, event | category | flops | bytes accessed | tf_op | source)
XLA Modules:
  0.0 1097.4 jit_solution(14312350249966847817)
XLA Ops:
  0.6 2.4 constant_dynamic-update-slice_fusion.1
  4.6 3.4 collective-permute-start.1
  8.0 2.5 collective-permute-start
  10.4 6.8 fusion.147
  19.2 2.2 collective-permute-start.3
  21.4 3.9 collective-permute-start.2
  25.3 1.8 multiply_bitcast_fusion.2
  27.3 1.5 collective-permute-done.2
  29.7 19.3 %fusion.5 = f32[3,32,32,256]{3,2,1,0:T(8,128)} fusion(f32[3,32,32,256]{3,2,1,0:T(8,128)S(1)} %copy-done.3, f32[6,32,32,255]{3,2,1,0:T(8,128)} %get-tuple-element.19, f32[6,32,32,255]{3,2,1,0:T(8,128)} %get-tuple-element.18, f32[6,34,1,256]{3,2,1,0:T(1,128)S(1)} %copy.46, f32[6,1,32,256]{3,2,1,0:T(8,128)} %copy-done.9, f32[6,32,32,256]{3,2,1,0:T(8,128)} %copy-done, ...), kind=kLoop, calls=%fused_computation.18 | loop fusion | flops 27525120 | bytes 29073408 | tf_op jit(solution)/shard_map/add | solution.py:83
  48.9 19.8 %convolution_bitcast_fusion = f32[3,32,8,32,64]{4,1,3,0,2:T(8,128)} fusion(f32[3,32,32,256]{3,2,1,0:T(8,128)} %fusion.5, s32[8,64]{1,0:T(8,128)S(1)} %multiply_add_fusion), kind=kOutput, calls=%fused_computation.11 | convolution fusion | flops 4833804288 | bytes 9439232 | tf_op jit(solution)/shard_map/cxyz,zgk->cygxk/dot_general | solution.py:44
  68.8 19.0 %convolution_bitcast_fusion.1 = f32[3,32,8,32,64]{4,1,3,0,2:T(8,128)} fusion(f32[3,32,32,256]{3,2,1,0:T(8,128)S(1)} %copy-done.4, s32[8,64]{1,0:T(8,128)S(1)} %multiply_add_fusion), kind=kOutput, calls=%fused_computation.12 | convolution fusion | flops 4833673216 | bytes 9439232 | tf_op jit(solution)/shard_map/cxyz,zgk->cygxk/dot_general | solution.py:44
  87.7 16.5 %copy.48 = f32[3,32,8,32,64]{4,3,2,1,0:T(8,128)} copy(f32[3,32,8,32,64]{4,1,3,0,2:T(8,128)} %convolution_bitcast_fusion) | data formatting | bytes 12582912 | tf_op jit(solution)/shard_map/cxyz,zgk->cygxk/transpose | solution.py:44
  104.2 12.3 %stack.25 = f32[1,3,32,8,2048]{4,3,2,1,0:T(8,128)} reshape(f32[3,32,8,32,64]{4,3,2,1,0:T(8,128)} %copy.48) | data formatting | bytes 12582912 | tf_op jit(solution)/shard_map/stack | solution.py:48
  116.5 16.4 %copy.47 = f32[3,32,8,32,64]{4,3,2,1,0:T(8,128)} copy(f32[3,32,8,32,64]{4,1,3,0,2:T(8,128)} %convolution_bitcast_fusion.1) | data formatting | bytes 12582912 | tf_op jit(solution)/shard_map/cxyz,zgk->cygxk/transpose | solution.py:44
  132.9 11.9 %stack.24 = f32[1,3,32,8,2048]{4,3,2,1,0:T(8,128)} reshape(f32[3,32,8,32,64]{4,3,2,1,0:T(8,128)} %copy.47) | data formatting | bytes 12582912 | tf_op jit(solution)/shard_map/stack | solution.py:48
  144.8 11.3 %pad_maximum_fusion = f32[2,3,32,8,2048]{4,3,2,1,0:T(8,128)} fusion(f32[1,3,32,8,2048]{4,3,2,1,0:T(8,128)} %stack.25, f32[1,3,32,8,2048]{4,3,2,1,0:T(8,128)} %stack.24), kind=kLoop, calls=%fused_computation | loop fusion | flops 3145728 | bytes 25165824 | tf_op jit(solution)/shard_map/stack | solution.py:48
  156.1 16.4 %copy.49 = f32[2,3,32,8,2048]{4,2,1,0,3:T(8,128)} copy(f32[2,3,32,8,2048]{4,3,2,1,0:T(8,128)} %pad_maximum_fusion) | data formatting | bytes 25165824 | tf_op jit(solution)/shard_map/stack | solution.py:48
  172.5 279.2 %all_to_all.30 = f32[2,3,32,8,2048]{4,2,1,0,3:T(8,128)} all-to-all(f32[2,3,32,8,2048]{4,2,1,0,3:T(8,128)} %copy.49), channel_id=1, replica_groups=mesh['gx'=4,'gy'=8] {'gy'}, dimensions={3} | all-to-all | bytes 25165824 | tf_op jit(solution)/shard_map/all_to_all | solution.py:98
  451.7 11.3 %copy.71 = f32[2,3,32,8,2048]{4,2,3,1,0:T(8,128)} copy(f32[2,3,32,8,2048]{4,2,1,0,3:T(8,128)} %all_to_all.30) | data formatting | bytes 25165824 | tf_op jit(solution)/shard_map/all_to_all | solution.py:98
  463.0 8.9 fusion.145
  472.0 28.1 %fusion.48 = f32[3,2048,512]{2,1,0:T(8,128)} fusion(f32[3,256,2048]{2,1,0:T(8,128)S(1)} %bitcast.116), kind=kOutput, calls=%fused_computation.100 | convolution fusion | flops 9665511424 | bytes 18874368 | tf_op jit(solution)/shard_map/my,cyn->cmn/dot_general | solution.py:105
  500.1 28.6 %fusion.50 = f32[3,2048,512]{2,1,0:T(8,128)} fusion(f32[3,256,2048]{2,1,0:T(8,128)S(1)} %bitcast.121), kind=kOutput, calls=%fused_computation.102 | convolution fusion | flops 9665511424 | bytes 18874368 | tf_op jit(solution)/shard_map/my,cyn->cmn/dot_general | solution.py:105
  528.7 2.5 tile.8
  531.2 29.9 %bitcast_multiply_fusion = f32[3,512,2048]{1,2,0:T(8,128)S(1)} fusion(f32[3,2048,512]{2,1,0:T(8,128)} %fusion.48, f32[512,2048]{0,1:T(8,128)} %bitcast.122, f32[3,256,2048]{2,1,0:T(8,128)} %bitcast.118), kind=kOutput, calls=%fused_computation.2 | convolution fusion | flops 9671933952 | bytes 35651584 | tf_op jit(solution)/shard_map/my,cyn->cmn/dot_general | solution.py:105
  561.1 30.2 %bitcast_multiply_fusion.1 = f32[3,512,2048]{1,2,0:T(8,128)} fusion(f32[3,2048,512]{2,1,0:T(8,128)} %fusion.50, f32[512,2048]{0,1:T(8,128)} %bitcast.123, f32[3,256,2048]{2,1,0:T(8,128)} %bitcast.117), kind=kOutput, calls=%fused_computation.3 | convolution fusion | flops 9671933952 | bytes 35651584 | tf_op jit(solution)/shard_map/my,cyn->cmn/dot_general | solution.py:105
  591.3 18.7 %fusion.44 = f32[3,2048,256]{2,1,0:T(8,128)} fusion(f32[3,512,2048]{1,2,0:T(8,128)} %bitcast_multiply_fusion.1), kind=kOutput, calls=%fused_computation.96 | convolution fusion | flops 9665642496 | bytes 18874368 | tf_op jit(solution)/shard_map/my,cyn->cmn/dot_general | solution.py:105
  610.1 13.3 %fusion.42 = f32[3,2048,256]{2,1,0:T(8,128)S(1)} fusion(f32[3,512,2048]{1,2,0:T(8,128)S(1)} %bitcast_multiply_fusion), kind=kOutput, calls=%fused_computation.94 | convolution fusion | flops 9665642496 | bytes 18874368 | tf_op jit(solution)/shard_map/my,cyn->cmn/dot_general | solution.py:105
  623.4 19.2 %subtract_bitcast_fusion = f32[1,3,256,2048]{2,3,1,0:T(8,128)} fusion(f32[3,2048,256]{2,1,0:T(8,128)} %fusion.44, f32[3,512,2048]{1,2,0:T(8,128)S(1)} %bitcast_multiply_fusion), kind=kOutput, calls=%fused_computation.6 | convolution fusion | flops 9667215360 | bytes 25165824 | tf_op jit(solution)/shard_map/my,cyn->cmn/dot_general | solution.py:105
  642.6 19.1 %add_bitcast_fusion = f32[1,3,256,2048]{2,3,1,0:T(8,128)} fusion(f32[3,2048,256]{2,1,0:T(8,128)S(1)} %fusion.42, f32[3,512,2048]{1,2,0:T(8,128)} %bitcast_multiply_fusion.1), kind=kOutput, calls=%fused_computation.5 | convolution fusion | flops 9667215360 | bytes 25165824 | tf_op jit(solution)/shard_map/my,cyn->cmn/dot_general | solution.py:105
  661.7 8.9 maximum_bitcast_fusion
  670.6 19.5 %copy.55 = f32[2,3,256,1,2048]{4,0,3,1,2:T(2,128)} copy(f32[2,3,256,1,2048]{2,4,1,0,3:T(8,128)} %maximum_bitcast_fusion) | data formatting | bytes 25165824 | tf_op jit(solution)/shard_map/reshape | solution.py:113
  690.1 279.9 %all_to_all.31 = f32[2,3,256,1,2048]{4,0,3,1,2:T(2,128)} all-to-all(f32[2,3,256,1,2048]{4,0,3,1,2:T(2,128)} %copy.55), channel_id=1, replica_groups=mesh['gx'=4,'gy'=8] {'gy'}, dimensions={2} | all-to-all | bytes 25165824 | tf_op jit(solution)/shard_map/all_to_all | solution.py:112
  970.1 16.4 %copy.56 = f32[2,3,256,1,2048]{4,2,1,0,3:T(8,128)} copy(f32[2,3,256,1,2048]{4,0,3,1,2:T(2,128)} %all_to_all.31) | data formatting | bytes 25165824 | tf_op jit(solution)/shard_map/all_to_all | solution.py:112
  986.5 8.9 fusion.144
  995.4 6.5 copy.58
  1001.8 11.4 %squeeze.21 = f32[3,32,8,32,64]{4,3,2,1,0:T(8,128)} reshape(f32[1,3,32,8,1,2048]{5,3,2,1,4,0:T(8,128)} %copy.58) | data formatting | bytes 12582912 | tf_op jit(solution)/shard_map/squeeze | solution.py:124
  1013.2 9.1 copy.57
  1022.3 11.4 %squeeze.20 = f32[3,32,8,32,64]{4,3,2,1,0:T(8,128)} reshape(f32[1,3,32,8,1,2048]{5,3,2,1,4,0:T(8,128)} %copy.57) | data formatting | bytes 12582912 | tf_op jit(solution)/shard_map/squeeze | solution.py:124
  1033.8 18.3 %fusion.38 = f32[256,3,32,32,1]{0,3,4,2,1:T(8,128)S(1)} fusion(f32[3,32,8,32,64]{4,3,2,1,0:T(8,128)} %squeeze.20, s32[8,64]{1,0:T(8,128)S(1)} %copy-done.8), kind=kOutput, calls=%fused_computation.90 | convolution fusion | flops 4833804288 | bytes 9439232 | tf_op jit(solution)/shard_map/cygxk,gkz->cxyz/dot_general | solution.py:122
  1052.0 18.4 %fusion.20 = f32[3,32,32,256]{3,1,2,0:T(8,128)S(1)} fusion(f32[256,3,32,32,1]{0,3,4,2,1:T(8,128)S(1)} %fusion.38, f32[3,32,8,32,64]{4,3,2,1,0:T(8,128)} %squeeze.21, s32[8,64]{1,0:T(8,128)S(1)} %copy-done.8), kind=kOutput, calls=%fused_computation.53 | convolution fusion | flops 4834590720 | bytes 12584960 | tf_op jit(solution)/shard_map/cygxk,gkz->cxyz/dot_general | solution.py:122
  1070.6 3.1 collective-permute-start.4
  1073.7 3.0 collective-permute-start.5
  1078.0 3.1 collective-permute-done.5
  1081.1 1.9 collective-permute-start.6
  1083.1 2.4 collective-permute-start.7
  1086.4 3.7 collective-permute-done.7
  1090.0 2.3 fusion.11
  1093.4 3.5 copy.59
  (46 shorter events, 8.0 us)
Async XLA Ops:
  0.6 2.8 copy-start.6
  3.7 14.8 %copy-start = (f32[6,32,32,256]{3,2,1,0:T(8,128)}, f32[6,32,32,256]{3,2,1,0:T(8,128)S(1)}, u32[]{:S(2)}) copy-start(f32[6,32,32,256]{3,2,1,0:T(8,128)S(1)} %constant_dynamic-update-slice_fusion) | copy-start | bytes 18874372
  4.6 12.7 %collective-permute-start.1 = (f32[6,1,32,256]{3,2,1,0:T(8,128)}, f32[6,1,32,256]{3,2,1,0:T(8,128)S(1)}, u32[]{:S(2)}, u32[]{:S(2)}) collective-permute-start(f32[6,1,32,256]{3,2,1,0:T(8,128)} %get-tuple-element.16), channel_id=1, source_target_pairs={{0,8},{8,16},{16,24},{1,9},{9,17},{17,25},{2,10},{10,18},{18,26},{... | collective-permute-start | bytes 589832 | tf_op jit(solution)/shard_map/ppermute | solution.py:20
  8.0 10.5 collective-permute-start
  17.2 8.0 copy-start.2
  18.5 0.7 copy-start.9
  19.2 10.5 copy-start.3
  19.2 7.8 collective-permute-start.3
  21.4 7.3 collective-permute-start.2
  27.1 41.7 %copy-start.7 = (s32[8,64]{1,0:T(8,128)}, s32[8,64]{1,0:T(8,128)S(1)}, u32[]{:S(2)}) copy-start(s32[8,64]{1,0:T(8,128)S(1)} %multiply_add_fusion) | copy-start | bytes 6148
  48.9 19.9 %copy-start.4 = (f32[3,32,32,256]{3,2,1,0:T(8,128)S(1)}, f32[3,32,32,256]{3,2,1,0:T(8,128)}, u32[]{:S(2)}) copy-start(f32[3,32,32,256]{3,2,1,0:T(8,128)} %fusion.5) | copy-start | bytes 9437188
  472.0 28.1 %copy-start.1 = (f32[1,3,8,32,1,2048]{5,3,2,1,4,0:T(8,128)}, f32[1,3,8,32,1,2048]{5,3,2,1,4,0:T(8,128)S(1)}, u32[]{:S(2)}) copy-start(f32[1,3,8,32,1,2048]{5,3,2,1,4,0:T(8,128)S(1)} %get-tuple-element.13) | copy-start | bytes 18874372
  472.0 28.1 %slice-start = ((s8[6291456]{0:T(1024)(128)(4,1)}), s8[4194304]{0:T(1024)(128)(4,1)S(1)}, s32[]{:S(2)}) async-start(s8[6291456]{0:T(1024)(128)(4,1)} %bitcast.119), calls=%async_computation.2 | async-start | bytes 8388608
  472.0 28.1 %slice-start.1 = ((s8[6291456]{0:T(1024)(128)(4,1)}), s8[2097152]{0:T(1024)(128)(4,1)S(1)}, s32[]{:S(2)}) async-start(s8[6291456]{0:T(1024)(128)(4,1)} %bitcast.119), calls=%async_computation.3 | async-start | bytes 4194304
  500.1 28.6 %copy-start.10 = (f32[512,64]{0,1:T(8,128)S(1)}, f32[512,64]{0,1:T(8,128)}, u32[]{:S(2)}) copy-start(f32[512,64]{0,1:T(8,128)} %param.5) | copy-start | bytes 393220
  642.6 19.1 %copy-start.5 = (f32[1,3,256,2048]{2,3,1,0:T(8,128)S(1)}, f32[1,3,256,2048]{2,3,1,0:T(8,128)}, u32[]{:S(2)}) copy-start(f32[1,3,256,2048]{2,3,1,0:T(8,128)} %subtract_bitcast_fusion) | copy-start | bytes 18874372
  1022.3 11.4 %copy-start.8 = (s32[8,64]{1,0:T(8,128)S(1)}, s32[8,64]{1,0:T(8,128)}, u32[]{:S(2)}) copy-start(s32[8,64]{1,0:T(8,128)} %copy-done.7) | copy-start | bytes 6148
  1070.6 7.4 collective-permute-start.4
  1073.7 7.4 collective-permute-start.5
  1081.1 5.2 collective-permute-start.6
  1083.1 6.9 collective-permute-start.7
where the time goes:
time: 1100 us
  blocking collectives  559 us (51%)
  matrix products  263 us (24%)
  local copies, waits for them, and re-layouts  197 us (18%)
  other arithmetic  45.8 us (4%)
  starting transfers between devices  22.3 us (2%)
    all_to_all x1, blocking collectives, on_device(): lax.all_to_all(result.reshape(2, result.shape[1], result.shape[2], 1, res...  280 us
    all_to_all x1, blocking collectives, on_device(): lax.all_to_all(spectrum, 'gy', split_axis=3, concat_axis=2, tiled=True)  279 us
    dot_general x8, matrix products, apply(): return jnp.einsum('my,cyn->cmn', matrix, source, precision=highest)  187 us
    another operation x3, local copies, waits for them, and re-layouts, forward_depth(): joined = jnp.stack([spectrum_real, spectrum_imag])  40.6 us
    dot_general x2, matrix products, apply(): return jnp.einsum('cxyz,zgk->cygxk', source, matrix, precision=highest)  38.8 us
    dot_general x2, matrix products, inverse(): return jnp.einsum('cygxk,gkz->cxyz', source, matrix, precision=highest)  36.6 us
    transpose x2, local copies, waits for them, and re-layouts, apply(): return jnp.einsum('cxyz,zgk->cygxk', source, matrix, precision=highest)  32.8 us
  transfers between devices with their start and end apart: 8, of which 4 were waited for; matrix products, arithmetic and copies ran while one was open for 1% of the time, Pallas kernels for 0%

commit v1 on v0

v1 whole, which is shorter than its diff:
```python
import functools
import math

import jax
import jax.numpy as jnp
import ml_dtypes
import numpy as np
from jax import lax
from jax.experimental import pallas as pl
from jax.experimental.pallas import tpu as pltpu
from jax.sharding import PartitionSpec as P

time_step = 0.2
viscosity = 0.1
radix = 4
VMEM = pltpu.VMEM
SMEM = pltpu.SMEM
limit = 56 * 1024 * 1024


def params():
    return pltpu.CompilerParams(vmem_limit_bytes=limit)


def in_vmem(count):
    return [pl.BlockSpec(memory_space=VMEM)] * count


def halves_np(matrix, axis):


    value = np.asarray(matrix, np.float32)
    high = value.astype(ml_dtypes.bfloat16)
    low = (value - high.astype(np.float32)).astype(ml_dtypes.bfloat16)
    return np.concatenate([high, high, low], axis=axis)


def parts(value, axis):
    high = value.astype(jnp.bfloat16)
    low = (value - high.astype(jnp.float32)).astype(jnp.bfloat16)
    return jnp.concatenate([high, low, high], axis=axis)


@functools.lru_cache(maxsize=None)
def constants(rows, depth):
    long_z, long_y = 2 * depth, 2 * rows
    half = long_y // radix
    k = np.arange(depth)[:, None]
    z = np.arange(depth)[None, :]
    turn = 2.0 * np.pi * (((2 * k + 1) * z) % (2 * long_z)) / (2 * long_z)
    forward_z = halves_np(np.concatenate([np.cos(turn), -np.sin(turn)], axis=0), 1)
    inverse_z = np.concatenate([np.cos(turn), -np.sin(turn)], axis=0) * (2.0 / long_z)
    inverse_z = halves_np(inverse_z.T, 1)
    b = np.arange(half)[:, None]
    p = np.arange(half)[None, :]
    ahead, back = [], []
    for q in range(radix):
        angle = 2.0 * np.pi * ((b * (radix * p + q)) % long_y) / long_y
        c, s = np.cos(angle), np.sin(angle)
        ahead.append(halves_np(np.block([[c, -s], [s, c]]), 0))
        c, s = c.T / long_y, s.T / long_y
        back.append(halves_np(np.block([[c, s], [-s, c]]), 0))
    shift = np.arange(depth)[:, None] + 0.5 - np.arange(long_z)[None, :]
    d = np.arange(1, depth)
    table = 1.0 + 2.0 * np.cos(2.0 * np.pi * np.arange(-2 * long_z, 2 * long_z)[:, None] * d[None, :] / (2 * long_z)).sum(1)
    index = np.rint(2 * shift).astype(np.int64) + 2 * long_z
    dirichlet = (table[index] / long_z).astype(np.float32)
    return forward_z, inverse_z, np.stack(ahead), np.stack(back), dirichlet


def plane_of(owner, chunk, local, chunks, width):
    if chunks == 1:
        return owner * width + local
    return owner * width * chunks + lax.bitwise_xor(owner & 1, chunk) * width + local


def advance_kernel(chunk, chunks, whole, me_ref, vort, vel, ylo, yhi, xlo, xhi, *rest):
    _, planes, band, depth = vort.shape
    if whole:
        new, sends = rest[0], rest[1:]
    else:
        sends, new = rest[:-1], rest[-1]
    groups = len(sends)
    width = sends[0].shape[1]
    me = me_ref[0]
    row = lax.broadcasted_iota(jnp.int32, (band, depth), 0)
    column = lax.broadcasted_iota(jnp.int32, (band, depth), 1)
    first_row, last_row = row == 0, row == band - 1
    first_column, last_column = column == 0, column == depth - 1

    def neighbours(source, comp, slot, x):
        here = source[comp, x]
        before = jnp.where(x > 0, source[comp, jnp.maximum(x - 1, 0)], xlo[slot])
        after = jnp.where(x < planes - 1, source[comp, jnp.minimum(x + 1, planes - 1)], xhi[slot])
        down = jnp.where(first_row, ylo[slot, pl.ds(x, 1), :], pltpu.roll(here, 1, 0))
        up = jnp.where(last_row, yhi[slot, pl.ds(x, 1), :], pltpu.roll(here, band - 1, 0))
        left = jnp.where(first_column, 0.0, pltpu.roll(here, 1, 1))
        right = jnp.where(last_column, 0.0, pltpu.roll(here, depth - 1, 1))
        return here, after, before, up, down, right, left

    def step(t, carry):
        if whole:
            x = t
        else:
            x = plane_of(t // width, chunk, t % width, chunks, width)
        w = [vort[c, x] for c in range(3)]
        for c in range(3):
            _, xp, xm, yp, ym, zp, zm = neighbours(vel, c, 3 + c, x)
            stretch = 0.5 * (w[0] * (xp - xm) + w[1] * (yp - ym) + w[2] * (zp - zm))
            here, xp, xm, yp, ym, zp, zm = neighbours(vort, c, c, x)
            laplace = xp + xm + yp + ym + zp + zm - 6.0 * here
            new[c, x] = here + time_step * (stretch + viscosity * laplace)
        return carry

    lax.fori_loop(0, planes if whole else groups * width, step, 0)
    for d in range(groups):
        owner = lax.bitwise_xor(me, d)
        for s in range(width):
            x = plane_of(owner, chunk, s, chunks, width)
            for c in range(3):
                sends[d][c, s] = new[c, x]


def advance(chunk, chunks, whole, me, groups, vort, vel, halos):
    _, planes, band, depth = vort.shape
    width = planes // groups // chunks
    block = jax.ShapeDtypeStruct((3, width, band, depth), jnp.float32)
    shapes = [block] * groups
    scratch = []
    if whole:
        shapes = [jax.ShapeDtypeStruct(vort.shape, jnp.float32)] + shapes
    else:
        scratch = [pltpu.VMEM(vort.shape, jnp.float32)]
    return pl.pallas_call(
        functools.partial(advance_kernel, chunk, chunks, whole),
        out_shape=shapes,
        in_specs=[pl.BlockSpec(memory_space=SMEM)] + in_vmem(6),
        out_specs=in_vmem(len(shapes)),
        scratch_shapes=scratch,
        compiler_params=params(),
        name=f"advance_{chunk}",
    )(me, vort, vel, *halos)


def solve_kernel(groups, me_ref, fz, bz, ey, by, green, *refs):
    sources, targets = refs[:groups], refs[groups : 2 * groups]
    plane, psi = refs[2 * groups :]
    _, width, band, depth = sources[0].shape
    rows = band * groups
    half = rows // 2
    me = me_ref[0]
    pad = 8
    halo_base = 3 * width * band
    zeros = jnp.zeros((pad, depth), jnp.float32)
    psi[pl.ds(0, pad), :] = zeros
    psi[pl.ds(pad + rows, pad), :] = zeros

    def step(t, carry):
        c, s = t // width, t % width
        for d in range(groups):
            start = pl.multiple_of(lax.bitwise_xor(me, d) * band, band)
            plane[pl.ds(start, band), :] = sources[d][c, s]
        spectrum = lax.dot_general(
            fz[...], parts(plane[...], 1), (((1,), (1,)), ((), ())), preferred_element_type=jnp.float32
        )
        low_r, high_r = spectrum[:depth, :half], spectrum[:depth, half:]
        low_i, high_i = spectrum[depth:, :half], spectrum[depth:, half:]
        turned = [
            (low_r + high_r, low_i + high_i),
            (low_r + high_i, low_i - high_r),
            (low_r - high_r, low_i - high_i),
            (low_r - high_i, low_i + high_r),
        ]
        total = None
        for q in range(radix):
            data = parts(jnp.concatenate(turned[q], axis=1), 1)
            freq = jnp.dot(data, ey[q], preferred_element_type=jnp.float32)
            gain = green[:, q * half : (q + 1) * half]
            freq = jnp.concatenate([freq[:, :half] * gain, freq[:, half:] * gain], axis=1)
            out = jnp.dot(parts(freq, 1), by[q], preferred_element_type=jnp.float32)
            re, im = out[:, :half], out[:, half:]
            second = [(re, im), (-im, re), (-re, -im), (im, -re)][q]
            mine = (re, im) + second
            total = mine if total is None else tuple(a + b for a, b in zip(total, mine))
        stacked = jnp.concatenate(
            [jnp.concatenate([total[0], total[2]], axis=1), jnp.concatenate([total[1], total[3]], axis=1)], axis=0
        )
        result = jnp.dot(bz[...], parts(stacked, 0), preferred_element_type=jnp.float32)
        psi[pl.ds(pad, rows), :] = result.T
        offset = pl.multiple_of((c * width + s) * band, band)
        edge = halo_base + ((c // 2) * width + s) * 2
        for d in range(groups):
            start = lax.bitwise_xor(me, d) * band
            targets[d][pl.ds(offset, band), :] = psi[pl.ds(pl.multiple_of(start + pad, pad), band), :]

            @pl.when(c != 1)
            def _():
                targets[d][pl.ds(edge, 1), :] = psi[pl.ds(start + pad - 1, 1), :]
                targets[d][pl.ds(edge + 1, 1), :] = psi[pl.ds(start + pad + band, 1), :]

        return carry

    lax.fori_loop(0, 3 * width, step, 0)


def solve(me, green, tables, blocks):
    groups = len(blocks)
    _, width, band, depth = blocks[0].shape
    rows = band * groups
    lines = 3 * width * band + 4 * width
    shape = jax.ShapeDtypeStruct((lines, depth), jnp.float32)
    return pl.pallas_call(
        functools.partial(solve_kernel, groups),
        out_shape=[shape] * groups,
        in_specs=[pl.BlockSpec(memory_space=SMEM)] + in_vmem(5 + groups),
        out_specs=in_vmem(groups),
        scratch_shapes=[pltpu.VMEM((rows, depth), jnp.float32), pltpu.VMEM((rows + 16, depth), jnp.float32)],
        compiler_params=params(),
        name="solve",
    )(me, *tables, green, *blocks)


def curl_kernel(groups, chunks, band, width, me_ref, xlo, xhi, *refs):
    blocks = refs[: groups * chunks]
    velocity, psi, edge = refs[groups * chunks :]
    planes, depth = velocity.shape[1], velocity.shape[3]
    me = me_ref[0]
    halo_base = 3 * width * band
    for k in range(chunks):
        for d in range(groups):
            owner = lax.bitwise_xor(me, d)
            block = blocks[k * groups + d]
            for s in range(width):
                x = plane_of(owner, k, s, chunks, width)
                for c in range(3):
                    psi[c, x + 1] = block[pl.ds((c * width + s) * band, band), :]
                for h in range(2):
                    edge[h, x] = block[pl.ds(halo_base + (h * width + s) * 2, 2), :]
    for h in range(2):
        psi[h + 1, 0] = xlo[h]
        psi[h + 1, planes + 1] = xhi[h]
    row = lax.broadcasted_iota(jnp.int32, (band, depth), 0)
    column = lax.broadcasted_iota(jnp.int32, (band, depth), 1)
    first_row, last_row = row == 0, row == band - 1
    first_column, last_column = column == 0, column == depth - 1

    def along_y(here, ends):
        down = jnp.where(first_row, ends[0:1], pltpu.roll(here, 1, 0))
        up = jnp.where(last_row, ends[1:2], pltpu.roll(here, band - 1, 0))
        return up - down

    def along_z(here):
        left = jnp.where(first_column, 0.0, pltpu.roll(here, 1, 1))
        right = jnp.where(last_column, 0.0, pltpu.roll(here, depth - 1, 1))
        return right - left

    def step(x, carry):
        px, py, pz = psi[0, x + 1], psi[1, x + 1], psi[2, x + 1]
        velocity[0, x] = 0.5 * (along_y(pz, edge[1, x]) - along_z(py))
        velocity[1, x] = 0.5 * (along_z(px) - (psi[2, x + 2] - psi[2, x]))
        velocity[2, x] = 0.5 * ((psi[1, x + 2] - psi[1, x]) - along_y(px, edge[0, x]))
        return carry

    lax.fori_loop(0, planes, step, 0)


def curl(me, groups, chunks, shape, edges, blocks):
    _, planes, band, depth = shape
    width = planes // groups // chunks
    return pl.pallas_call(
        functools.partial(curl_kernel, groups, chunks, band, width),
        out_shape=jax.ShapeDtypeStruct(shape, jnp.float32),
        in_specs=[pl.BlockSpec(memory_space=SMEM)] + in_vmem(2 + len(blocks)),
        out_specs=pl.BlockSpec(memory_space=VMEM),
        scratch_shapes=[
            pltpu.VMEM((3, planes + 2, band, depth), jnp.float32),
            pltpu.VMEM((2, planes, 2, depth), jnp.float32),
        ],
        compiler_params=params(),
        name="curl",
    )(me, *edges, *blocks)


def pairs(size, step):
    return [(i, i + step) for i in range(size) if 0 <= i + step < size]


def swap(blocks):
    groups = len(blocks)
    moved = [blocks[0]] + [None] * (groups - 1)
    order = sorted(range(1, groups), reverse=True)
    for d in order:
        moved[d] = lax.ppermute(blocks[d], "gy", [(i, i ^ d) for i in range(groups)])
    return moved


def on_device(vorticity, velocity_old, green_hat):
    groups = lax.axis_size("gy")
    across_x = lax.axis_size("gx")
    _, planes, band, depth = vorticity.shape
    rows = band * groups
    per_owner = planes // groups
    chunks = 2 if per_owner % 2 == 0 else 1
    width = per_owner // chunks
    me = lax.axis_index("gy")
    me_array = me.reshape(1)

    fields = (vorticity, velocity_old)
    first_rows = jnp.concatenate([f[:, :, 0] for f in fields], axis=0)
    last_rows = jnp.concatenate([f[:, :, band - 1] for f in fields], axis=0)
    first_x = jnp.concatenate([f[:, 0] for f in fields], axis=0)
    last_x = jnp.concatenate([f[:, planes - 1] for f in fields], axis=0)
    halos = (
        lax.ppermute(last_rows, "gy", pairs(groups, 1)),
        lax.ppermute(first_rows, "gy", pairs(groups, -1)),
        lax.ppermute(last_x, "gx", pairs(across_x, 1)),
        lax.ppermute(first_x, "gx", pairs(across_x, -1)),
    )

    forward_z, inverse_z, ahead, back, dirichlet = constants(rows, depth)
    tables = (jnp.asarray(forward_z), jnp.asarray(inverse_z), jnp.asarray(ahead), jnp.asarray(back))
    gathered = lax.all_gather(green_hat, "gy", axis=1, tiled=True)
    arranged = gathered.reshape(2 * rows // radix, radix, 2 * depth)
    green = jnp.einsum("kj,pqj->kqp", jnp.asarray(dirichlet), arranged, precision=lax.Precision.HIGHEST)
    green = green.reshape(depth, 2 * rows)

    received = []
    vorticity_new = None
    for k in range(chunks):
        whole = k == chunks - 1
        outs = advance(k, chunks, whole, me_array, groups, vorticity, velocity_old, halos)
        if whole:
            vorticity_new, outs = outs[0], outs[1:]
        received.append(swap(list(outs)))
    returned = []
    for k in range(chunks):
        solved = solve(me_array, green, tables, received[k])
        returned.append(swap(list(solved)))

    lines = slice(width * band, 3 * width * band)

    def plane_at(x):
        owner = x // per_owner
        local = x % per_owner
        k = (local // width) ^ (owner & 1) if chunks == 2 else 0
        picked = lax.select_n(lax.bitwise_xor(me, owner), *[
            block[lines].reshape(2, width, band, depth)[:, local % width] for block in returned[k]
        ])
        return picked

    edges = (
        lax.ppermute(plane_at(planes - 1), "gx", pairs(across_x, 1)),
        lax.ppermute(plane_at(0), "gx", pairs(across_x, -1)),
    )
    blocks = [block for group in returned for block in group]
    velocity = curl(me_array, groups, chunks, vorticity.shape, edges, blocks)
    return vorticity_new, velocity


def solution(mesh):
    placed = P(None, "gx", "gy", None)
    return jax.shard_map(
        on_device,
        mesh=mesh,
        in_specs=(placed, placed, P(None, "gy")),
        out_specs=(placed, placed),
        check_vma=False,
    )
```

time: 1100 us -> 220 us (0.20)
  blocking collectives: 559 us -> 0 us
  matrix products: 263 us -> 1.17 us
  local copies, waits for them, and re-layouts: 197 us -> 10.2 us
  waiting for transfers between devices: 9.47 us -> 82 us
  Pallas kernels: 0 us -> 64.9 us
  other arithmetic: 45.8 us -> 0.14 us
  starting transfers between devices: 22.3 us -> 46 us
  between operations: 1.39 us -> 14.7 us
    all_to_all x2 -> x0, blocking collectives: 559 us -> none  [the longest x1 280 us: on_device(): lax.all_to_all(result.reshape(2, result.shape[1], result.shape[2], 1, res...]
    dot_general x12 -> x1, matrix products: 263 us -> 1.17 us  [on_device(): jnp.einsum('kj,pqj->kqp', jnp.asarray(dirichlet), arranged, precision=lax...]
    ppermute x8 -> x34, waiting for transfers between devices: 9.47 us -> 81.3 us  [the longest x28 73.4 us: swap(): lax.ppermute(blocks[d], 'gy', [(i, i ^ d) for i in range(groups)])]
    pallas_call x0 -> x5, Pallas kernels: none -> 64.9 us  [the longest x2 39 us: solve(): pl.pallas_call(functools.partial(solve_kernel, groups), out_shape=[shape]...]
    another operation x4 -> x0, local copies, waits for them, and re-layouts: 43.1 us -> none  [the longest x3 40.6 us: forward_depth(): joined = jnp.stack([spectrum_real, spectrum_imag])]
    slice x10, local copies, waits for them, and re-layouts: 42.6 us -> 4.07 us  [the longest x2 3.03 us: on_device(): first_rows = jnp.concatenate([f[:, :, 0] for f in fields], axis=0)]
    transpose x2 -> x0, local copies, waits for them, and re-layouts: 32.8 us -> none  [apply(): return jnp.einsum('cxyz,zgk->cygxk', source, matrix, precision=highest)]
    all_to_all x2 -> x0, local copies, waits for them, and re-layouts: 27.7 us -> none  [the longest x1 16.4 us: on_device(): lax.all_to_all(result.reshape(2, result.shape[1], result.shape[2], 1, res...]
  transfers between devices with their start and end apart: 8 -> 35, of which waited for: 4 -> 14; matrix products, arithmetic and copies ran while one was open for 1% -> 4% of each run, Pallas kernels for 0% -> 26%
where the time goes in v1:
time: 220 us; the launch traced here: 219 us
  waiting for transfers between devices  82 us (37%)
  Pallas kernels  64.9 us (30%)
  starting transfers between devices  46 us (21%)
  between operations  14.7 us (7%)
  local copies, waits for them, and re-layouts  10.2 us (5%)
    ppermute x28, waiting for transfers between devices, swap(): lax.ppermute(blocks[d], 'gy', [(i, i ^ d) for i in range(groups)])  73.4 us
    pallas_call x2, Pallas kernels, solve(): pl.pallas_call(functools.partial(solve_kernel, groups), out_shape=[shape]...  39 us
    ppermute x28, starting transfers between devices, swap(): lax.ppermute(blocks[d], 'gy', [(i, i ^ d) for i in range(groups)])  27.8 us
    pallas_call x2, Pallas kernels, advance(): pl.pallas_call(functools.partial(advance_kernel, chunk, chunks, whole), o...  18.5 us
    pallas_call x1, Pallas kernels, curl(): pl.pallas_call(functools.partial(curl_kernel, groups, chunks, band, width...  7.36 us
    ppermute x1, waiting for transfers between devices, on_device(): lax.ppermute(first_x, 'gx', pairs(across_x, -1))  5.14 us
  transfers between devices with their start and end apart: 35, of which 14 were waited for; matrix products, arithmetic and copies ran while one was open for 4% of the time, Pallas kernels for 26%

profile of v1, /device:TPU:10, one launch (start us, length us, event | category | flops | bytes accessed | tf_op | source)
XLA Modules:
  0.0 219.0 jit_solution(9463437702003667233)
XLA Ops:
  7.2 0.7 all-gather.2.cloned.1.call-update
  7.9 1.5 fusion.18
  9.4 1.5 fusion.19
  11.0 1.9 collective-permute-start
  13.0 3.6 %collective-permute-start.1 = (f32[6,32,256]{2,1,0:T(8,128)S(1)}, f32[6,32,256]{2,1,0:T(8,128)S(1)}, u32[]{:S(2)}, u32[]{:S(2)}) collective-permute-start(f32[6,32,256]{2,1,0:T(8,128)S(1)} %pad_maximum_fusion.1), channel_id=1, source_target_pairs={{1,0},{2,1},{3,2},{4,3},{5,4},{6,5},{7,6},{9,8},{10,9},{11,10},{12... | collective-permute-start | bytes 589832 | tf_op jit(solution)/shard_map/ppermute | solution.py:315
  16.6 1.1 slice_bitcast_fusion
  17.7 3.4 %collective-permute-start.2 = (f32[6,32,256]{2,1,0:T(8,128)S(1)}, f32[6,32,256]{2,1,0:T(8,128)S(1)}, u32[]{:S(2)}, u32[]{:S(2)}) collective-permute-start(f32[6,32,256]{2,1,0:T(8,128)S(1)} %pad_maximum_fusion.2), channel_id=1, source_target_pairs={{0,8},{8,16},{16,24},{1,9},{9,17},{17,25},{2,10},{10,18},{18,26},{... | collective-permute-start | bytes 589832 | tf_op jit(solution)/shard_map/ppermute | solution.py:316
  21.1 2.5 %collective-permute-start.3 = (f32[6,32,256]{2,1,0:T(8,128)S(1)}, f32[6,32,256]{2,1,0:T(8,128)S(1)}, u32[]{:S(2)}, u32[]{:S(2)}) collective-permute-start(f32[6,32,256]{2,1,0:T(8,128)S(1)} %pad_maximum_fusion.3), channel_id=1, source_target_pairs={{8,0},{16,8},{24,16},{9,1},{17,9},{25,17},{10,2},{18,10},{26,18},{... | collective-permute-start | bytes 589832 | tf_op jit(solution)/shard_map/ppermute | solution.py:317
  23.7 2.7 %collective-permute-done.2.xlo = f32[6,32,256]{2,1,0:T(8,128)S(1)} collective-permute-done((f32[6,32,256]{2,1,0:T(8,128)S(1)}, f32[6,32,256]{2,1,0:T(8,128)S(1)}, u32[]{:S(2)}, u32[]{:S(2)}) %collective-permute-start.2) | collective-permute-done | bytes 196640 | tf_op jit(solution)/shard_map/ppermute | solution.py:316
  26.4 5.1 %collective-permute-done.3.xhi = f32[6,32,256]{2,1,0:T(8,128)S(1)} collective-permute-done((f32[6,32,256]{2,1,0:T(8,128)S(1)}, f32[6,32,256]{2,1,0:T(8,128)S(1)}, u32[]{:S(2)}, u32[]{:S(2)}) %collective-permute-start.3) | collective-permute-done | bytes 196640 | tf_op jit(solution)/shard_map/ppermute | solution.py:317
  31.6 0.7 copy-done.3
  32.2 7.3 %advance_0.1 = (f32[3,2,32,256]{3,2,1,0:T(8,128)}, f32[3,2,32,256]{3,2,1,0:T(8,128)}, f32[3,2,32,256]{3,2,1,0:T(8,128)}, f32[3,2,32,256]{3,2,1,0:T(8,128)}, f32[...) custom-call(s32[1]{0:T(128)} %bitcast.me_ref, ...), custom_call_target="tpu_custom_call" | custom-call | tf_op jit(solution)/shard_map/advance_0/pallas_call | solution.py:134
  39.5 1.8 collective-permute-start.6
  41.3 1.5 collective-permute-start.7
  42.8 1.1 collective-permute-start.8
  43.9 1.6 collective-permute-start.9
  45.5 11.2 %advance_1.1 = (f32[3,32,32,256]{3,2,1,0:T(8,128)}, f32[3,2,32,256]{3,2,1,0:T(8,128)}, f32[3,2,32,256]{3,2,1,0:T(8,128)}, f32[3,2,32,256]{3,2,1,0:T(8,128)}, f32...) custom-call(s32[1]{0:T(128)} %bitcast.me_ref, ...), custom_call_target="tpu_custom_call" | custom-call | tf_op jit(solution)/shard_map/advance_1/pallas_call | solution.py:134
  56.8 1.6 copy.41
  59.4 2.3 %collective-permute-start.21 = (f32[3,2,32,256]{3,2,1,0:T(8,128)}, f32[3,2,32,256]{3,2,1,0:T(8,128)S(1)}, u32[]{:S(2)}, u32[]{:S(2)}) collective-permute-start(f32[3,2,32,256]{3,2,1,0:T(8,128)} %get-tuple-element.54), channel_id=1, source_target_pairs={{0,2},{1,3},{2,0},{3,1},{4,6},{5,7},{6,4},{7,5},{8,10},{9,11},{10,... | collective-permute-start | bytes 589832 | tf_op jit(solution)/shard_map/ppermute | solution.py:293
  61.7 7.9 %collective-permute-done.8.refs_5_ = f32[3,2,32,256]{3,2,1,0:T(8,128)} collective-permute-done((f32[3,2,32,256]{3,2,1,0:T(8,128)}, f32[3,2,32,256]{3,2,1,0:T(8,128)}, u32[]{:S(2)}, u32[]{:S(2)}) %collective-permute-start.8) | collective-permute-done | bytes 196640 | tf_op jit(solution)/shard_map/ppermute | solution.py:293
  69.6 1.6 collective-permute-start.22
  71.2 3.3 %collective-permute-done.9.refs_6_ = f32[3,2,32,256]{3,2,1,0:T(8,128)} collective-permute-done((f32[3,2,32,256]{3,2,1,0:T(8,128)}, f32[3,2,32,256]{3,2,1,0:T(8,128)}, u32[]{:S(2)}, u32[]{:S(2)}) %collective-permute-start.9) | collective-permute-done | bytes 196640 | tf_op jit(solution)/shard_map/ppermute | solution.py:293
  74.5 1.2 fusion
  75.7 1.0 copy.60.green
  76.7 5.5 %collective-permute-done.10.refs_7_ = f32[3,2,32,256]{3,2,1,0:T(8,128)S(1)} collective-permute-done((f32[3,2,32,256]{3,2,1,0:T(8,128)}, f32[3,2,32,256]{3,2,1,0:T(8,128)S(1)}, u32[]{:S(2)}, u32[]{:S(2)}) %collective-permute-start.10) | collective-permute-done | bytes 196640 | tf_op jit(solution)/shard_map/ppermute | solution.py:293
  82.2 0.7 copy-done.30
  82.9 19.5 %solve.2 = (f32[200,256]{1,0:T(8,128)}, f32[200,256]{1,0:T(8,128)}, f32[200,256]{1,0:T(8,128)}, f32[200,256]{1,0:T(8,128)}, f32[200,256]{1,0:T(8,128)}, /*index=...) custom-call(s32[1]{0:T(128)} %bitcast.me_ref, bf16[512,768]{1,0:T(8,128)(2,1)} %constant.28.clone.fz, ...), custom_call_target="tpu_custom_call" | custom-call | tf_op jit(solution)/shard_map/solve/pallas_call | solution.py:212
  102.9 2.7 %collective-permute-start.24 = (f32[3,2,32,256]{3,2,1,0:T(8,128)S(1)}, f32[3,2,32,256]{3,2,1,0:T(8,128)S(1)}, u32[]{:S(2)}, u32[]{:S(2)}) collective-permute-start(f32[3,2,32,256]{3,2,1,0:T(8,128)S(1)} %copy-done.35), channel_id=1, source_target_pairs={{0,5},{1,4},{2,7},{3,6},{4,1},{5,0},{6,3},{7,2},{8,13},{9,12},{10,... | collective-permute-start | bytes 589832 | tf_op jit(solution)/shard_map/ppermute | solution.py:293
  105.9 1.9 collective-permute-start.26
  107.8 15.8 %collective-permute-done.24.refs_5_ = f32[3,2,32,256]{3,2,1,0:T(8,128)S(1)} collective-permute-done((f32[3,2,32,256]{3,2,1,0:T(8,128)S(1)}, f32[3,2,32,256]{3,2,1,0:T(8,128)S(1)}, u32[]{:S(2)}, u32[]{:S(2)}) %collective-permute-start.24) | collective-permute-done | bytes 196640 | tf_op jit(solution)/shard_map/ppermute | solution.py:293
  123.5 1.9 collective-permute-start.13
  125.4 3.0 %collective-permute-done.25.refs_6_ = f32[3,2,32,256]{3,2,1,0:T(8,128)S(1)} collective-permute-done((f32[3,2,32,256]{3,2,1,0:T(8,128)S(1)}, f32[3,2,32,256]{3,2,1,0:T(8,128)S(1)}, u32[]{:S(2)}, u32[]{:S(2)}) %collective-permute-start.25) | collective-permute-done | bytes 196640 | tf_op jit(solution)/shard_map/ppermute | solution.py:293
  128.5 8.6 %collective-permute-done.26.refs_7_ = f32[3,2,32,256]{3,2,1,0:T(8,128)S(1)} collective-permute-done((f32[3,2,32,256]{3,2,1,0:T(8,128)S(1)}, f32[3,2,32,256]{3,2,1,0:T(8,128)S(1)}, u32[]{:S(2)}, u32[]{:S(2)}) %collective-permute-start.26) | collective-permute-done | bytes 196640 | tf_op jit(solution)/shard_map/ppermute | solution.py:293
  137.1 1.8 collective-permute-start.16
  139.0 1.0 slice.112
  140.0 19.5 %solve.3 = (f32[200,256]{1,0:T(8,128)}, f32[200,256]{1,0:T(8,128)}, f32[200,256]{1,0:T(8,128)}, f32[200,256]{1,0:T(8,128)}, f32[200,256]{1,0:T(8,128)}, /*index=...) custom-call(s32[1]{0:T(128)} %bitcast.me_ref, bf16[512,768]{1,0:T(8,128)(2,1)} %constant.28.clone.fz, ...), custom_call_target="tpu_custom_call" | custom-call | tf_op jit(solution)/shard_map/solve/pallas_call | solution.py:212
  160.0 4.7 %collective-permute-start.28 = (f32[200,256]{1,0:T(8,128)}, f32[200,256]{1,0:T(8,128)S(1)}, u32[]{:S(2)}, u32[]{:S(2)}) collective-permute-start(f32[200,256]{1,0:T(8,128)} %get-tuple-element.62), channel_id=1, source_target_pairs={{0,2},{1,3},{2,0},{3,1},{4,6},{5,7},{6,4},{7,5},{8,10},{9,11},{10,... | collective-permute-start | bytes 614408 | tf_op jit(solution)/shard_map/ppermute | solution.py:293
  164.8 1.3 collective-permute-start.30
  166.1 1.7 collective-permute-done.17.refs_7_
  167.9 1.8 collective-permute-start.32
  169.7 5.9 %collective-permute-done.28.refs_10_ = f32[200,256]{1,0:T(8,128)S(1)} collective-permute-done((f32[200,256]{1,0:T(8,128)}, f32[200,256]{1,0:T(8,128)S(1)}, u32[]{:S(2)}, u32[]{:S(2)}) %collective-permute-start.28) | collective-permute-done | bytes 204832 | tf_op jit(solution)/shard_map/ppermute | solution.py:293
  175.7 3.6 %collective-permute-done.29.refs_11_ = f32[200,256]{1,0:T(8,128)S(1)} collective-permute-done((f32[200,256]{1,0:T(8,128)}, f32[200,256]{1,0:T(8,128)S(1)}, u32[]{:S(2)}, u32[]{:S(2)}) %collective-permute-start.29) | collective-permute-done | bytes 204832 | tf_op jit(solution)/shard_map/ppermute | solution.py:293
  179.2 2.4 %collective-permute-start.19 = (f32[2,32,256]{2,1,0:T(8,128)S(1)}, f32[2,32,256]{2,1,0:T(8,128)S(1)}, u32[]{:S(2)}, u32[]{:S(2)}) collective-permute-start(f32[2,32,256]{2,1,0:T(8,128)S(1)} %fusion.5), channel_id=1, source_target_pairs={{8,0},{16,8},{24,16},{9,1},{17,9},{25,17},{10,2},{18,10},{26,18},{... | collective-permute-start | bytes 196616 | tf_op jit(solution)/shard_map/ppermute | solution.py:353
  181.7 4.3 %collective-permute-start.18 = (f32[2,32,256]{2,1,0:T(8,128)S(1)}, f32[2,32,256]{2,1,0:T(8,128)S(1)}, u32[]{:S(2)}, u32[]{:S(2)}) collective-permute-start(f32[2,32,256]{2,1,0:T(8,128)S(1)} %fusion.13), channel_id=1, source_target_pairs={{0,8},{8,16},{16,24},{1,9},{9,17},{17,25},{2,10},{10,18},{18,26},{... | collective-permute-start | bytes 196616 | tf_op jit(solution)/shard_map/ppermute | solution.py:352
  186.0 7.9 %collective-permute-done.31.refs_13_ = f32[200,256]{1,0:T(8,128)S(1)} collective-permute-done((f32[200,256]{1,0:T(8,128)}, f32[200,256]{1,0:T(8,128)S(1)}, u32[]{:S(2)}, u32[]{:S(2)}) %collective-permute-start.31) | collective-permute-done | bytes 204832 | tf_op jit(solution)/shard_map/ppermute | solution.py:293
  193.9 6.4 %collective-permute-done.32.refs_14_ = f32[200,256]{1,0:T(8,128)S(1)} collective-permute-done((f32[200,256]{1,0:T(8,128)}, f32[200,256]{1,0:T(8,128)S(1)}, u32[]{:S(2)}, u32[]{:S(2)}) %collective-permute-start.32) | collective-permute-done | bytes 204832 | tf_op jit(solution)/shard_map/ppermute | solution.py:293
  200.4 3.7 %collective-permute-done.33.refs_15_ = f32[200,256]{1,0:T(8,128)S(1)} collective-permute-done((f32[200,256]{1,0:T(8,128)}, f32[200,256]{1,0:T(8,128)S(1)}, u32[]{:S(2)}, u32[]{:S(2)}) %collective-permute-start.33) | collective-permute-done | bytes 204832 | tf_op jit(solution)/shard_map/ppermute | solution.py:293
  204.8 7.4 %curl.1 = f32[3,32,32,256]{3,2,1,0:T(8,128)} custom-call(s32[1]{0:T(128)} %bitcast.me_ref, f32[2,32,256]{2,1,0:T(8,128)} %copy-done.32, f32[2,32,256]{2,1,0:T(8,128)} %copy-done.31, f32[200,256]{1,0:T(8,128)} %get-tuple-element.44.refs_0_, f32[200,256]{1,0:T(8,128)} %copy-done.4, f32[200,256]{1,0:T(8,128)} %copy-done.5, f32[200,256]{1,0:T(8,128)} %copy-done.6, ...), custom_call_target="tpu_custom_call" | custom-call | tf_op jit(solution)/shard_map/curl/pallas_call | solution.py:270
  (123 shorter events, 3.3 us)
Async XLA Ops:
  7.2 49.6 %all-gather.2.cloned.1.call-start = ((), (), s32[]{:S(2)}) async-start(), calls=%async_computation | async-start | bytes 1179648 | tf_op jit(solution)/shard_map/all_gather | solution.py:322
  11.0 12.6 %collective-permute-start = (f32[6,32,256]{2,1,0:T(8,128)S(1)}, f32[6,32,256]{2,1,0:T(8,128)S(1)}, u32[]{:S(2)}, u32[]{:S(2)}) collective-permute-start(f32[6,32,256]{2,1,0:T(8,128)S(1)} %pad_maximum_fusion), channel_id=1, source_target_pairs={{0,1},{1,2},{2,3},{3,4},{4,5},{5,6},{6,7},{8,9},{9,10},{10,11},{11... | collective-permute-start | bytes 589832 | tf_op jit(solution)/shard_map/ppermute | solution.py:314
  13.0 10.7 %collective-permute-start.1 = (f32[6,32,256]{2,1,0:T(8,128)S(1)}, f32[6,32,256]{2,1,0:T(8,128)S(1)}, u32[]{:S(2)}, u32[]{:S(2)}) collective-permute-start(f32[6,32,256]{2,1,0:T(8,128)S(1)} %pad_maximum_fusion.1), channel_id=1, source_target_pairs={{1,0},{2,1},{3,2},{4,3},{5,4},{6,5},{7,6},{9,8},{10,9},{11,10},{12... | collective-permute-start | bytes 589832 | tf_op jit(solution)/shard_map/ppermute | solution.py:315
  17.7 8.7 %collective-permute-start.2 = (f32[6,32,256]{2,1,0:T(8,128)S(1)}, f32[6,32,256]{2,1,0:T(8,128)S(1)}, u32[]{:S(2)}, u32[]{:S(2)}) collective-permute-start(f32[6,32,256]{2,1,0:T(8,128)S(1)} %pad_maximum_fusion.2), channel_id=1, source_target_pairs={{0,8},{8,16},{16,24},{1,9},{9,17},{17,25},{2,10},{10,18},{18,26},{... | collective-permute-start | bytes 589832 | tf_op jit(solution)/shard_map/ppermute | solution.py:316
  21.1 10.4 %collective-permute-start.3 = (f32[6,32,256]{2,1,0:T(8,128)S(1)}, f32[6,32,256]{2,1,0:T(8,128)S(1)}, u32[]{:S(2)}, u32[]{:S(2)}) collective-permute-start(f32[6,32,256]{2,1,0:T(8,128)S(1)} %pad_maximum_fusion.3), channel_id=1, source_target_pairs={{8,0},{16,8},{24,16},{9,1},{17,9},{25,17},{10,2},{18,10},{26,18},{... | collective-permute-start | bytes 589832 | tf_op jit(solution)/shard_map/ppermute | solution.py:317
  39.5 4.4 %collective-permute-start.4 = (f32[3,2,32,256]{3,2,1,0:T(8,128)}, f32[3,2,32,256]{3,2,1,0:T(8,128)S(1)}, u32[]{:S(2)}, u32[]{:S(2)}) collective-permute-start(f32[3,2,32,256]{3,2,1,0:T(8,128)} %get-tuple-element.37), channel_id=1, source_target_pairs={{0,1},{1,0},{2,3},{3,2},{4,5},{5,4},{6,7},{7,6},{8,9},{9,8},{10,11... | collective-permute-start | bytes 589832 | tf_op jit(solution)/shard_map/ppermute | solution.py:293
  39.5 19.2 %collective-permute-start.5 = (f32[3,2,32,256]{3,2,1,0:T(8,128)}, f32[3,2,32,256]{3,2,1,0:T(8,128)S(1)}, u32[]{:S(2)}, u32[]{:S(2)}) collective-permute-start(f32[3,2,32,256]{3,2,1,0:T(8,128)} %get-tuple-element.38), channel_id=1, source_target_pairs={{0,2},{1,3},{2,0},{3,1},{4,6},{5,7},{6,4},{7,5},{8,10},{9,11},{10,... | collective-permute-start | bytes 589832 | tf_op jit(solution)/shard_map/ppermute | solution.py:293
  39.5 19.5 %collective-permute-start.6 = (f32[3,2,32,256]{3,2,1,0:T(8,128)}, f32[3,2,32,256]{3,2,1,0:T(8,128)S(1)}, u32[]{:S(2)}, u32[]{:S(2)}) collective-permute-start(f32[3,2,32,256]{3,2,1,0:T(8,128)} %get-tuple-element.39), channel_id=1, source_target_pairs={{0,3},{1,2},{2,1},{3,0},{4,7},{5,6},{6,5},{7,4},{8,11},{9,10},{10,... | collective-permute-start | bytes 589832 | tf_op jit(solution)/shard_map/ppermute | solution.py:293
  41.3 18.0 %collective-permute-start.7 = (f32[3,2,32,256]{3,2,1,0:T(8,128)}, f32[3,2,32,256]{3,2,1,0:T(8,128)S(1)}, u32[]{:S(2)}, u32[]{:S(2)}) collective-permute-start(f32[3,2,32,256]{3,2,1,0:T(8,128)} %get-tuple-element.40), channel_id=1, source_target_pairs={{0,4},{1,5},{2,6},{3,7},{4,0},{5,1},{6,2},{7,3},{8,12},{9,13},{10,... | collective-permute-start | bytes 589832 | tf_op jit(solution)/shard_map/ppermute | solution.py:293
  42.8 26.7 %collective-permute-start.8 = (f32[3,2,32,256]{3,2,1,0:T(8,128)}, f32[3,2,32,256]{3,2,1,0:T(8,128)}, u32[]{:S(2)}, u32[]{:S(2)}) collective-permute-start(f32[3,2,32,256]{3,2,1,0:T(8,128)} %get-tuple-element.41), channel_id=1, source_target_pairs={{0,5},{1,4},{2,7},{3,6},{4,1},{5,0},{6,3},{7,2},{8,13},{9,12},{10,... | collective-permute-start | bytes 589832 | tf_op jit(solution)/shard_map/ppermute | solution.py:293
  43.9 30.6 %collective-permute-start.9 = (f32[3,2,32,256]{3,2,1,0:T(8,128)}, f32[3,2,32,256]{3,2,1,0:T(8,128)}, u32[]{:S(2)}, u32[]{:S(2)}) collective-permute-start(f32[3,2,32,256]{3,2,1,0:T(8,128)} %get-tuple-element.42), channel_id=1, source_target_pairs={{0,6},{1,7},{2,4},{3,5},{4,2},{5,3},{6,0},{7,1},{8,14},{9,15},{10,... | collective-permute-start | bytes 589832 | tf_op jit(solution)/shard_map/ppermute | solution.py:293
  58.7 23.5 %copy-start.24 = (f32[3,2,32,256]{3,2,1,0:T(8,128)}, f32[3,2,32,256]{3,2,1,0:T(8,128)S(1)}, u32[]{:S(2)}) copy-start(f32[3,2,32,256]{3,2,1,0:T(8,128)S(1)} %collective-permute-done.5.refs_2_) | copy-start | bytes 589828
  58.7 23.5 %collective-permute-start.10 = (f32[3,2,32,256]{3,2,1,0:T(8,128)}, f32[3,2,32,256]{3,2,1,0:T(8,128)S(1)}, u32[]{:S(2)}, u32[]{:S(2)}) collective-permute-start(f32[3,2,32,256]{3,2,1,0:T(8,128)} %get-tuple-element.43), channel_id=1, source_target_pairs={{0,7},{1,6},{2,5},{3,4},{4,3},{5,2},{6,1},{7,0},{8,15},{9,14},{10,... | collective-permute-start | bytes 589832 | tf_op jit(solution)/shard_map/ppermute | solution.py:293
  59.0 43.8 %collective-permute-start.20 = (f32[3,2,32,256]{3,2,1,0:T(8,128)}, f32[3,2,32,256]{3,2,1,0:T(8,128)S(1)}, u32[]{:S(2)}, u32[]{:S(2)}) collective-permute-start(f32[3,2,32,256]{3,2,1,0:T(8,128)} %get-tuple-element.53), channel_id=1, source_target_pairs={{0,1},{1,0},{2,3},{3,2},{4,5},{5,4},{6,7},{7,6},{8,9},{9,8},{10,11... | collective-permute-start | bytes 589832 | tf_op jit(solution)/shard_map/ppermute | solution.py:293
  59.4 43.5 %collective-permute-start.21 = (f32[3,2,32,256]{3,2,1,0:T(8,128)}, f32[3,2,32,256]{3,2,1,0:T(8,128)S(1)}, u32[]{:S(2)}, u32[]{:S(2)}) collective-permute-start(f32[3,2,32,256]{3,2,1,0:T(8,128)} %get-tuple-element.54), channel_id=1, source_target_pairs={{0,2},{1,3},{2,0},{3,1},{4,6},{5,7},{6,4},{7,5},{8,10},{9,11},{10,... | collective-permute-start | bytes 589832 | tf_op jit(solution)/shard_map/ppermute | solution.py:293
  69.6 36.0 %collective-permute-start.22 = (f32[3,2,32,256]{3,2,1,0:T(8,128)}, f32[3,2,32,256]{3,2,1,0:T(8,128)S(1)}, u32[]{:S(2)}, u32[]{:S(2)}) collective-permute-start(f32[3,2,32,256]{3,2,1,0:T(8,128)} %get-tuple-element.55), channel_id=1, source_target_pairs={{0,3},{1,2},{2,1},{3,0},{4,7},{5,6},{6,5},{7,4},{8,11},{9,10},{10,... | collective-permute-start | bytes 589832 | tf_op jit(solution)/shard_map/ppermute | solution.py:293
  74.5 31.4 %collective-permute-start.23 = (f32[3,2,32,256]{3,2,1,0:T(8,128)}, f32[3,2,32,256]{3,2,1,0:T(8,128)S(1)}, u32[]{:S(2)}, u32[]{:S(2)}) collective-permute-start(f32[3,2,32,256]{3,2,1,0:T(8,128)} %get-tuple-element.56), channel_id=1, source_target_pairs={{0,4},{1,5},{2,6},{3,7},{4,0},{5,1},{6,2},{7,3},{8,12},{9,13},{10,... | collective-permute-start | bytes 589832 | tf_op jit(solution)/shard_map/ppermute | solution.py:293
  102.4 34.7 %collective-permute-start.11 = (f32[200,256]{1,0:T(8,128)}, f32[200,256]{1,0:T(8,128)S(1)}, u32[]{:S(2)}, u32[]{:S(2)}) collective-permute-start(f32[200,256]{1,0:T(8,128)} %get-tuple-element.45), channel_id=1, source_target_pairs={{0,1},{1,0},{2,3},{3,2},{4,5},{5,4},{6,7},{7,6},{8,9},{9,8},{10,11... | collective-permute-start | bytes 614408 | tf_op jit(solution)/shard_map/ppermute | solution.py:293
  102.9 37.1 %copy-start.19 = (f32[3,2,32,256]{3,2,1,0:T(8,128)}, f32[3,2,32,256]{3,2,1,0:T(8,128)S(1)}, u32[]{:S(2)}) copy-start(f32[3,2,32,256]{3,2,1,0:T(8,128)S(1)} %collective-permute-done.20.refs_1_) | copy-start | bytes 589828
  102.9 36.1 %collective-permute-start.12 = (f32[200,256]{1,0:T(8,128)}, f32[200,256]{1,0:T(8,128)S(1)}, u32[]{:S(2)}, u32[]{:S(2)}) collective-permute-start(f32[200,256]{1,0:T(8,128)} %get-tuple-element.46), channel_id=1, source_target_pairs={{0,2},{1,3},{2,0},{3,1},{4,6},{5,7},{6,4},{7,5},{8,10},{9,11},{10,... | collective-permute-start | bytes 614408 | tf_op jit(solution)/shard_map/ppermute | solution.py:293
  102.9 37.1 %copy-start.20 = (f32[3,2,32,256]{3,2,1,0:T(8,128)}, f32[3,2,32,256]{3,2,1,0:T(8,128)S(1)}, u32[]{:S(2)}) copy-start(f32[3,2,32,256]{3,2,1,0:T(8,128)S(1)} %collective-permute-done.21.refs_2_) | copy-start | bytes 589828
  102.9 20.6 %collective-permute-start.24 = (f32[3,2,32,256]{3,2,1,0:T(8,128)S(1)}, f32[3,2,32,256]{3,2,1,0:T(8,128)S(1)}, u32[]{:S(2)}, u32[]{:S(2)}) collective-permute-start(f32[3,2,32,256]{3,2,1,0:T(8,128)S(1)} %copy-done.35), channel_id=1, source_target_pairs={{0,5},{1,4},{2,7},{3,6},{4,1},{5,0},{6,3},{7,2},{8,13},{9,12},{10,... | collective-permute-start | bytes 589832 | tf_op jit(solution)/shard_map/ppermute | solution.py:293
  105.6 34.4 %copy-start.21 = (f32[3,2,32,256]{3,2,1,0:T(8,128)}, f32[3,2,32,256]{3,2,1,0:T(8,128)S(1)}, u32[]{:S(2)}) copy-start(f32[3,2,32,256]{3,2,1,0:T(8,128)S(1)} %collective-permute-done.22.refs_3_) | copy-start | bytes 589828
  105.6 22.9 %collective-permute-start.25 = (f32[3,2,32,256]{3,2,1,0:T(8,128)S(1)}, f32[3,2,32,256]{3,2,1,0:T(8,128)S(1)}, u32[]{:S(2)}, u32[]{:S(2)}) collective-permute-start(f32[3,2,32,256]{3,2,1,0:T(8,128)S(1)} %copy-done.34), channel_id=1, source_target_pairs={{0,6},{1,7},{2,4},{3,5},{4,2},{5,3},{6,0},{7,1},{8,14},{9,15},{10,... | collective-permute-start | bytes 589832 | tf_op jit(solution)/shard_map/ppermute | solution.py:293
  105.9 34.1 %copy-start.22 = (f32[3,2,32,256]{3,2,1,0:T(8,128)}, f32[3,2,32,256]{3,2,1,0:T(8,128)S(1)}, u32[]{:S(2)}) copy-start(f32[3,2,32,256]{3,2,1,0:T(8,128)S(1)} %collective-permute-done.23.refs_4_) | copy-start | bytes 589828
  105.9 31.2 %collective-permute-start.26 = (f32[3,2,32,256]{3,2,1,0:T(8,128)S(1)}, f32[3,2,32,256]{3,2,1,0:T(8,128)S(1)}, u32[]{:S(2)}, u32[]{:S(2)}) collective-permute-start(f32[3,2,32,256]{3,2,1,0:T(8,128)S(1)} %copy-done.33), channel_id=1, source_target_pairs={{0,7},{1,6},{2,5},{3,4},{4,3},{5,2},{6,1},{7,0},{8,15},{9,14},{10,... | collective-permute-start | bytes 589832 | tf_op jit(solution)/shard_map/ppermute | solution.py:293
  123.5 36.0 %collective-permute-start.13 = (f32[200,256]{1,0:T(8,128)}, f32[200,256]{1,0:T(8,128)S(1)}, u32[]{:S(2)}, u32[]{:S(2)}) collective-permute-start(f32[200,256]{1,0:T(8,128)} %get-tuple-element.47), channel_id=1, source_target_pairs={{0,3},{1,2},{2,1},{3,0},{4,7},{5,6},{6,5},{7,4},{8,11},{9,10},{10,... | collective-permute-start | bytes 614408 | tf_op jit(solution)/shard_map/ppermute | solution.py:293
  128.5 31.5 %collective-permute-start.14 = (f32[200,256]{1,0:T(8,128)}, f32[200,256]{1,0:T(8,128)S(1)}, u32[]{:S(2)}, u32[]{:S(2)}) collective-permute-start(f32[200,256]{1,0:T(8,128)} %get-tuple-element.48), channel_id=1, source_target_pairs={{0,4},{1,5},{2,6},{3,7},{4,0},{5,1},{6,2},{7,3},{8,12},{9,13},{10,... | collective-permute-start | bytes 614408 | tf_op jit(solution)/shard_map/ppermute | solution.py:293
  137.1 27.6 %collective-permute-start.15 = (f32[200,256]{1,0:T(8,128)}, f32[200,256]{1,0:T(8,128)S(1)}, u32[]{:S(2)}, u32[]{:S(2)}) collective-permute-start(f32[200,256]{1,0:T(8,128)} %get-tuple-element.49), channel_id=1, source_target_pairs={{0,5},{1,4},{2,7},{3,6},{4,1},{5,0},{6,3},{7,2},{8,13},{9,12},{10,... | collective-permute-start | bytes 614408 | tf_op jit(solution)/shard_map/ppermute | solution.py:293
  137.1 27.7 %collective-permute-start.16 = (f32[200,256]{1,0:T(8,128)}, f32[200,256]{1,0:T(8,128)S(1)}, u32[]{:S(2)}, u32[]{:S(2)}) collective-permute-start(f32[200,256]{1,0:T(8,128)} %get-tuple-element.50), channel_id=1, source_target_pairs={{0,6},{1,7},{2,4},{3,5},{4,2},{5,3},{6,0},{7,1},{8,14},{9,15},{10,... | collective-permute-start | bytes 614408 | tf_op jit(solution)/shard_map/ppermute | solution.py:293
  138.9 28.9 %collective-permute-start.17 = (f32[200,256]{1,0:T(8,128)}, f32[200,256]{1,0:T(8,128)S(1)}, u32[]{:S(2)}, u32[]{:S(2)}) collective-permute-start(f32[200,256]{1,0:T(8,128)} %get-tuple-element.51), channel_id=1, source_target_pairs={{0,7},{1,6},{2,5},{3,4},{4,3},{5,2},{6,1},{7,0},{8,15},{9,14},{10,... | collective-permute-start | bytes 614408 | tf_op jit(solution)/shard_map/ppermute | solution.py:293
  159.6 44.5 %copy-start.6 = (f32[200,256]{1,0:T(8,128)}, f32[200,256]{1,0:T(8,128)S(1)}, u32[]{:S(2)}) copy-start(f32[200,256]{1,0:T(8,128)S(1)} %collective-permute-done.13.refs_3_) | copy-start | bytes 614404
  159.6 8.3 %collective-permute-start.27 = (f32[200,256]{1,0:T(8,128)}, f32[200,256]{1,0:T(8,128)S(1)}, u32[]{:S(2)}, u32[]{:S(2)}) collective-permute-start(f32[200,256]{1,0:T(8,128)} %get-tuple-element.61), channel_id=1, source_target_pairs={{0,1},{1,0},{2,3},{3,2},{4,5},{5,4},{6,7},{7,6},{8,9},{9,8},{10,11... | collective-permute-start | bytes 614408 | tf_op jit(solution)/shard_map/ppermute | solution.py:293
  160.0 44.1 %copy-start.7 = (f32[200,256]{1,0:T(8,128)}, f32[200,256]{1,0:T(8,128)S(1)}, u32[]{:S(2)}) copy-start(f32[200,256]{1,0:T(8,128)S(1)} %collective-permute-done.14.refs_4_) | copy-start | bytes 614404
  160.0 15.6 %collective-permute-start.28 = (f32[200,256]{1,0:T(8,128)}, f32[200,256]{1,0:T(8,128)S(1)}, u32[]{:S(2)}, u32[]{:S(2)}) collective-permute-start(f32[200,256]{1,0:T(8,128)} %get-tuple-element.62), channel_id=1, source_target_pairs={{0,2},{1,3},{2,0},{3,1},{4,6},{5,7},{6,4},{7,5},{8,10},{9,11},{10,... | collective-permute-start | bytes 614408 | tf_op jit(solution)/shard_map/ppermute | solution.py:293
  164.7 39.4 %copy-start.8 = (f32[200,256]{1,0:T(8,128)}, f32[200,256]{1,0:T(8,128)S(1)}, u32[]{:S(2)}) copy-start(f32[200,256]{1,0:T(8,128)S(1)} %collective-permute-done.15.refs_5_) | copy-start | bytes 614404
  164.7 14.5 %collective-permute-start.29 = (f32[200,256]{1,0:T(8,128)}, f32[200,256]{1,0:T(8,128)S(1)}, u32[]{:S(2)}, u32[]{:S(2)}) collective-permute-start(f32[200,256]{1,0:T(8,128)} %get-tuple-element.63), channel_id=1, source_target_pairs={{0,3},{1,2},{2,1},{3,0},{4,7},{5,6},{6,5},{7,4},{8,11},{9,10},{10,... | collective-permute-start | bytes 614408 | tf_op jit(solution)/shard_map/ppermute | solution.py:293
  164.8 39.3 %copy-start.9 = (f32[200,256]{1,0:T(8,128)}, f32[200,256]{1,0:T(8,128)S(1)}, u32[]{:S(2)}) copy-start(f32[200,256]{1,0:T(8,128)S(1)} %collective-permute-done.16.refs_6_) | copy-start | bytes 614404
  164.8 16.8 %collective-permute-start.30 = (f32[200,256]{1,0:T(8,128)}, f32[200,256]{1,0:T(8,128)S(1)}, u32[]{:S(2)}, u32[]{:S(2)}) collective-permute-start(f32[200,256]{1,0:T(8,128)} %get-tuple-element.64), channel_id=1, source_target_pairs={{0,4},{1,5},{2,6},{3,7},{4,0},{5,1},{6,2},{7,3},{8,12},{9,13},{10,... | collective-permute-start | bytes 614408 | tf_op jit(solution)/shard_map/ppermute | solution.py:293
  167.8 36.3 %copy-start.10 = (f32[200,256]{1,0:T(8,128)}, f32[200,256]{1,0:T(8,128)S(1)}, u32[]{:S(2)}) copy-start(f32[200,256]{1,0:T(8,128)S(1)} %collective-permute-done.17.refs_7_) | copy-start | bytes 614404
  167.8 26.1 %collective-permute-start.31 = (f32[200,256]{1,0:T(8,128)}, f32[200,256]{1,0:T(8,128)S(1)}, u32[]{:S(2)}, u32[]{:S(2)}) collective-permute-start(f32[200,256]{1,0:T(8,128)} %get-tuple-element.65), channel_id=1, source_target_pairs={{0,5},{1,4},{2,7},{3,6},{4,1},{5,0},{6,3},{7,2},{8,13},{9,12},{10,... | collective-permute-start | bytes 614408 | tf_op jit(solution)/shard_map/ppermute | solution.py:293
  167.9 36.3 %copy-start.12 = (f32[200,256]{1,0:T(8,128)}, f32[200,256]{1,0:T(8,128)S(1)}, u32[]{:S(2)}) copy-start(f32[200,256]{1,0:T(8,128)S(1)} %collective-permute-done.27.refs_9_) | copy-start | bytes 614404
  167.9 32.5 %collective-permute-start.32 = (f32[200,256]{1,0:T(8,128)}, f32[200,256]{1,0:T(8,128)S(1)}, u32[]{:S(2)}, u32[]{:S(2)}) collective-permute-start(f32[200,256]{1,0:T(8,128)} %get-tuple-element.66), channel_id=1, source_target_pairs={{0,6},{1,7},{2,4},{3,5},{4,2},{5,3},{6,0},{7,1},{8,14},{9,15},{10,... | collective-permute-start | bytes 614408 | tf_op jit(solution)/shard_map/ppermute | solution.py:293
  175.6 28.5 %copy-start.13 = (f32[200,256]{1,0:T(8,128)}, f32[200,256]{1,0:T(8,128)S(1)}, u32[]{:S(2)}) copy-start(f32[200,256]{1,0:T(8,128)S(1)} %collective-permute-done.28.refs_10_) | copy-start | bytes 614404
  175.6 28.4 %collective-permute-start.33 = (f32[200,256]{1,0:T(8,128)}, f32[200,256]{1,0:T(8,128)S(1)}, u32[]{:S(2)}, u32[]{:S(2)}) collective-permute-start(f32[200,256]{1,0:T(8,128)} %get-tuple-element.67), channel_id=1, source_target_pairs={{0,7},{1,6},{2,5},{3,4},{4,3},{5,2},{6,1},{7,0},{8,15},{9,14},{10,... | collective-permute-start | bytes 614408 | tf_op jit(solution)/shard_map/ppermute | solution.py:293
  179.2 24.9 %copy-start.14 = (f32[200,256]{1,0:T(8,128)}, f32[200,256]{1,0:T(8,128)S(1)}, u32[]{:S(2)}) copy-start(f32[200,256]{1,0:T(8,128)S(1)} %collective-permute-done.29.refs_11_) | copy-start | bytes 614404
  179.2 24.9 %collective-permute-start.19 = (f32[2,32,256]{2,1,0:T(8,128)S(1)}, f32[2,32,256]{2,1,0:T(8,128)S(1)}, u32[]{:S(2)}, u32[]{:S(2)}) collective-permute-start(f32[2,32,256]{2,1,0:T(8,128)S(1)} %fusion.5), channel_id=1, source_target_pairs={{8,0},{16,8},{24,16},{9,1},{17,9},{25,17},{10,2},{18,10},{26,18},{... | collective-permute-start | bytes 196616 | tf_op jit(solution)/shard_map/ppermute | solution.py:353
  181.7 22.4 %collective-permute-start.18 = (f32[2,32,256]{2,1,0:T(8,128)S(1)}, f32[2,32,256]{2,1,0:T(8,128)S(1)}, u32[]{:S(2)}, u32[]{:S(2)}) collective-permute-start(f32[2,32,256]{2,1,0:T(8,128)S(1)} %fusion.13), channel_id=1, source_target_pairs={{0,8},{8,16},{16,24},{1,9},{9,17},{17,25},{2,10},{10,18},{18,26},{... | collective-permute-start | bytes 196616 | tf_op jit(solution)/shard_map/ppermute | solution.py:352
  (23 other events, 256.9 us)
Sparse Core Ops, SparseCore 0:
  9.6 23.8 all-gather.1

commit v2 on v1

v2 whole, which is shorter than its diff:
```python
import functools
import math

import jax
import jax.numpy as jnp
import ml_dtypes
import numpy as np
from jax import lax
from jax.experimental import pallas as pl
from jax.experimental.pallas import tpu as pltpu
from jax.sharding import PartitionSpec as P

time_step = 0.2
viscosity = 0.1
radix = 4
batch = 3
VMEM = pltpu.VMEM
SMEM = pltpu.SMEM


def params(mebibytes):
    return pltpu.CompilerParams(vmem_limit_bytes=mebibytes * 1024 * 1024)


def in_vmem(count):
    return [pl.BlockSpec(memory_space=VMEM)] * count


def halves_np(matrix, axis):


    value = np.asarray(matrix, np.float32)
    high = value.astype(ml_dtypes.bfloat16)
    low = (value - high.astype(np.float32)).astype(ml_dtypes.bfloat16)
    return np.concatenate([high, high, low], axis=axis)


def parts(value, axis):
    high = value.astype(jnp.bfloat16)
    low = (value - high.astype(jnp.float32)).astype(jnp.bfloat16)
    return jnp.concatenate([high, low, high], axis=axis)


@functools.lru_cache(maxsize=None)
def constants(rows, depth):
    long_z, long_y = 2 * depth, 2 * rows
    half = long_y // radix
    k = np.arange(depth)[:, None]
    z = np.arange(depth)[None, :]
    turn = 2.0 * np.pi * (((2 * k + 1) * z) % (2 * long_z)) / (2 * long_z)
    forward_z = halves_np(np.concatenate([np.cos(turn), -np.sin(turn)], axis=0), 1)
    inverse_z = np.concatenate([np.cos(turn), -np.sin(turn)], axis=0) * (2.0 / long_z)
    inverse_z = halves_np(inverse_z.T, 1)
    b = np.arange(half)[:, None]
    p = np.arange(half)[None, :]
    ahead, back = [], []
    for q in range(radix):
        angle = 2.0 * np.pi * ((b * (radix * p + q)) % long_y) / long_y
        c, s = np.cos(angle), np.sin(angle)
        ahead.append(halves_np(np.block([[c, -s], [s, c]]), 0))
        c, s = c.T / long_y, s.T / long_y
        back.append(halves_np(np.block([[c, s], [-s, c]]), 0))
    shift = np.arange(depth)[:, None] + 0.5 - np.arange(long_z)[None, :]
    d = np.arange(1, depth)
    table = 1.0 + 2.0 * np.cos(2.0 * np.pi * np.arange(-2 * long_z, 2 * long_z)[:, None] * d[None, :] / (2 * long_z)).sum(1)
    index = np.rint(2 * shift).astype(np.int64) + 2 * long_z
    return forward_z, inverse_z, np.stack(ahead), np.stack(back), table[index] / long_z


@functools.lru_cache(maxsize=None)
def gain_tables(rows, depth):
    dirichlet = constants(rows, depth)[4]
    long_y, long_z = 2 * rows, 2 * depth
    direct, mirrored, single = [], [], []
    for side in range(2):
        k = side * depth + np.arange(depth)
        direct.append(dirichlet[:, k])
        mirrored.append(dirichlet[:, (long_z - k) % long_z] * (k % depth != 0)[None, :])
        single.append(dirichlet[:, depth - side * depth])
    place = np.arange(long_y)
    lines = radix * (place % (long_y // radix)) + place // (long_y // radix)
    order = np.zeros((2 * long_y, long_y))
    order[lines, place] = 1.0
    order[long_y + (long_y - lines) % long_y, place] = 1.0
    tables = np.stack([np.stack(direct), np.stack(mirrored)], axis=1)
    return tables.astype(np.float32), np.stack(single).astype(np.float32), order.astype(np.float32)


def gain_riders(green_hat, depth):
    near = green_hat.reshape(-1, depth)
    far = green_hat[:, 0].reshape(-1, depth)
    return near, jnp.pad(far, ((0, -far.shape[0] % 8), (0, 0)))


def gains(me, green_hat, near, received, lines):
    groups = len(received)
    half = groups // 2
    long_y, columns = green_hat.shape
    depth = near.shape[1]
    highest = lax.Precision.HIGHEST
    tables, single, order = gain_tables(long_y // 2, depth)
    side, place = me // half, me % half
    blocks = jnp.stack([near] + [received[d][lines:] for d in range(1, half)])
    blocks = jnp.take(blocks, lax.bitwise_xor(place, jnp.arange(half)), axis=0)
    body = blocks.reshape(half, long_y, columns)
    firsts = jnp.stack([received[d][lines : lines + long_y // depth] for d in range(half, groups)])
    column = jnp.take(firsts, place, axis=0).reshape(1, long_y)
    table = jnp.asarray(tables)[side].reshape(2 * depth, half, columns)
    mixed = jnp.einsum("kjc,jmc->km", table, body, precision=highest)
    mixed = mixed.reshape(2, depth, long_y)
    mixed = mixed.at[0].add(jnp.asarray(single)[side][:, None] * column)
    mixed = jnp.concatenate([mixed[0], mixed[1]], axis=1)
    return jnp.dot(mixed, jnp.asarray(order), precision=highest)


def plane_of(owner, local, total):
    return owner * total + jnp.where((owner & 1) == 0, local, total - 1 - local)


def arranged(blocks):
    return [blocks[d] for d in sequence_of(len(blocks))]


def by_step(blocks):
    places = {d: n for n, d in enumerate(sequence_of(len(blocks)))}
    return [blocks[places[d]] for d in range(len(blocks))]


def sequence_of(groups):
    far = list(range(groups - 1, groups // 2 - 1, -1))
    near = list(range(groups // 2 - 1, 0, -1))
    mixed = [0]
    while far or near:
        mixed += far[:1] + near[:1]
        far, near = far[1:], near[1:]
    return mixed


def advance_kernel(groups, chunk, chunks, me_ref, vort, vel, xlo, xhi, ylo, yhi, *rest):
    new, sends = rest[-groups - 5], rest[-groups - 4 : -4]
    frame, block, load_sem, store_sem = rest[-4:]
    _, planes, band, depth = vort.shape
    width = frame.shape[3] - 2
    me = me_ref[0]
    row = lax.broadcasted_iota(jnp.int32, (band, depth), 0)
    column = lax.broadcasted_iota(jnp.int32, (band, depth), 1)
    first_row, last_row = row == 0, row == band - 1
    first_column, last_column = column == 0, column == depth - 1
    sequence = arranged(range(groups))
    place, loads, stores = {}, {}, []
    for d in sequence:
        owner = lax.bitwise_xor(me, d)
        even = (owner & 1) == 0
        low = chunk * width
        start = owner * width * chunks + jnp.where(even, low, width * chunks - width - low)
        base = jnp.clip(start - 1, 0, planes - width - 2)
        place[d] = (even, start, base)
        loads[d] = [
            pltpu.make_async_copy(field.at[:, pl.ds(base, width + 2)], frame.at[d, f], load_sem.at[d, f])
            for f, field in enumerate((vort, vel))
        ]
        for load in loads[d]:
            load.start()
    lines = 3 * width * band
    if chunk == 0:
        near, far = rest[:2]
        for d in sequence[1:]:
            rider = near if d < groups // 2 else far
            target = sends[d].at[pl.ds(lines, rider.shape[0]), :]
            stores.append(pltpu.make_async_copy(rider, target, store_sem.at[d, 1 + width]))
            stores[-1].start()
    for d in sequence:
        even, start, base = place[d]
        for load in loads[d]:
            load.wait()
        for s in range(width):
            x = start + s
            here_at = x - base
            before_at = jnp.maximum(here_at - 1, 0)
            after_at = jnp.minimum(here_at + 1, width + 1)

            def neighbours(f, c):
                slot = 3 * f + c
                here = frame[d, f, c, here_at]
                before, after = frame[d, f, c, before_at], frame[d, f, c, after_at]
                if s == 0:
                    before = jnp.where(x > 0, before, xlo[slot])
                if s == width - 1:
                    after = jnp.where(x < planes - 1, after, xhi[slot])
                down = jnp.where(first_row, ylo[slot, pl.ds(x, 1), :], pltpu.roll(here, 1, 0))
                up = jnp.where(last_row, yhi[slot, pl.ds(x, 1), :], pltpu.roll(here, band - 1, 0))
                left = jnp.where(first_column, 0.0, pltpu.roll(here, 1, 1))
                right = jnp.where(last_column, 0.0, pltpu.roll(here, depth - 1, 1))
                return here, after, before, up, down, right, left

            local = jnp.where(even, s, width - 1 - s)
            w = [frame[d, 0, c, here_at] for c in range(3)]
            for c in range(3):
                _, xp, xm, yp, ym, zp, zm = neighbours(1, c)
                stretch = 0.5 * (w[0] * (xp - xm) + w[1] * (yp - ym) + w[2] * (zp - zm))
                here, xp, xm, yp, ym, zp, zm = neighbours(0, c)
                laplace = xp + xm + yp + ym + zp + zm - 6.0 * here
                line = pl.multiple_of((c * width + local) * band, band)
                block[d, pl.ds(line, band), :] = here + time_step * (stretch + viscosity * laplace)
        stores.append(pltpu.make_async_copy(block.at[d], sends[d].at[pl.ds(0, lines), :], store_sem.at[d, 0]))
        stores[-1].start()
        for s in range(width):
            local = jnp.where(even, s, width - 1 - s)
            for c in range(3):
                line = pl.multiple_of((c * width + local) * band, band)
                source = block.at[d, pl.ds(line, band), :]
                stores.append(pltpu.make_async_copy(source, new.at[c, start + s], store_sem.at[d, 2 + width + 3 * s + c]))
                stores[-1].start()
    for store in stores:
        store.wait()


def advance(chunk, chunks, me, groups, vort, vel, halos, riders, partial):
    _, planes, band, depth = vort.shape
    width = planes // groups // chunks
    lines = 3 * width * band
    more = list(riders) if partial is None else [partial]
    anywhere = pl.BlockSpec(memory_space=pl.ANY)
    shapes = [jax.ShapeDtypeStruct(vort.shape, jnp.float32)]
    for d in range(groups):
        extra = 0 if d == 0 or partial is not None else riders[0 if d < groups // 2 else 1].shape[0]
        shapes.append(jax.ShapeDtypeStruct((lines + extra, depth), jnp.float32))
    out = pl.pallas_call(
        functools.partial(advance_kernel, groups, chunk, chunks),
        out_shape=shapes,
        in_specs=[pl.BlockSpec(memory_space=SMEM)] + [anywhere] * 2 + in_vmem(4)
        + (in_vmem(2) if partial is None else [anywhere]),
        out_specs=[anywhere] * (1 + groups),
        scratch_shapes=[
            pltpu.VMEM((groups, 2, 3, width + 2, band, depth), jnp.float32),
            pltpu.VMEM((groups, lines, depth), jnp.float32),
            pltpu.SemaphoreType.DMA((groups, 2)),
            pltpu.SemaphoreType.DMA((groups, 2 + 4 * width)),
        ],
        input_output_aliases={} if partial is None else {7: 0},
        compiler_params=params(56),
        name=f"advance_{chunk}",
    )(me, vort, vel, *halos, *more)
    return out[0], list(out[1:])


def solve_kernel(groups, stage, width, band, me_ref, fz, bz, ey, by, green, *refs):
    sources, refs = by_step(refs[:groups]), refs[groups:]
    if stage == "second":
        carried, refs = refs[0], refs[1:]
    targets, refs = refs[:groups], refs[groups:]
    if stage == "first":
        carried, refs = refs[0], refs[1:]
    data, psi = refs
    depth = sources[0].shape[1]
    rows = band * groups
    half = rows // 2
    me = me_ref[0]
    pad = 8
    sent = (1, 2) if stage == "first" else (0, 1, 2)
    edged = (2,) if stage == "first" else (0, 2)
    zeros = jnp.zeros((pad, depth), jnp.float32)
    count = 3 * width
    starts = [pl.multiple_of(lax.bitwise_xor(me, d) * band, band) for d in range(groups)]
    for i in range(count):
        psi[i, pl.ds(0, pad), :] = zeros
        psi[i, pl.ds(pad + rows, pad), :] = zeros
        for d in range(groups):
            value = sources[d][pl.ds(i * band, band), :]
            high = value.astype(jnp.bfloat16)
            low = (value - high.astype(jnp.float32)).astype(jnp.bfloat16)
            data[i, pl.ds(starts[d], band), :] = jnp.concatenate([high, low, high], axis=1)

    for begin in range(0, count, batch):
        members = range(begin, begin + batch)
        spectra = [
            lax.dot_general(fz[...], data[i], (((1,), (1,)), ((), ())), preferred_element_type=jnp.float32)
            for i in members
        ]
        total = None
        for q in range(radix):
            lines = []
            for spectrum in spectra:
                low_r, high_r = spectrum[:depth, :half], spectrum[:depth, half:]
                low_i, high_i = spectrum[depth:, :half], spectrum[depth:, half:]
                turned = [
                    lambda: (low_r + high_r, low_i + high_i),
                    lambda: (low_r + high_i, low_i - high_r),
                    lambda: (low_r - high_r, low_i - high_i),
                    lambda: (low_r - high_i, low_i + high_r),
                ][q]()
                lines.append(parts(jnp.concatenate(turned, axis=1), 1))
            freq = jnp.dot(jnp.concatenate(lines, axis=0), ey[q], preferred_element_type=jnp.float32)
            gain = green[:, q * half : (q + 1) * half]
            gain = jnp.concatenate([gain, gain], axis=1)
            lines = [parts(freq[n * depth : (n + 1) * depth] * gain, 1) for n in range(batch)]
            out = jnp.dot(jnp.concatenate(lines, axis=0), by[q], preferred_element_type=jnp.float32)
            re, im = out[:, :half], out[:, half:]
            second = [(re, im), (-im, re), (-re, -im), (im, -re)][q]
            mine = (re, im) + second
            total = mine if total is None else tuple(a + b for a, b in zip(total, mine))
        for n, i in enumerate(members):
            own = [value[n * depth : (n + 1) * depth] for value in total]
            stacked = jnp.concatenate(
                [jnp.concatenate([own[0], own[2]], axis=1), jnp.concatenate([own[1], own[3]], axis=1)], axis=0
            )
            result = jnp.dot(bz[...], parts(stacked, 0), preferred_element_type=jnp.float32)
            psi[i, pl.ds(pad, rows), :] = result.T

    if stage != "plain":
        sign = jnp.where((me & 1) == 0, -1.0, 1.0)
        column = lax.broadcasted_iota(jnp.int32, (rows, depth), 1)
        if stage == "first":
            source = psi.at[0]
            target = 1
        else:
            source = carried.at[width - 1]
            target = 0
        here = sign * source[pl.ds(pad, rows), :]
        up = sign * source[pl.ds(pad + 1, rows), :]
        down = sign * source[pl.ds(pad - 1, rows), :]
        left = jnp.where(column == 0, 0.0, pltpu.roll(here, 1, 1))
        right = jnp.where(column == depth - 1, 0.0, pltpu.roll(here, depth - 1, 1))
        psi[width + target, pl.ds(pad, rows), :] += up - down
        psi[2 * width + target, pl.ds(pad, rows), :] += right - left
        for s in range(width):
            if stage == "first":
                carried[s] = psi[s]
            else:
                psi[s] += carried[s]

    for d in range(groups):
        for a, c in enumerate(sent):
            for s in range(width):
                offset = (a * width + s) * band
                aligned = pl.multiple_of(starts[d] + pad, pad)
                targets[d][pl.ds(offset, band), :] = psi[c * width + s, pl.ds(aligned, band), :]
        for a, c in enumerate(edged):
            for s in range(width):
                offset = len(sent) * width * band + (a * width + s) * 2
                targets[d][pl.ds(offset, 1), :] = psi[c * width + s, pl.ds(starts[d] + pad - 1, 1), :]
                targets[d][pl.ds(offset + 1, 1), :] = psi[c * width + s, pl.ds(starts[d] + pad + band, 1), :]


def solve(stage, width, band, me, green, tables, blocks, carried=()):
    groups = len(blocks)
    depth = blocks[0].shape[1]
    rows = band * groups
    sent, edged = (2, 1) if stage == "first" else (3, 2)
    lines = sent * width * band + 8
    shapes = [jax.ShapeDtypeStruct((lines, depth), jnp.float32)] * groups
    if stage == "first":
        shapes = shapes + [jax.ShapeDtypeStruct((width, rows + 16, depth), jnp.float32)]
    out = pl.pallas_call(
        functools.partial(solve_kernel, groups, stage, width, band),
        out_shape=shapes,
        in_specs=[pl.BlockSpec(memory_space=SMEM)] + in_vmem(5 + groups + len(carried)),
        out_specs=in_vmem(len(shapes)),
        scratch_shapes=[
            pltpu.VMEM((3 * width, rows, 3 * depth), jnp.bfloat16),
            pltpu.VMEM((3 * width, rows + 16, depth), jnp.float32),
        ],
        compiler_params=params(56),
        name="solve_" + stage,
    )(me, *tables, green, *arranged(blocks), *carried)
    return out[:groups], tuple(out[groups:])


def curl_kernel(groups, gauge, width, me_ref, xlo, xhi, *refs):
    chunks = len(refs[:-4]) // groups
    blocks = [block for k in range(chunks) for block in by_step(refs[k * groups : (k + 1) * groups])]
    velocity, front, block, sem = refs[groups * chunks :]
    band, depth = block.shape[3:]
    total = chunks * width
    me = me_ref[0]

    def comps(k):
        return (1, 2) if gauge and k == 0 else (0, 1, 2)

    def read(d, m, c):
        k, s = m // width, m % width
        start = (comps(k).index(c) * width + s) * band
        return blocks[k * groups + d][pl.ds(start, band), :]

    def ends(d, m, c):
        k, s = m // width, m % width
        order = (2,) if len(comps(k)) == 2 else (0, 2)
        start = len(comps(k)) * width * band + (order.index(c) * width + s) * 2
        return blocks[k * groups + d][pl.ds(start, 1), :], blocks[k * groups + d][pl.ds(start + 1, 1), :]

    for h in range(2):
        front[0, h] = xlo[h]
        front[groups + 1, h] = xhi[h]
        for d in range(groups):
            front[lax.bitwise_xor(me, d) + 1, h] = read(d, 0, h + 1)
    row = lax.broadcasted_iota(jnp.int32, (band, depth), 0)
    column = lax.broadcasted_iota(jnp.int32, (band, depth), 1)
    first_row, last_row = row == 0, row == band - 1
    first_column, last_column = column == 0, column == depth - 1

    def along_y(d, m, c):
        here = read(d, m, c)
        below, above = ends(d, m, c)
        down = jnp.where(first_row, below, pltpu.roll(here, 1, 0))
        up = jnp.where(last_row, above, pltpu.roll(here, band - 1, 0))
        return up - down

    def along_z(here):
        left = jnp.where(first_column, 0.0, pltpu.roll(here, 1, 1))
        right = jnp.where(last_column, 0.0, pltpu.roll(here, depth - 1, 1))
        return right - left

    copies = []
    for d in range(groups):
        owner = lax.bitwise_xor(me, d)
        even = (owner & 1) == 0
        sign = jnp.where(even, 0.5, -0.5)
        side = jnp.where(even, owner, owner + 2)

        def along_x(m, c):
            after = read(d, m + 1, c) if m < total - 1 else read(d ^ 1, m, c)
            before = read(d, m - 1, c) if m > 0 else front[side, c - 1]
            return sign * (after - before)

        for m in range(total):
            place = jnp.where(even, m, total - 1 - m)
            no_x = 0 not in comps(m // width)
            block[d, 0, place] = 0.5 * (along_y(d, m, 2) - along_z(read(d, m, 1)))
            first, second = -along_x(m, 2), along_x(m, 1)
            if not no_x:
                first = first + 0.5 * along_z(read(d, m, 0))
                second = second - 0.5 * along_y(d, m, 0)
            block[d, 1, place] = first
            block[d, 2, place] = second
        for c in range(3):
            target = velocity.at[c, pl.ds(owner * total, total)]
            copy = pltpu.make_async_copy(block.at[d, c], target, sem.at[d, c])
            copy.start()
            copies.append(copy)
    for copy in copies:
        copy.wait()


def curl(me, groups, gauge, shape, edges, blocks):
    _, planes, band, depth = shape
    chunks = len(blocks) // groups
    total = planes // groups
    return pl.pallas_call(
        functools.partial(curl_kernel, groups, gauge, total // chunks),
        out_shape=jax.ShapeDtypeStruct(shape, jnp.float32),
        in_specs=[pl.BlockSpec(memory_space=SMEM)] + in_vmem(2 + len(blocks)),
        out_specs=pl.BlockSpec(memory_space=pl.ANY),
        scratch_shapes=[
            pltpu.VMEM((groups + 2, 2, band, depth), jnp.float32),
            pltpu.VMEM((groups, 3, total, band, depth), jnp.float32),
            pltpu.SemaphoreType.DMA((groups, 3)),
        ],
        compiler_params=params(56),
        name="curl",
    )(me, *edges, *blocks)


def outline_kernel(*refs):
    row_low, row_high = refs[:2], refs[2:4]
    first_rows, last_rows = refs[5:]
    _, planes, lines, _ = row_low[0].shape
    for f in range(2):
        for c in range(3):
            for x in range(planes):
                first_rows[3 * f + c, pl.ds(x, 1), :] = row_low[f][c, x, pl.ds(0, 1), :]
                last_rows[3 * f + c, pl.ds(x, 1), :] = row_high[f][c, x, pl.ds(lines - 1, 1), :]


def outline_x_kernel(*refs):
    low, high = refs[:2], refs[2:4]
    first_x, last_x = refs[4:]
    for f in range(2):
        for c in range(3):
            first_x[3 * f + c] = low[f][c, 0]
            last_x[3 * f + c] = high[f][c, 0]


def outline_x(fields):
    _, planes, band, depth = fields[0].shape
    plane = (3, 1, band, depth)
    specs = [pl.BlockSpec(plane, lambda t: (0, 0, 0, 0))] * 2
    specs += [pl.BlockSpec(plane, lambda t: (0, planes - 1, 0, 0))] * 2
    shape = jax.ShapeDtypeStruct((6, band, depth), jnp.float32)
    return pl.pallas_call(
        outline_x_kernel,
        grid=(1,),
        out_shape=[shape] * 2,
        in_specs=specs,
        out_specs=[pl.BlockSpec(shape.shape, lambda t: (0, 0, 0))] * 2,
        compiler_params=params(56),
        name="outline_x",
    )(*fields, *fields)


def outline(fields, after):
    _, planes, band, depth = fields[0].shape
    lines = 8
    row = (3, planes, lines, depth)
    specs = [pl.BlockSpec(row, lambda t: (0, 0, 0, 0))] * 2
    specs += [pl.BlockSpec(row, lambda t: (0, 0, band // lines - 1, 0))] * 2
    specs += [pl.BlockSpec(memory_space=pl.ANY)]
    shape = jax.ShapeDtypeStruct((6, planes, depth), jnp.float32)
    return pl.pallas_call(
        outline_kernel,
        grid=(1,),
        out_shape=[shape] * 2,
        in_specs=specs,
        out_specs=[pl.BlockSpec(shape.shape, lambda t: (0, 0, 0))] * 2,
        compiler_params=params(56),
        name="outline",
    )(*fields, *fields, after)


def pick_kernel(groups, starts, me_ref, *refs):
    blocks, (low, high, sem) = by_step(refs[:groups]), refs[groups:]
    _, band, _ = low.shape
    me = me_ref[0]
    for place, (target, owner) in enumerate(((low, 0), (high, groups - 1))):
        for d in range(groups):

            @pl.when(lax.bitwise_xor(me, owner) == d)
            def _():
                copies = [
                    pltpu.make_async_copy(blocks[d].at[pl.ds(start, band), :], target.at[h], sem.at[place, h])
                    for h, start in enumerate(starts)
                ]
                for copy in copies:
                    copy.start()
                for copy in copies:
                    copy.wait()


def pick(me, starts, band, blocks):
    shape = jax.ShapeDtypeStruct((2, band, blocks[0].shape[1]), jnp.float32)
    return pl.pallas_call(
        functools.partial(pick_kernel, len(blocks), starts),
        out_shape=[shape] * 2,
        in_specs=[pl.BlockSpec(memory_space=SMEM)] + [pl.BlockSpec(memory_space=pl.ANY)] * len(blocks),
        out_specs=in_vmem(2),
        scratch_shapes=[pltpu.SemaphoreType.DMA((2, 2))],
        compiler_params=params(56),
        name="pick",
    )(me, *arranged(blocks))


def pairs(size, step):
    return [(i, i + step) for i in range(size) if 0 <= i + step < size]


def swap(blocks):
    groups = len(blocks)
    moved = [blocks[0]] + [None] * (groups - 1)
    for d in range(1, groups):
        moved[d] = lax.ppermute(blocks[d], "gy", [(i, i ^ d) for i in range(groups)])
    return moved


def on_device(vorticity, velocity_old, green_hat):
    groups = lax.axis_size("gy")
    across_x = lax.axis_size("gx")
    _, planes, band, depth = vorticity.shape
    rows = band * groups
    per_owner = planes // groups
    chunks = 2 if per_owner % 2 == 0 else 1
    width = per_owner // chunks
    me = lax.axis_index("gy")
    me_array = me.reshape(1)

    fields = (vorticity, velocity_old)
    first_x, last_x = outline_x(fields)
    from_x = (
        lax.ppermute(last_x, "gx", pairs(across_x, 1)),
        lax.ppermute(first_x, "gx", pairs(across_x, -1)),
    )
    first_rows, last_rows = outline(fields, first_x)
    halos = from_x + (
        lax.ppermute(last_rows, "gy", pairs(groups, 1)),
        lax.ppermute(first_rows, "gy", pairs(groups, -1)),
    )

    forward_z, inverse_z, ahead, back, _ = constants(rows, depth)
    tables = (jnp.asarray(forward_z), jnp.asarray(inverse_z), jnp.asarray(ahead), jnp.asarray(back))
    received = []
    vorticity_new = None
    riders = gain_riders(green_hat, depth)
    for k in range(chunks):
        vorticity_new, outs = advance(k, chunks, me_array, groups, vorticity, velocity_old, halos, riders, vorticity_new)
        received.append(swap(outs))
        if k == 0:
            green = gains(me, green_hat, riders[0], received[0], 3 * width * band)
    gauge = chunks == 2 and width == 2
    solved, carried = solve("first" if gauge else "plain", width, band, me_array, green, tables, received[0])
    returned = []
    if chunks == 2:
        solved, late = lax.optimization_barrier((solved, arranged(received[1])))
        received[1] = by_step(late)
    returned.append(swap(solved))
    if chunks == 2:
        solved, _ = solve("second" if gauge else "plain", width, band, me_array, green, tables, received[1], carried)
        returned.append(swap(solved))

    base = width * band * (0 if gauge else 1)
    early = returned[0]
    if chunks == 2:
        late = groups // 2 - 1
        early, returned[1][late] = lax.optimization_barrier((arranged(early), returned[1][late]))
        early = by_step(early)
    low, high = pick(me_array, (base, base + width * band), band, early)
    edges = (
        lax.ppermute(high, "gx", pairs(across_x, 1)),
        lax.ppermute(low, "gx", pairs(across_x, -1)),
    )
    blocks = [block for group in returned for block in arranged(group)]
    velocity = curl(me_array, groups, gauge, vorticity.shape, edges, blocks)
    return vorticity_new, velocity


def solution(mesh):
    placed = P(None, "gx", "gy", None)
    return jax.shard_map(
        on_device,
        mesh=mesh,
        in_specs=(placed, placed, P(None, "gy")),
        out_specs=(placed, placed),
        check_vma=False,
    )
```

time: 220 us -> 180 us (0.82)
  waiting for transfers between devices: 82 us -> 62.1 us
  Pallas kernels: 64.9 us -> 51.2 us
  between operations: 14.7 us -> 1.5 us
  starting transfers between devices: 46 us -> 53.7 us
  local copies, waits for them, and re-layouts: 10.2 us -> 4.48 us
  matrix products: 1.17 us -> 6.71 us
    ppermute x28, waiting for transfers between devices: 73.4 us -> 56.7 us  [swap(): lax.ppermute(blocks[d], 'gy', [(i, i ^ d) for i in range(groups)])]
    pallas_call x5 -> x8, Pallas kernels: 64.9 us -> 51.2 us  [the longest x2 27.4 us: solve(): pl.pallas_call(functools.partial(solve_kernel, groups, stage, width, band...]
    ppermute x28, starting transfers between devices: 27.8 us -> 35.8 us  [swap(): lax.ppermute(blocks[d], 'gy', [(i, i ^ d) for i in range(groups)])]
    dot_general x1 -> x3, matrix products: 1.17 us -> 6.71 us  [the longest x1 3.54 us: gains(): mixed = jnp.einsum('kjc,jmc->km', table, body, precision=highest)]
    ppermute x1, waiting for transfers between devices: 5.14 us -> 0.01 us  [on_device(): lax.ppermute(first_x, 'gx', pairs(across_x, -1))]
    ppermute x2, waiting for transfers between devices: 0.01 us -> 4.35 us  [the longest x1 4.34 us: on_device(): lax.ppermute(low, 'gx', pairs(across_x, -1))]
    slice x10 -> x1, local copies, waits for them, and re-layouts: 4.07 us -> 0.02 us  [gain_riders(): far = green_hat[:, 0].reshape(-1, depth)]
    ppermute x1, waiting for transfers between devices: 2.74 us -> 0.01 us  [on_device(): lax.ppermute(last_x, 'gx', pairs(across_x, 1))]
  transfers between devices with their start and end apart: 35 -> 34, of which waited for: 14 -> 11; matrix products, arithmetic and copies ran while one was open for 4% -> 5% of each run, Pallas kernels for 26% -> 22%
where the time goes in v2:
time: 180 us
  waiting for transfers between devices  62.1 us (34%)
  starting transfers between devices  53.7 us (30%)
  Pallas kernels  51.2 us (28%)
  matrix products  6.71 us (4%)
  local copies, waits for them, and re-layouts  4.48 us (2%)
    ppermute x28, waiting for transfers between devices, swap(): lax.ppermute(blocks[d], 'gy', [(i, i ^ d) for i in range(groups)])  56.7 us
    ppermute x28, starting transfers between devices, swap(): lax.ppermute(blocks[d], 'gy', [(i, i ^ d) for i in range(groups)])  35.8 us
    pallas_call x2, Pallas kernels, solve(): pl.pallas_call(functools.partial(solve_kernel, groups, stage, width, band...  27.4 us
    pallas_call x2, Pallas kernels, advance(): pl.pallas_call(functools.partial(advance_kernel, groups, chunk, chunks),...  13 us
    ppermute x1, waiting for transfers between devices, on_device(): lax.ppermute(low, 'gx', pairs(across_x, -1))  4.34 us
    ppermute x1, starting transfers between devices, on_device(): lax.ppermute(high, 'gx', pairs(across_x, 1))  4.28 us
    pallas_call x1, Pallas kernels, curl(): pl.pallas_call(functools.partial(curl_kernel, groups, gauge, total // chu...  3.9 us
    ppermute x1, starting transfers between devices, on_device(): lax.ppermute(first_rows, 'gy', pairs(groups, -1))  3.64 us
  transfers between devices with their start and end apart: 34, of which 11 were waited for; matrix products, arithmetic and copies ran while one was open for 5% of the time, Pallas kernels for 22%

profile of v2, /device:TPU:10, one launch (start us, length us, event | category | flops | bytes accessed | tf_op | source)
XLA Modules:
  0.0 179.7 jit_solution(2346534502173263098)
XLA Ops:
  0.6 1.8 %outline_x.1 = (f32[6,32,256]{2,1,0:T(8,128)}, f32[6,32,256]{2,1,0:T(8,128)}) custom-call(f32[3,32,32,256]{3,2,1,0:T(8,128)} %vort.3, f32[3,32,32,256]{3,2,1,0:T(8,128)} %vel.3, f32[3,32,32,256]{3,2,1,0:T(8,128)} %vort.3, f32[3,32,32,256]{3,2,1,0:T(8,128)} %vel.3), custom_call_target="tpu_custom_call" | custom-call | tf_op jit(solution)/shard_map/outline_x/pallas_call | solution.py:489
  2.4 3.4 %collective-permute-start = (f32[6,32,256]{2,1,0:T(8,128)}, f32[6,32,256]{2,1,0:T(8,128)S(1)}, u32[]{:S(2)}, u32[]{:S(2)}) collective-permute-start(f32[6,32,256]{2,1,0:T(8,128)} %get-tuple-element.80), channel_id=1, source_target_pairs={{0,8},{8,16},{16,24},{1,9},{9,17},{17,25},{2,10},{10,18},{18,26},{... | collective-permute-start | bytes 589832 | tf_op jit(solution)/shard_map/ppermute | solution.py:577
  5.9 2.6 %collective-permute-start.1 = (f32[6,32,256]{2,1,0:T(8,128)}, f32[6,32,256]{2,1,0:T(8,128)S(1)}, u32[]{:S(2)}, u32[]{:S(2)}) collective-permute-start(f32[6,32,256]{2,1,0:T(8,128)} %get-tuple-element.81.refs_4_), channel_id=1, source_target_pairs={{8,0},{16,8},{24,16},{9,1},{17,9},{25,17},{10,2},{18,10},{26,18},{... | collective-permute-start | bytes 589832 | tf_op jit(solution)/shard_map/ppermute | solution.py:578
  8.5 2.8 %outline.1 = (f32[6,32,256]{2,1,0:T(8,128)}, f32[6,32,256]{2,1,0:T(8,128)}) custom-call(f32[3,32,32,256]{3,2,1,0:T(8,128)} %vort.3, f32[3,32,32,256]{3,2,1,0:T(8,128)} %vel.3, f32[3,32,32,256]{3,2,1,0:T(8,128)} %vort.3, f32[3,32,32,256]{3,2,1,0:T(8,128)} %vel.3, f32[6,32,256]{2,1,0:T(8,128)} %get-tuple-element.81.refs_4_), custom_call_target="tpu_custom_call" | custom-call | tf_op jit(solution)/shard_map/outline/pallas_call | solution.py:508
  11.3 2.0 %collective-permute-start.2 = (f32[6,32,256]{2,1,0:T(8,128)}, f32[6,32,256]{2,1,0:T(8,128)S(1)}, u32[]{:S(2)}, u32[]{:S(2)}) collective-permute-start(f32[6,32,256]{2,1,0:T(8,128)} %get-tuple-element.82), channel_id=1, source_target_pairs={{0,1},{1,2},{2,3},{3,4},{4,5},{5,6},{6,7},{8,9},{9,10},{10,11},{11... | collective-permute-start | bytes 589832 | tf_op jit(solution)/shard_map/ppermute | solution.py:582
  13.3 3.6 %collective-permute-start.3 = (f32[6,32,256]{2,1,0:T(8,128)}, f32[6,32,256]{2,1,0:T(8,128)S(1)}, u32[]{:S(2)}, u32[]{:S(2)}) collective-permute-start(f32[6,32,256]{2,1,0:T(8,128)} %get-tuple-element.83), channel_id=1, source_target_pairs={{1,0},{2,1},{3,2},{4,3},{5,4},{6,5},{7,6},{9,8},{10,9},{11,10},{12... | collective-permute-start | bytes 589832 | tf_op jit(solution)/shard_map/ppermute | solution.py:583
  17.3 0.8 reshape.113.rest_0_
  18.7 0.6 pad.6.rest_1_
  19.4 1.1 collective-permute-done.3.yhi
  20.5 0.7 copy-done.5
  21.2 6.6 %advance_0.1 = (f32[3,32,32,256]{3,2,1,0:T(8,128)}, f32[192,256]{1,0:T(8,128)}, f32[320,256]{1,0:T(8,128)}, f32[320,256]{1,0:T(8,128)}, f32[320,256]{1,0:T(8,128...) custom-call(s32[1]{0:T(128)} %bitcast.me_ref, f32[3,32,32,256]{3,2,1,0:T(8,128)} %vort.3, ...), custom_call_target="tpu_custom_call" | custom-call | tf_op jit(solution)/shard_map/advance_0/pallas_call | solution.py:228
  27.7 2.7 %collective-permute-start.7 = (f32[200,256]{1,0:T(8,128)}, f32[200,256]{1,0:T(8,128)S(1)}, u32[]{:S(2)}, u32[]{:S(2)}) collective-permute-start(f32[200,256]{1,0:T(8,128)} %get-tuple-element.89), channel_id=1, source_target_pairs={{0,4},{1,5},{2,6},{3,7},{4,0},{5,1},{6,2},{7,3},{8,12},{9,13},{10,... | collective-permute-start | bytes 614408 | tf_op jit(solution)/shard_map/ppermute | solution.py:559
  30.4 1.5 collective-permute-start.8
  31.9 1.6 collective-permute-start.9
  34.0 6.5 %advance_1.1 = (f32[3,32,32,256]{3,2,1,0:T(8,128)}, f32[192,256]{1,0:T(8,128)}, f32[192,256]{1,0:T(8,128)}, f32[192,256]{1,0:T(8,128)}, f32[192,256]{1,0:T(8,128...) custom-call(s32[1]{0:T(128)} %bitcast.me_ref, ...), custom_call_target="tpu_custom_call", output_to_operand_aliasing={{0}: (7, {})} | custom-call | tf_op jit(solution)/shard_map/advance_1/pallas_call | solution.py:228
  40.5 13.3 %collective-permute-done.7.refs_7_ = f32[200,256]{1,0:T(8,128)S(1)} collective-permute-done((f32[200,256]{1,0:T(8,128)}, f32[200,256]{1,0:T(8,128)S(1)}, u32[]{:S(2)}, u32[]{:S(2)}) %collective-permute-start.7) | collective-permute-done | bytes 204832 | tf_op jit(solution)/shard_map/ppermute | solution.py:559
  53.8 4.4 %collective-permute-done.8.refs_5_ = f32[200,256]{1,0:T(8,128)S(1)} collective-permute-done((f32[200,256]{1,0:T(8,128)}, f32[200,256]{1,0:T(8,128)S(1)}, u32[]{:S(2)}, u32[]{:S(2)}) %collective-permute-start.8) | collective-permute-done | bytes 204832 | tf_op jit(solution)/shard_map/ppermute | solution.py:559
  58.2 4.4 %collective-permute-done.9.refs_3_ = f32[200,256]{1,0:T(8,128)S(1)} collective-permute-done((f32[200,256]{1,0:T(8,128)}, f32[200,256]{1,0:T(8,128)S(1)}, u32[]{:S(2)}, u32[]{:S(2)}) %collective-permute-start.9) | collective-permute-done | bytes 204832 | tf_op jit(solution)/shard_map/ppermute | solution.py:559
  62.6 3.7 %collective-permute-done.10.refs_1_ = f32[200,256]{1,0:T(8,128)S(1)} collective-permute-done((f32[200,256]{1,0:T(8,128)}, f32[200,256]{1,0:T(8,128)S(1)}, u32[]{:S(2)}, u32[]{:S(2)}) %collective-permute-start.10) | collective-permute-done | bytes 204832 | tf_op jit(solution)/shard_map/ppermute | solution.py:559
  66.4 4.2 %collective-permute-start.14 = (f32[192,256]{1,0:T(8,128)}, f32[192,256]{1,0:T(8,128)}, u32[]{:S(2)}, u32[]{:S(2)}) collective-permute-start(f32[192,256]{1,0:T(8,128)} %get-tuple-element.106), channel_id=1, source_target_pairs={{0,2},{1,3},{2,0},{3,1},{4,6},{5,7},{6,4},{7,5},{8,10},{9,11},{10,... | collective-permute-start | bytes 589832 | tf_op jit(solution)/shard_map/ppermute | solution.py:559
  70.7 3.8 %collective-permute-done.6.refs_2_ = f32[320,256]{1,0:T(8,128)S(1)} collective-permute-done((f32[320,256]{1,0:T(8,128)S(1)}, f32[320,256]{1,0:T(8,128)S(1)}, u32[]{:S(2)}, u32[]{:S(2)}) %collective-permute-start.6) | collective-permute-done | bytes 327712 | tf_op jit(solution)/shard_map/ppermute | solution.py:559
  74.4 4.8 %collective-permute-start.15 = (f32[192,256]{1,0:T(8,128)}, f32[192,256]{1,0:T(8,128)}, u32[]{:S(2)}, u32[]{:S(2)}) collective-permute-start(f32[192,256]{1,0:T(8,128)} %get-tuple-element.107), channel_id=1, source_target_pairs={{0,5},{1,4},{2,7},{3,6},{4,1},{5,0},{6,3},{7,2},{8,13},{9,12},{10,... | collective-permute-start | bytes 589832 | tf_op jit(solution)/shard_map/ppermute | solution.py:559
  79.3 0.6 gather_fusion
  80.2 3.5 %convolution_bitcast_fusion = f32[2,256,512]{2,1,0:T(8,128)S(1)} fusion(f32[4,512,64]{2,1,0:T(8,128)S(1)} %gather.11, f32[4,8,2,8,256]{4,3,2,1,0:T(8,128)S(1)} %bitcast.42, pred[4]{0:T(512)(128)(4,1)S(1)} %compare_and_fusion), kind=kOutput, calls=%fused_computation.1 | convolution fusion | flops 805437440 | bytes 2097156 | tf_op jit(solution)/shard_map/kjc,jmc->km/dot_general | solution.py:109
  83.7 1.3 fusion.5
  85.1 1.5 collective-permute-done.12.refs_2_
  86.7 1.9 %convolution_add_fusion.green = f32[256,512]{1,0:T(8,128)} fusion(f32[256,512]{1,0:T(8,128)S(1)} %fusion.5, f32[512,512]{1,0:T(8,128)S(1)} %copy-done, f32[2,256,512]{2,1,0:T(8,128)S(1)} %convolution_bitcast_fusion), kind=kOutput, calls=%fused_computation.2 | convolution fusion | flops 805437440 | bytes 2621440 | tf_op jit(solution)/shard_map/dot_general | solution.py:113
  88.6 13.5 %solve_first.1 = (f32[136,256]{1,0:T(8,128)}, f32[136,256]{1,0:T(8,128)}, f32[136,256]{1,0:T(8,128)}, f32[136,256]{1,0:T(8,128)}, f32[136,256]{1,0:T(8,128)}, /*...) custom-call(s32[1]{0:T(128)} %bitcast.me_ref, ...), custom_call_target="tpu_custom_call" | custom-call | tf_op jit(solution)/shard_map/solve_first/pallas_call | solution.py:354
  102.1 3.9 %collective-permute-start.18 = (f32[136,256]{1,0:T(8,128)}, f32[136,256]{1,0:T(8,128)S(1)}, u32[]{:S(2)}, u32[]{:S(2)}) collective-permute-start(f32[136,256]{1,0:T(8,128)} %get-tuple-element.111), channel_id=1, source_target_pairs={{0,7},{1,6},{2,5},{3,4},{4,3},{5,2},{6,1},{7,0},{8,15},{9,14},{10,... | collective-permute-start | bytes 417800 | tf_op jit(solution)/shard_map/ppermute | solution.py:559
  106.3 3.5 %collective-permute-start.20 = (f32[136,256]{1,0:T(8,128)}, f32[136,256]{1,0:T(8,128)S(1)}, u32[]{:S(2)}, u32[]{:S(2)}) collective-permute-start(f32[136,256]{1,0:T(8,128)} %get-tuple-element.113), channel_id=1, source_target_pairs={{0,6},{1,7},{2,4},{3,5},{4,2},{5,3},{6,0},{7,1},{8,14},{9,15},{10,... | collective-permute-start | bytes 417800 | tf_op jit(solution)/shard_map/ppermute | solution.py:559
  109.8 1.7 collective-permute-start.22
  111.5 13.9 %solve_second.1 = (f32[200,256]{1,0:T(8,128)}, f32[200,256]{1,0:T(8,128)}, f32[200,256]{1,0:T(8,128)}, f32[200,256]{1,0:T(8,128)}, f32[200,256]{1,0:T(8,128)}, /...) custom-call(s32[1]{0:T(128)} %bitcast.me_ref, bf16[512,768]{1,0:T(8,128)(2,1)} %constant.101.clone.fz, ...), custom_call_target="tpu_custom_call" | custom-call | tf_op jit(solution)/shard_map/solve_second/pallas_call | solution.py:354
  125.6 1.7 collective-permute-start.25
  127.3 1.1 collective-permute-start.28
  128.5 1.4 collective-permute-start.24
  129.9 1.7 collective-permute-start.29
  131.6 1.4 collective-permute-start.30
  132.9 16.0 %collective-permute-done.24.refs_7_ = f32[136,256]{1,0:T(8,128)S(1)} collective-permute-done((f32[136,256]{1,0:T(8,128)S(1)}, f32[136,256]{1,0:T(8,128)S(1)}, u32[]{:S(2)}, u32[]{:S(2)}) %collective-permute-start.24) | collective-permute-done | bytes 139296 | tf_op jit(solution)/shard_map/ppermute | solution.py:559
  148.9 2.6 %collective-permute-start.31 = (f32[200,256]{1,0:T(8,128)}, f32[200,256]{1,0:T(8,128)S(1)}, u32[]{:S(2)}, u32[]{:S(2)}) collective-permute-start(f32[200,256]{1,0:T(8,128)} %get-tuple-element.143), channel_id=1, source_target_pairs={{0,5},{1,4},{2,7},{3,6},{4,1},{5,0},{6,3},{7,2},{8,13},{9,12},{10,... | collective-permute-start | bytes 614408 | tf_op jit(solution)/shard_map/ppermute | solution.py:559
  151.5 0.9 collective-permute-start.32
  152.5 2.2 %pick.1 = (f32[2,32,256]{2,1,0:T(8,128)}, f32[2,32,256]{2,1,0:T(8,128)}) custom-call(s32[1]{0:T(128)} %bitcast.me_ref, f32[136,256]{1,0:T(8,128)} %get-tuple-element.128.refs_0_, f32[136,256]{1,0:T(8,128)} %copy-done.9, f32[136,256]{1,0:T(8,128)} %copy-done.10, f32[136,256]{1,0:T(8,128)} %copy-done.11, f32[136,256]{1,0:T(8,128)} %copy-done.12, ...), custom_call_target="tpu_custom_call" | custom-call | tf_op jit(solution)/shard_map/pick/pallas_call | solution.py:540
  154.7 8.7 %collective-permute-done.29.refs_11_ = f32[200,256]{1,0:T(8,128)S(1)} collective-permute-done((f32[200,256]{1,0:T(8,128)}, f32[200,256]{1,0:T(8,128)S(1)}, u32[]{:S(2)}, u32[]{:S(2)}) %collective-permute-start.29) | collective-permute-done | bytes 204832 | tf_op jit(solution)/shard_map/ppermute | solution.py:559
  163.4 4.3 %collective-permute-start.26 = (f32[2,32,256]{2,1,0:T(8,128)}, f32[2,32,256]{2,1,0:T(8,128)S(1)}, u32[]{:S(2)}, u32[]{:S(2)}) collective-permute-start(f32[2,32,256]{2,1,0:T(8,128)} %get-tuple-element.136), channel_id=1, source_target_pairs={{0,8},{8,16},{16,24},{1,9},{9,17},{17,25},{2,10},{10,18},{18,26},{... | collective-permute-start | bytes 196616 | tf_op jit(solution)/shard_map/ppermute | solution.py:615
  167.7 1.9 %collective-permute-start.27 = (f32[2,32,256]{2,1,0:T(8,128)}, f32[2,32,256]{2,1,0:T(8,128)S(1)}, u32[]{:S(2)}, u32[]{:S(2)}) collective-permute-start(f32[2,32,256]{2,1,0:T(8,128)} %get-tuple-element.137), channel_id=1, source_target_pairs={{8,0},{16,8},{24,16},{9,1},{17,9},{25,17},{10,2},{18,10},{26,18},{... | collective-permute-start | bytes 196616 | tf_op jit(solution)/shard_map/ppermute | solution.py:616
  169.7 0.9 collective-permute-done.33.refs_15_
  170.7 4.3 %collective-permute-done.27.xhi = f32[2,32,256]{2,1,0:T(8,128)S(1)} collective-permute-done((f32[2,32,256]{2,1,0:T(8,128)}, f32[2,32,256]{2,1,0:T(8,128)S(1)}, u32[]{:S(2)}, u32[]{:S(2)}) %collective-permute-start.27) | collective-permute-done | bytes 65568 | tf_op jit(solution)/shard_map/ppermute | solution.py:616
  175.1 0.6 copy-done.32
  175.7 3.9 %curl.1 = f32[3,32,32,256]{3,2,1,0:T(8,128)} custom-call(s32[1]{0:T(128)} %bitcast.me_ref, f32[2,32,256]{2,1,0:T(8,128)} %copy-done.31, f32[2,32,256]{2,1,0:T(8,128)} %copy-done.32, f32[136,256]{1,0:T(8,128)} %get-tuple-element.128.refs_0_, f32[136,256]{1,0:T(8,128)} %copy-done.9, f32[136,256]{1,0:T(8,128)} %copy-done.10, f32[136,256]{1,0:T(8,128)} %copy-done.11, ...), custom_call_target="tpu_custom_call" | custom-call | tf_op jit(solution)/shard_map/curl/pallas_call | solution.py:448
  (135 shorter events, 2.7 us)
Async XLA Ops:
  2.4 16.9 %collective-permute-start = (f32[6,32,256]{2,1,0:T(8,128)}, f32[6,32,256]{2,1,0:T(8,128)S(1)}, u32[]{:S(2)}, u32[]{:S(2)}) collective-permute-start(f32[6,32,256]{2,1,0:T(8,128)} %get-tuple-element.80), channel_id=1, source_target_pairs={{0,8},{8,16},{16,24},{1,9},{9,17},{17,25},{2,10},{10,18},{18,26},{... | collective-permute-start | bytes 589832 | tf_op jit(solution)/shard_map/ppermute | solution.py:577
  5.9 13.5 %collective-permute-start.1 = (f32[6,32,256]{2,1,0:T(8,128)}, f32[6,32,256]{2,1,0:T(8,128)S(1)}, u32[]{:S(2)}, u32[]{:S(2)}) collective-permute-start(f32[6,32,256]{2,1,0:T(8,128)} %get-tuple-element.81.refs_4_), channel_id=1, source_target_pairs={{8,0},{16,8},{24,16},{9,1},{17,9},{25,17},{10,2},{18,10},{26,18},{... | collective-permute-start | bytes 589832 | tf_op jit(solution)/shard_map/ppermute | solution.py:578
  11.3 8.1 %collective-permute-start.2 = (f32[6,32,256]{2,1,0:T(8,128)}, f32[6,32,256]{2,1,0:T(8,128)S(1)}, u32[]{:S(2)}, u32[]{:S(2)}) collective-permute-start(f32[6,32,256]{2,1,0:T(8,128)} %get-tuple-element.82), channel_id=1, source_target_pairs={{0,1},{1,2},{2,3},{3,4},{4,5},{5,6},{6,7},{8,9},{9,10},{10,11},{11... | collective-permute-start | bytes 589832 | tf_op jit(solution)/shard_map/ppermute | solution.py:582
  13.3 7.1 %collective-permute-start.3 = (f32[6,32,256]{2,1,0:T(8,128)}, f32[6,32,256]{2,1,0:T(8,128)S(1)}, u32[]{:S(2)}, u32[]{:S(2)}) collective-permute-start(f32[6,32,256]{2,1,0:T(8,128)} %get-tuple-element.83), channel_id=1, source_target_pairs={{1,0},{2,1},{3,2},{4,3},{5,4},{6,5},{7,6},{9,8},{10,9},{11,10},{12... | collective-permute-start | bytes 589832 | tf_op jit(solution)/shard_map/ppermute | solution.py:583
  27.7 26.0 %collective-permute-start.7 = (f32[200,256]{1,0:T(8,128)}, f32[200,256]{1,0:T(8,128)S(1)}, u32[]{:S(2)}, u32[]{:S(2)}) collective-permute-start(f32[200,256]{1,0:T(8,128)} %get-tuple-element.89), channel_id=1, source_target_pairs={{0,4},{1,5},{2,6},{3,7},{4,0},{5,1},{6,2},{7,3},{8,12},{9,13},{10,... | collective-permute-start | bytes 614408 | tf_op jit(solution)/shard_map/ppermute | solution.py:559
  30.4 27.8 %collective-permute-start.8 = (f32[200,256]{1,0:T(8,128)}, f32[200,256]{1,0:T(8,128)S(1)}, u32[]{:S(2)}, u32[]{:S(2)}) collective-permute-start(f32[200,256]{1,0:T(8,128)} %get-tuple-element.90), channel_id=1, source_target_pairs={{0,5},{1,4},{2,7},{3,6},{4,1},{5,0},{6,3},{7,2},{8,13},{9,12},{10,... | collective-permute-start | bytes 614408 | tf_op jit(solution)/shard_map/ppermute | solution.py:559
  31.9 30.7 %collective-permute-start.9 = (f32[200,256]{1,0:T(8,128)}, f32[200,256]{1,0:T(8,128)S(1)}, u32[]{:S(2)}, u32[]{:S(2)}) collective-permute-start(f32[200,256]{1,0:T(8,128)} %get-tuple-element.91), channel_id=1, source_target_pairs={{0,6},{1,7},{2,4},{3,5},{4,2},{5,3},{6,0},{7,1},{8,14},{9,15},{10,... | collective-permute-start | bytes 614408 | tf_op jit(solution)/shard_map/ppermute | solution.py:559
  33.5 32.8 %collective-permute-start.10 = (f32[200,256]{1,0:T(8,128)}, f32[200,256]{1,0:T(8,128)S(1)}, u32[]{:S(2)}, u32[]{:S(2)}) collective-permute-start(f32[200,256]{1,0:T(8,128)} %get-tuple-element.92), channel_id=1, source_target_pairs={{0,7},{1,6},{2,5},{3,4},{4,3},{5,2},{6,1},{7,0},{8,15},{9,14},{10,... | collective-permute-start | bytes 614408 | tf_op jit(solution)/shard_map/ppermute | solution.py:559
  33.5 32.8 %collective-permute-start.4 = (f32[320,256]{1,0:T(8,128)}, f32[320,256]{1,0:T(8,128)S(1)}, u32[]{:S(2)}, u32[]{:S(2)}) collective-permute-start(f32[320,256]{1,0:T(8,128)} %get-tuple-element.86), channel_id=1, source_target_pairs={{0,1},{1,0},{2,3},{3,2},{4,5},{5,4},{6,7},{7,6},{8,9},{9,8},{10,11... | collective-permute-start | bytes 983048 | tf_op jit(solution)/shard_map/ppermute | solution.py:559
  34.0 19.8 %copy-start.35 = (f32[320,256]{1,0:T(8,128)S(1)}, f32[320,256]{1,0:T(8,128)}, u32[]{:S(2)}) copy-start(f32[320,256]{1,0:T(8,128)} %get-tuple-element.87) | copy-start | bytes 983044
  34.0 24.2 %copy-start.34 = (f32[320,256]{1,0:T(8,128)S(1)}, f32[320,256]{1,0:T(8,128)}, u32[]{:S(2)}) copy-start(f32[320,256]{1,0:T(8,128)} %get-tuple-element.88) | copy-start | bytes 983044
  53.8 12.6 %collective-permute-start.5 = (f32[320,256]{1,0:T(8,128)S(1)}, f32[320,256]{1,0:T(8,128)S(1)}, u32[]{:S(2)}, u32[]{:S(2)}) collective-permute-start(f32[320,256]{1,0:T(8,128)S(1)} %copy-done.35), channel_id=1, source_target_pairs={{0,2},{1,3},{2,0},{3,1},{4,6},{5,7},{6,4},{7,5},{8,10},{9,11},{10,... | collective-permute-start | bytes 983048 | tf_op jit(solution)/shard_map/ppermute | solution.py:559
  58.2 16.2 %collective-permute-start.6 = (f32[320,256]{1,0:T(8,128)S(1)}, f32[320,256]{1,0:T(8,128)S(1)}, u32[]{:S(2)}, u32[]{:S(2)}) collective-permute-start(f32[320,256]{1,0:T(8,128)S(1)} %copy-done.34), channel_id=1, source_target_pairs={{0,3},{1,2},{2,1},{3,0},{4,7},{5,6},{6,5},{7,4},{8,11},{9,10},{10,... | collective-permute-start | bytes 983048 | tf_op jit(solution)/shard_map/ppermute | solution.py:559
  62.6 16.7 %copy-start.19 = (f32[200,256]{1,0:T(8,128)}, f32[200,256]{1,0:T(8,128)S(1)}, u32[]{:S(2)}) copy-start(f32[200,256]{1,0:T(8,128)S(1)} %collective-permute-done.9.refs_3_) | copy-start | bytes 614404
  62.6 22.4 %collective-permute-start.11 = (f32[192,256]{1,0:T(8,128)}, f32[192,256]{1,0:T(8,128)}, u32[]{:S(2)}, u32[]{:S(2)}) collective-permute-start(f32[192,256]{1,0:T(8,128)} %get-tuple-element.103), channel_id=1, source_target_pairs={{0,7},{1,6},{2,5},{3,4},{4,3},{5,2},{6,1},{7,0},{8,15},{9,14},{10,... | collective-permute-start | bytes 589832 | tf_op jit(solution)/shard_map/ppermute | solution.py:559
  66.3 20.4 %collective-permute-start.12 = (f32[192,256]{1,0:T(8,128)}, f32[192,256]{1,0:T(8,128)}, u32[]{:S(2)}, u32[]{:S(2)}) collective-permute-start(f32[192,256]{1,0:T(8,128)} %get-tuple-element.104), channel_id=1, source_target_pairs={{0,3},{1,2},{2,1},{3,0},{4,7},{5,6},{6,5},{7,4},{8,11},{9,10},{10,... | collective-permute-start | bytes 589832 | tf_op jit(solution)/shard_map/ppermute | solution.py:559
  66.3 17.4 %copy-start.6 = (f32[320,256]{1,0:T(8,128)}, f32[320,256]{1,0:T(8,128)S(1)}, u32[]{:S(2)}) copy-start(f32[320,256]{1,0:T(8,128)S(1)} %collective-permute-done.4.refs_6_) | copy-start | bytes 983044
  66.3 35.7 %collective-permute-start.13 = (f32[192,256]{1,0:T(8,128)}, f32[192,256]{1,0:T(8,128)}, u32[]{:S(2)}, u32[]{:S(2)}) collective-permute-start(f32[192,256]{1,0:T(8,128)} %get-tuple-element.105), channel_id=1, source_target_pairs={{0,6},{1,7},{2,4},{3,5},{4,2},{5,3},{6,0},{7,1},{8,14},{9,15},{10,... | collective-permute-start | bytes 589832 | tf_op jit(solution)/shard_map/ppermute | solution.py:559
  66.4 35.6 %collective-permute-start.14 = (f32[192,256]{1,0:T(8,128)}, f32[192,256]{1,0:T(8,128)}, u32[]{:S(2)}, u32[]{:S(2)}) collective-permute-start(f32[192,256]{1,0:T(8,128)} %get-tuple-element.106), channel_id=1, source_target_pairs={{0,2},{1,3},{2,0},{3,1},{4,6},{5,7},{6,4},{7,5},{8,10},{9,11},{10,... | collective-permute-start | bytes 589832 | tf_op jit(solution)/shard_map/ppermute | solution.py:559
  74.4 27.6 %collective-permute-start.15 = (f32[192,256]{1,0:T(8,128)}, f32[192,256]{1,0:T(8,128)}, u32[]{:S(2)}, u32[]{:S(2)}) collective-permute-start(f32[192,256]{1,0:T(8,128)} %get-tuple-element.107), channel_id=1, source_target_pairs={{0,5},{1,4},{2,7},{3,6},{4,1},{5,0},{6,3},{7,2},{8,13},{9,12},{10,... | collective-permute-start | bytes 589832 | tf_op jit(solution)/shard_map/ppermute | solution.py:559
  85.0 17.0 %collective-permute-start.16 = (f32[192,256]{1,0:T(8,128)S(1)}, f32[192,256]{1,0:T(8,128)S(1)}, u32[]{:S(2)}, u32[]{:S(2)}) collective-permute-start(f32[192,256]{1,0:T(8,128)S(1)} %copy-done.37), channel_id=1, source_target_pairs={{0,1},{1,0},{2,3},{3,2},{4,5},{5,4},{6,7},{7,6},{8,9},{9,8},{10,11... | collective-permute-start | bytes 589832 | tf_op jit(solution)/shard_map/ppermute | solution.py:559
  86.7 15.4 %collective-permute-start.17 = (f32[192,256]{1,0:T(8,128)S(1)}, f32[192,256]{1,0:T(8,128)S(1)}, u32[]{:S(2)}, u32[]{:S(2)}) collective-permute-start(f32[192,256]{1,0:T(8,128)S(1)} %copy-done.36), channel_id=1, source_target_pairs={{0,4},{1,5},{2,6},{3,7},{4,0},{5,1},{6,2},{7,3},{8,12},{9,13},{10,... | collective-permute-start | bytes 589832 | tf_op jit(solution)/shard_map/ppermute | solution.py:559
  102.1 23.2 %collective-permute-start.18 = (f32[136,256]{1,0:T(8,128)}, f32[136,256]{1,0:T(8,128)S(1)}, u32[]{:S(2)}, u32[]{:S(2)}) collective-permute-start(f32[136,256]{1,0:T(8,128)} %get-tuple-element.111), channel_id=1, source_target_pairs={{0,7},{1,6},{2,5},{3,4},{4,3},{5,2},{6,1},{7,0},{8,15},{9,14},{10,... | collective-permute-start | bytes 417800 | tf_op jit(solution)/shard_map/ppermute | solution.py:559
  106.0 19.6 %collective-permute-start.19 = (f32[136,256]{1,0:T(8,128)}, f32[136,256]{1,0:T(8,128)S(1)}, u32[]{:S(2)}, u32[]{:S(2)}) collective-permute-start(f32[136,256]{1,0:T(8,128)} %get-tuple-element.112), channel_id=1, source_target_pairs={{0,3},{1,2},{2,1},{3,0},{4,7},{5,6},{6,5},{7,4},{8,11},{9,10},{10,... | collective-permute-start | bytes 417800 | tf_op jit(solution)/shard_map/ppermute | solution.py:559
  106.3 21.0 %collective-permute-start.20 = (f32[136,256]{1,0:T(8,128)}, f32[136,256]{1,0:T(8,128)S(1)}, u32[]{:S(2)}, u32[]{:S(2)}) collective-permute-start(f32[136,256]{1,0:T(8,128)} %get-tuple-element.113), channel_id=1, source_target_pairs={{0,6},{1,7},{2,4},{3,5},{4,2},{5,3},{6,0},{7,1},{8,14},{9,15},{10,... | collective-permute-start | bytes 417800 | tf_op jit(solution)/shard_map/ppermute | solution.py:559
  109.8 18.7 %collective-permute-start.21 = (f32[136,256]{1,0:T(8,128)}, f32[136,256]{1,0:T(8,128)S(1)}, u32[]{:S(2)}, u32[]{:S(2)}) collective-permute-start(f32[136,256]{1,0:T(8,128)} %get-tuple-element.114), channel_id=1, source_target_pairs={{0,2},{1,3},{2,0},{3,1},{4,6},{5,7},{6,4},{7,5},{8,10},{9,11},{10,... | collective-permute-start | bytes 417800 | tf_op jit(solution)/shard_map/ppermute | solution.py:559
  109.8 20.1 %collective-permute-start.22 = (f32[136,256]{1,0:T(8,128)}, f32[136,256]{1,0:T(8,128)S(1)}, u32[]{:S(2)}, u32[]{:S(2)}) collective-permute-start(f32[136,256]{1,0:T(8,128)} %get-tuple-element.115), channel_id=1, source_target_pairs={{0,5},{1,4},{2,7},{3,6},{4,1},{5,0},{6,3},{7,2},{8,13},{9,12},{10,... | collective-permute-start | bytes 417800 | tf_op jit(solution)/shard_map/ppermute | solution.py:559
  111.4 13.9 %copy-start.39 = (f32[136,256]{1,0:T(8,128)S(1)}, f32[136,256]{1,0:T(8,128)}, u32[]{:S(2)}) copy-start(f32[136,256]{1,0:T(8,128)} %get-tuple-element.116) | copy-start | bytes 417796
  111.5 17.0 %copy-start.38 = (f32[136,256]{1,0:T(8,128)S(1)}, f32[136,256]{1,0:T(8,128)}, u32[]{:S(2)}) copy-start(f32[136,256]{1,0:T(8,128)} %get-tuple-element.117) | copy-start | bytes 417796
  125.3 27.1 %copy-start.9 = (f32[136,256]{1,0:T(8,128)}, f32[136,256]{1,0:T(8,128)S(1)}, u32[]{:S(2)}) copy-start(f32[136,256]{1,0:T(8,128)S(1)} %collective-permute-done.18.refs_1_) | copy-start | bytes 417796
  125.4 6.2 %collective-permute-start.23 = (f32[136,256]{1,0:T(8,128)S(1)}, f32[136,256]{1,0:T(8,128)S(1)}, u32[]{:S(2)}, u32[]{:S(2)}) collective-permute-start(f32[136,256]{1,0:T(8,128)S(1)} %copy-done.39), channel_id=1, source_target_pairs={{0,1},{1,0},{2,3},{3,2},{4,5},{5,4},{6,7},{7,6},{8,9},{9,8},{10,11... | collective-permute-start | bytes 417800 | tf_op jit(solution)/shard_map/ppermute | solution.py:559
  125.6 26.8 %copy-start.10 = (f32[136,256]{1,0:T(8,128)}, f32[136,256]{1,0:T(8,128)S(1)}, u32[]{:S(2)}) copy-start(f32[136,256]{1,0:T(8,128)S(1)} %collective-permute-done.19.refs_2_) | copy-start | bytes 417796
  125.6 25.8 %collective-permute-start.25 = (f32[200,256]{1,0:T(8,128)}, f32[200,256]{1,0:T(8,128)S(1)}, u32[]{:S(2)}, u32[]{:S(2)}) collective-permute-start(f32[200,256]{1,0:T(8,128)} %get-tuple-element.127), channel_id=1, source_target_pairs={{0,3},{1,2},{2,1},{3,0},{4,7},{5,6},{6,5},{7,4},{8,11},{9,10},{10,... | collective-permute-start | bytes 614408 | tf_op jit(solution)/shard_map/ppermute | solution.py:559
  127.3 25.1 %copy-start.11 = (f32[136,256]{1,0:T(8,128)}, f32[136,256]{1,0:T(8,128)S(1)}, u32[]{:S(2)}) copy-start(f32[136,256]{1,0:T(8,128)S(1)} %collective-permute-done.20.refs_3_) | copy-start | bytes 417796
  127.3 25.0 %collective-permute-start.28 = (f32[200,256]{1,0:T(8,128)}, f32[200,256]{1,0:T(8,128)S(1)}, u32[]{:S(2)}, u32[]{:S(2)}) collective-permute-start(f32[200,256]{1,0:T(8,128)} %get-tuple-element.139), channel_id=1, source_target_pairs={{0,7},{1,6},{2,5},{3,4},{4,3},{5,2},{6,1},{7,0},{8,15},{9,14},{10,... | collective-permute-start | bytes 614408 | tf_op jit(solution)/shard_map/ppermute | solution.py:559
  128.5 24.0 %copy-start.12 = (f32[136,256]{1,0:T(8,128)}, f32[136,256]{1,0:T(8,128)S(1)}, u32[]{:S(2)}) copy-start(f32[136,256]{1,0:T(8,128)S(1)} %collective-permute-done.21.refs_4_) | copy-start | bytes 417796
  128.5 20.4 %collective-permute-start.24 = (f32[136,256]{1,0:T(8,128)S(1)}, f32[136,256]{1,0:T(8,128)S(1)}, u32[]{:S(2)}, u32[]{:S(2)}) collective-permute-start(f32[136,256]{1,0:T(8,128)S(1)} %copy-done.38), channel_id=1, source_target_pairs={{0,4},{1,5},{2,6},{3,7},{4,0},{5,1},{6,2},{7,3},{8,12},{9,13},{10,... | collective-permute-start | bytes 417800 | tf_op jit(solution)/shard_map/ppermute | solution.py:559
  129.9 22.6 %copy-start.13 = (f32[136,256]{1,0:T(8,128)}, f32[136,256]{1,0:T(8,128)S(1)}, u32[]{:S(2)}) copy-start(f32[136,256]{1,0:T(8,128)S(1)} %collective-permute-done.22.refs_5_) | copy-start | bytes 417796
  129.9 33.6 %collective-permute-start.29 = (f32[200,256]{1,0:T(8,128)}, f32[200,256]{1,0:T(8,128)S(1)}, u32[]{:S(2)}, u32[]{:S(2)}) collective-permute-start(f32[200,256]{1,0:T(8,128)} %get-tuple-element.141), channel_id=1, source_target_pairs={{0,6},{1,7},{2,4},{3,5},{4,2},{5,3},{6,0},{7,1},{8,14},{9,15},{10,... | collective-permute-start | bytes 614408 | tf_op jit(solution)/shard_map/ppermute | solution.py:559
  131.6 20.9 %copy-start.14 = (f32[136,256]{1,0:T(8,128)}, f32[136,256]{1,0:T(8,128)S(1)}, u32[]{:S(2)}) copy-start(f32[136,256]{1,0:T(8,128)S(1)} %collective-permute-done.23.refs_6_) | copy-start | bytes 417796
  131.6 36.2 %collective-permute-start.30 = (f32[200,256]{1,0:T(8,128)}, f32[200,256]{1,0:T(8,128)S(1)}, u32[]{:S(2)}, u32[]{:S(2)}) collective-permute-start(f32[200,256]{1,0:T(8,128)} %get-tuple-element.142), channel_id=1, source_target_pairs={{0,2},{1,3},{2,0},{3,1},{4,6},{5,7},{6,4},{7,5},{8,10},{9,11},{10,... | collective-permute-start | bytes 614408 | tf_op jit(solution)/shard_map/ppermute | solution.py:559
  148.9 20.8 %collective-permute-start.31 = (f32[200,256]{1,0:T(8,128)}, f32[200,256]{1,0:T(8,128)S(1)}, u32[]{:S(2)}, u32[]{:S(2)}) collective-permute-start(f32[200,256]{1,0:T(8,128)} %get-tuple-element.143), channel_id=1, source_target_pairs={{0,5},{1,4},{2,7},{3,6},{4,1},{5,0},{6,3},{7,2},{8,13},{9,12},{10,... | collective-permute-start | bytes 614408 | tf_op jit(solution)/shard_map/ppermute | solution.py:559
  151.5 23.6 %copy-start.21 = (f32[200,256]{1,0:T(8,128)}, f32[200,256]{1,0:T(8,128)S(1)}, u32[]{:S(2)}) copy-start(f32[200,256]{1,0:T(8,128)S(1)} %collective-permute-done.25.refs_10_) | copy-start | bytes 614404
  151.5 18.2 %collective-permute-start.32 = (f32[200,256]{1,0:T(8,128)}, f32[200,256]{1,0:T(8,128)S(1)}, u32[]{:S(2)}, u32[]{:S(2)}) collective-permute-start(f32[200,256]{1,0:T(8,128)} %get-tuple-element.144), channel_id=1, source_target_pairs={{0,1},{1,0},{2,3},{3,2},{4,5},{5,4},{6,7},{7,6},{8,9},{9,8},{10,11... | collective-permute-start | bytes 614408 | tf_op jit(solution)/shard_map/ppermute | solution.py:559
  152.4 22.6 %copy-start.22 = (f32[200,256]{1,0:T(8,128)}, f32[200,256]{1,0:T(8,128)S(1)}, u32[]{:S(2)}) copy-start(f32[200,256]{1,0:T(8,128)S(1)} %collective-permute-done.28.refs_9_) | copy-start | bytes 614404
  152.4 18.3 %collective-permute-start.33 = (f32[200,256]{1,0:T(8,128)}, f32[200,256]{1,0:T(8,128)S(1)}, u32[]{:S(2)}, u32[]{:S(2)}) collective-permute-start(f32[200,256]{1,0:T(8,128)} %get-tuple-element.145), channel_id=1, source_target_pairs={{0,4},{1,5},{2,6},{3,7},{4,0},{5,1},{6,2},{7,3},{8,12},{9,13},{10,... | collective-permute-start | bytes 614408 | tf_op jit(solution)/shard_map/ppermute | solution.py:559
  163.4 7.2 %collective-permute-start.26 = (f32[2,32,256]{2,1,0:T(8,128)}, f32[2,32,256]{2,1,0:T(8,128)S(1)}, u32[]{:S(2)}, u32[]{:S(2)}) collective-permute-start(f32[2,32,256]{2,1,0:T(8,128)} %get-tuple-element.136), channel_id=1, source_target_pairs={{0,8},{8,16},{16,24},{1,9},{9,17},{17,25},{2,10},{10,18},{18,26},{... | collective-permute-start | bytes 196616 | tf_op jit(solution)/shard_map/ppermute | solution.py:615
  167.7 7.3 %collective-permute-start.27 = (f32[2,32,256]{2,1,0:T(8,128)}, f32[2,32,256]{2,1,0:T(8,128)S(1)}, u32[]{:S(2)}, u32[]{:S(2)}) collective-permute-start(f32[2,32,256]{2,1,0:T(8,128)} %get-tuple-element.137), channel_id=1, source_target_pairs={{8,0},{16,8},{24,16},{9,1},{17,9},{25,17},{10,2},{18,10},{26,18},{... | collective-permute-start | bytes 196616 | tf_op jit(solution)/shard_map/ppermute | solution.py:616
  (26 other events, 162.0 us)

commit v3 on v2

--- a/solution.py
+++ b/solution.py
@@ -117,16 +117,18 @@
     return owner * total + jnp.where((owner & 1) == 0, local, total - 1 - local)
 
 
-def arranged(blocks):
-    return [blocks[d] for d in sequence_of(len(blocks))]
-
-
-def by_step(blocks):
-    places = {d: n for n, d in enumerate(sequence_of(len(blocks)))}
+def arranged(blocks, back=False):
+    return [blocks[d] for d in sequence_of(len(blocks), back)]
+
+
+def by_step(blocks, back=False):
+    places = {d: n for n, d in enumerate(sequence_of(len(blocks), back))}
     return [blocks[places[d]] for d in range(len(blocks))]
 
 
-def sequence_of(groups):
+def sequence_of(groups, back):
+    if back:
+        return [0] + list(range(groups - 1, 0, -1))
     far = list(range(groups - 1, groups // 2 - 1, -1))
     near = list(range(groups // 2 - 1, 0, -1))
     mixed = [0]
@@ -136,8 +138,8 @@
     return mixed
 
 
-def advance_kernel(groups, chunk, chunks, me_ref, vort, vel, xlo, xhi, ylo, yhi, *rest):
-    new, sends = rest[-groups - 5], rest[-groups - 4 : -4]
+def advance_kernel(steps, chunk, chunks, me_ref, vort, vel, xlo, xhi, ylo, yhi, *rest):
+    new, sends = rest[-len(steps) - 5], rest[-len(steps) - 4 : -4]
     frame, block, load_sem, store_sem = rest[-4:]
     _, planes, band, depth = vort.shape
     width = frame.shape[3] - 2
@@ -146,32 +148,31 @@
     column = lax.broadcasted_iota(jnp.int32, (band, depth), 1)
     first_row, last_row = row == 0, row == band - 1
     first_column, last_column = column == 0, column == depth - 1
-    sequence = arranged(range(groups))
     place, loads, stores = {}, {}, []
-    for d in sequence:
+    for n, d in enumerate(steps):
         owner = lax.bitwise_xor(me, d)
         even = (owner & 1) == 0
         low = chunk * width
         start = owner * width * chunks + jnp.where(even, low, width * chunks - width - low)
         base = jnp.clip(start - 1, 0, planes - width - 2)
-        place[d] = (even, start, base)
-        loads[d] = [
-            pltpu.make_async_copy(field.at[:, pl.ds(base, width + 2)], frame.at[d, f], load_sem.at[d, f])
+        place[n] = (even, start, base)
+        loads[n] = [
+            pltpu.make_async_copy(field.at[:, pl.ds(base, width + 2)], frame.at[n, f], load_sem.at[n, f])
             for f, field in enumerate((vort, vel))
         ]
-        for load in loads[d]:
+        for load in loads[n]:
             load.start()
     lines = 3 * width * band
-    if chunk == 0:
-        near, far = rest[:2]
-        for d in sequence[1:]:
-            rider = near if d < groups // 2 else far
-            target = sends[d].at[pl.ds(lines, rider.shape[0]), :]
-            stores.append(pltpu.make_async_copy(rider, target, store_sem.at[d, 1 + width]))
-            stores[-1].start()
-    for d in sequence:
-        even, start, base = place[d]
-        for load in loads[d]:
+    if sends[-1].shape[0] > lines:
+        rider = rest[0]
+        for n, d in enumerate(steps):
+            if d > 0:
+                target = sends[n].at[pl.ds(lines, rider.shape[0]), :]
+                stores.append(pltpu.make_async_copy(rider, target, store_sem.at[n, 1 + width]))
+                stores[-1].start()
+    for n in range(len(steps)):
+        even, start, base = place[n]
+        for load in loads[n]:
             load.wait()
         for s in range(width):
             x = start + s
@@ -181,8 +182,8 @@
 
             def neighbours(f, c):
                 slot = 3 * f + c
-                here = frame[d, f, c, here_at]
-                before, after = frame[d, f, c, before_at], frame[d, f, c, after_at]
+                here = frame[n, f, c, here_at]
+                before, after = frame[n, f, c, before_at], frame[n, f, c, after_at]
                 if s == 0:
                     before = jnp.where(x > 0, before, xlo[slot])
                 if s == width - 1:
@@ -194,52 +195,52 @@
                 return here, after, before, up, down, right, left
 
             local = jnp.where(even, s, width - 1 - s)
-            w = [frame[d, 0, c, here_at] for c in range(3)]
+            w = [frame[n, 0, c, here_at] for c in range(3)]
             for c in range(3):
                 _, xp, xm, yp, ym, zp, zm = neighbours(1, c)
                 stretch = 0.5 * (w[0] * (xp - xm) + w[1] * (yp - ym) + w[2] * (zp - zm))
                 here, xp, xm, yp, ym, zp, zm = neighbours(0, c)
                 laplace = xp + xm + yp + ym + zp + zm - 6.0 * here
                 line = pl.multiple_of((c * width + local) * band, band)
-                block[d, pl.ds(line, band), :] = here + time_step * (stretch + viscosity * laplace)
-        stores.append(pltpu.make_async_copy(block.at[d], sends[d].at[pl.ds(0, lines), :], store_sem.at[d, 0]))
+                block[n, pl.ds(line, band), :] = here + time_step * (stretch + viscosity * laplace)
+        stores.append(pltpu.make_async_copy(block.at[n], sends[n].at[pl.ds(0, lines), :], store_sem.at[n, 0]))
         stores[-1].start()
         for s in range(width):
             local = jnp.where(even, s, width - 1 - s)
             for c in range(3):
                 line = pl.multiple_of((c * width + local) * band, band)
-                source = block.at[d, pl.ds(line, band), :]
-                stores.append(pltpu.make_async_copy(source, new.at[c, start + s], store_sem.at[d, 2 + width + 3 * s + c]))
+                source = block.at[n, pl.ds(line, band), :]
+                stores.append(pltpu.make_async_copy(source, new.at[c, start + s], store_sem.at[n, 2 + width + 3 * s + c]))
                 stores[-1].start()
     for store in stores:
         store.wait()
 
 
-def advance(chunk, chunks, me, groups, vort, vel, halos, riders, partial):
+def advance(steps, chunk, chunks, me, groups, vort, vel, halos, rider, partial):
     _, planes, band, depth = vort.shape
     width = planes // groups // chunks
     lines = 3 * width * band
-    more = list(riders) if partial is None else [partial]
     anywhere = pl.BlockSpec(memory_space=pl.ANY)
+    more = [v for v in (rider, partial) if v is not None]
+    specs = ([] if rider is None else in_vmem(1)) + ([] if partial is None else [anywhere])
     shapes = [jax.ShapeDtypeStruct(vort.shape, jnp.float32)]
-    for d in range(groups):
-        extra = 0 if d == 0 or partial is not None else riders[0 if d < groups // 2 else 1].shape[0]
+    for d in steps:
+        extra = 0 if d == 0 or rider is None else rider.shape[0]
         shapes.append(jax.ShapeDtypeStruct((lines + extra, depth), jnp.float32))
     out = pl.pallas_call(
-        functools.partial(advance_kernel, groups, chunk, chunks),
+        functools.partial(advance_kernel, steps, chunk, chunks),
         out_shape=shapes,
-        in_specs=[pl.BlockSpec(memory_space=SMEM)] + [anywhere] * 2 + in_vmem(4)
-        + (in_vmem(2) if partial is None else [anywhere]),
-        out_specs=[anywhere] * (1 + groups),
+        in_specs=[pl.BlockSpec(memory_space=SMEM)] + [anywhere] * 2 + in_vmem(4) + specs,
+        out_specs=[anywhere] * (1 + len(steps)),
         scratch_shapes=[
-            pltpu.VMEM((groups, 2, 3, width + 2, band, depth), jnp.float32),
-            pltpu.VMEM((groups, lines, depth), jnp.float32),
-            pltpu.SemaphoreType.DMA((groups, 2)),
-            pltpu.SemaphoreType.DMA((groups, 2 + 4 * width)),
+            pltpu.VMEM((len(steps), 2, 3, width + 2, band, depth), jnp.float32),
+            pltpu.VMEM((len(steps), lines, depth), jnp.float32),
+            pltpu.SemaphoreType.DMA((len(steps), 2)),
+            pltpu.SemaphoreType.DMA((len(steps), 2 + 4 * width)),
         ],
-        input_output_aliases={} if partial is None else {7: 0},
+        input_output_aliases={} if partial is None else {6 + len(more): 0},
         compiler_params=params(56),
-        name=f"advance_{chunk}",
+        name=f"advance_{chunk}_{len(more)}",
     )(me, vort, vel, *halos, *more)
     return out[0], list(out[1:])
 
@@ -368,7 +369,7 @@
 
 def curl_kernel(groups, gauge, width, me_ref, xlo, xhi, *refs):
     chunks = len(refs[:-4]) // groups
-    blocks = [block for k in range(chunks) for block in by_step(refs[k * groups : (k + 1) * groups])]
+    blocks = [block for k in range(chunks) for block in by_step(refs[k * groups : (k + 1) * groups], True)]
     velocity, front, block, sem = refs[groups * chunks :]
     band, depth = block.shape[3:]
     total = chunks * width
@@ -461,63 +462,42 @@
 
 
 def outline_kernel(*refs):
-    row_low, row_high = refs[:2], refs[2:4]
-    first_rows, last_rows = refs[5:]
+    row_low, row_high, x_low, x_high = refs[:2], refs[2:4], refs[4:6], refs[6:8]
+    first_rows, last_rows, first_x, last_x = refs[8:]
     _, planes, lines, _ = row_low[0].shape
     for f in range(2):
         for c in range(3):
+            first_x[3 * f + c] = x_low[f][c, 0]
+            last_x[3 * f + c] = x_high[f][c, 0]
             for x in range(planes):
                 first_rows[3 * f + c, pl.ds(x, 1), :] = row_low[f][c, x, pl.ds(0, 1), :]
                 last_rows[3 * f + c, pl.ds(x, 1), :] = row_high[f][c, x, pl.ds(lines - 1, 1), :]
 
 
-def outline_x_kernel(*refs):
-    low, high = refs[:2], refs[2:4]
-    first_x, last_x = refs[4:]
-    for f in range(2):
-        for c in range(3):
-            first_x[3 * f + c] = low[f][c, 0]
-            last_x[3 * f + c] = high[f][c, 0]
-
-
-def outline_x(fields):
-    _, planes, band, depth = fields[0].shape
-    plane = (3, 1, band, depth)
-    specs = [pl.BlockSpec(plane, lambda t: (0, 0, 0, 0))] * 2
-    specs += [pl.BlockSpec(plane, lambda t: (0, planes - 1, 0, 0))] * 2
-    shape = jax.ShapeDtypeStruct((6, band, depth), jnp.float32)
-    return pl.pallas_call(
-        outline_x_kernel,
-        grid=(1,),
-        out_shape=[shape] * 2,
-        in_specs=specs,
-        out_specs=[pl.BlockSpec(shape.shape, lambda t: (0, 0, 0))] * 2,
-        compiler_params=params(56),
-        name="outline_x",
-    )(*fields, *fields)
-
-
-def outline(fields, after):
+def outline(fields):
     _, planes, band, depth = fields[0].shape
     lines = 8
     row = (3, planes, lines, depth)
+    plane = (3, 1, band, depth)
     specs = [pl.BlockSpec(row, lambda t: (0, 0, 0, 0))] * 2
     specs += [pl.BlockSpec(row, lambda t: (0, 0, band // lines - 1, 0))] * 2
-    specs += [pl.BlockSpec(memory_space=pl.ANY)]
-    shape = jax.ShapeDtypeStruct((6, planes, depth), jnp.float32)
+    specs += [pl.BlockSpec(plane, lambda t: (0, 0, 0, 0))] * 2
+    specs += [pl.BlockSpec(plane, lambda t: (0, planes - 1, 0, 0))] * 2
+    shapes = [jax.ShapeDtypeStruct((6, planes, depth), jnp.float32)] * 2
+    shapes += [jax.ShapeDtypeStruct((6, band, depth), jnp.float32)] * 2
     return pl.pallas_call(
         outline_kernel,
         grid=(1,),
-        out_shape=[shape] * 2,
+        out_shape=shapes,
         in_specs=specs,
-        out_specs=[pl.BlockSpec(shape.shape, lambda t: (0, 0, 0))] * 2,
+        out_specs=[pl.BlockSpec(v.shape, lambda t: (0, 0, 0)) for v in shapes],
         compiler_params=params(56),
         name="outline",
-    )(*fields, *fields, after)
+    )(*fields, *fields, *fields, *fields)
 
 
 def pick_kernel(groups, starts, me_ref, *refs):
-    blocks, (low, high, sem) = by_step(refs[:groups]), refs[groups:]
+    blocks, (low, high, sem) = by_step(refs[:groups], True), refs[groups:]
     _, band, _ = low.shape
     me = me_ref[0]
     for place, (target, owner) in enumerate(((low, 0), (high, groups - 1))):
@@ -545,7 +525,7 @@
         scratch_shapes=[pltpu.SemaphoreType.DMA((2, 2))],
         compiler_params=params(56),
         name="pick",
-    )(me, *arranged(blocks))
+    )(me, *arranged(blocks, True))
 
 
 def pairs(size, step):
@@ -572,12 +552,11 @@
     me_array = me.reshape(1)
 
     fields = (vorticity, velocity_old)
-    first_x, last_x = outline_x(fields)
+    first_rows, last_rows, first_x, last_x = outline(fields)
     from_x = (
         lax.ppermute(last_x, "gx", pairs(across_x, 1)),
         lax.ppermute(first_x, "gx", pairs(across_x, -1)),
     )
-    first_rows, last_rows = outline(fields, first_x)
     halos = from_x + (
         lax.ppermute(last_rows, "gy", pairs(groups, 1)),
         lax.ppermute(first_rows, "gy", pairs(groups, -1)),
@@ -589,7 +568,14 @@
     vorticity_new = None
     riders = gain_riders(green_hat, depth)
     for k in range(chunks):
-        vorticity_new, outs = advance(k, chunks, me_array, groups, vorticity, velocity_old, halos, riders, vorticity_new)
+        fixed = (me_array, groups, vorticity, velocity_old, halos)
+        if k == 0:
+            far, near = tuple(range(groups - 1, groups // 2 - 1, -1)), tuple(range(groups // 2))
+            vorticity_new, late = advance(far, k, chunks, *fixed, riders[1], None)
+            vorticity_new, outs = advance(near, k, chunks, *fixed, riders[0], vorticity_new)
+            outs = outs + late[::-1]
+        else:
+            vorticity_new, outs = advance(tuple(range(groups)), k, chunks, *fixed, None, vorticity_new)
         received.append(swap(outs))
         if k == 0:
             green = gains(me, green_hat, riders[0], received[0], 3 * width * band)
@@ -608,14 +594,14 @@
     early = returned[0]
     if chunks == 2:
         late = groups // 2 - 1
-        early, returned[1][late] = lax.optimization_barrier((arranged(early), returned[1][late]))
-        early = by_step(early)
+        early, returned[1][late] = lax.optimization_barrier((arranged(early, True), returned[1][late]))
+        early = by_step(early, True)
     low, high = pick(me_array, (base, base + width * band), band, early)
     edges = (
         lax.ppermute(high, "gx", pairs(across_x, 1)),
         lax.ppermute(low, "gx", pairs(across_x, -1)),
     )
-    blocks = [block for group in returned for block in arranged(group)]
+    blocks = [block for group in returned for block in arranged(group, True)]
     velocity = curl(me_array, groups, gauge, vorticity.shape, edges, blocks)
     return vorticity_new, velocity
 

time: 180 us -> 173 us (0.961); the launches traced: 180 us -> 170 us
  waiting for transfers between devices: 62.1 us -> 51.6 us
    ppermute x28, waiting for transfers between devices: 56.7 us -> 47.2 us  [swap(): lax.ppermute(blocks[d], 'gy', [(i, i ^ d) for i in range(groups)])]
  transfers between devices with their start and end apart: 34 -> 34, of which waited for: 11 -> 15; matrix products, arithmetic and copies ran while one was open for 5% -> 6% of each run, Pallas kernels for 22% -> 24%
where the time goes in v3:
time: 173 us; the launch traced here: 170 us
  starting transfers between devices  53.3 us (31%)
  Pallas kernels  52.7 us (30%)
  waiting for transfers between devices  51.6 us (30%)
  matrix products  6.71 us (4%)
  local copies, waits for them, and re-layouts  4.47 us (3%)
    ppermute x28, waiting for transfers between devices, swap(): lax.ppermute(blocks[d], 'gy', [(i, i ^ d) for i in range(groups)])  47.2 us
    ppermute x28, starting transfers between devices, swap(): lax.ppermute(blocks[d], 'gy', [(i, i ^ d) for i in range(groups)])  35.6 us
    pallas_call x2, Pallas kernels, solve(): pl.pallas_call(functools.partial(solve_kernel, groups, stage, width, band...  27.4 us
    pallas_call x3, Pallas kernels, advance(): pl.pallas_call(functools.partial(advance_kernel, steps, chunk, chunks), o...  16.1 us
    ppermute x1, starting transfers between devices, on_device(): lax.ppermute(high, 'gx', pairs(across_x, 1))  4.27 us
    pallas_call x1, Pallas kernels, curl(): pl.pallas_call(functools.partial(curl_kernel, groups, gauge, total // chu...  3.9 us
    ppermute x1, starting transfers between devices, on_device(): lax.ppermute(first_rows, 'gy', pairs(groups, -1))  3.64 us
    dot_general x1, matrix products, gains(): mixed = jnp.einsum('kjc,jmc->km', table, body, precision=highest)  3.54 us
  transfers between devices with their start and end apart: 34, of which 15 were waited for; matrix products, arithmetic and copies ran while one was open for 6% of the time, Pallas kernels for 24%

profile of v3, /device:TPU:10, one launch (start us, length us, event | category | flops | bytes accessed | tf_op | source)
XLA Modules:
  0.0 170.5 jit_solution(13176029754582102054)
XLA Ops:
  0.7 3.1 %outline.1 = (f32[6,32,256]{2,1,0:T(8,128)}, f32[6,32,256]{2,1,0:T(8,128)}, f32[6,32,256]{2,1,0:T(8,128)}, f32[6,32,256]{2,1,0:T(8,128)}) custom-call(f32[3,32,32,256]{3,2,1,0:T(8,128)} %vort.5, f32[3,32,32,256]{3,2,1,0:T(8,128)} %vel.5, f32[3,32,32,256]{3,2,1,0:T(8,128)} %vort.5, f32[3,32,32,256]{3,2,1,0:T(8,128)} %vel.5, f32[3,32,32,256]{3,2,1,0:T(8,128)} %vort.5, ...), custom_call_target="tpu_custom_call" | custom-call | tf_op jit(solution)/shard_map/outline/pallas_call | solution.py:488
  3.8 3.5 %collective-permute-start = (f32[6,32,256]{2,1,0:T(8,128)}, f32[6,32,256]{2,1,0:T(8,128)S(1)}, u32[]{:S(2)}, u32[]{:S(2)}) collective-permute-start(f32[6,32,256]{2,1,0:T(8,128)} %get-tuple-element.81), channel_id=1, source_target_pairs={{0,8},{8,16},{16,24},{1,9},{9,17},{17,25},{2,10},{10,18},{18,26},{... | collective-permute-start | bytes 589832 | tf_op jit(solution)/shard_map/ppermute | solution.py:557
  7.3 2.5 %collective-permute-start.1 = (f32[6,32,256]{2,1,0:T(8,128)}, f32[6,32,256]{2,1,0:T(8,128)S(1)}, u32[]{:S(2)}, u32[]{:S(2)}) collective-permute-start(f32[6,32,256]{2,1,0:T(8,128)} %get-tuple-element.82), channel_id=1, source_target_pairs={{8,0},{16,8},{24,16},{9,1},{17,9},{25,17},{10,2},{18,10},{26,18},{... | collective-permute-start | bytes 589832 | tf_op jit(solution)/shard_map/ppermute | solution.py:558
  9.8 1.9 %collective-permute-start.2 = (f32[6,32,256]{2,1,0:T(8,128)}, f32[6,32,256]{2,1,0:T(8,128)S(1)}, u32[]{:S(2)}, u32[]{:S(2)}) collective-permute-start(f32[6,32,256]{2,1,0:T(8,128)} %get-tuple-element.83), channel_id=1, source_target_pairs={{0,1},{1,2},{2,3},{3,4},{4,5},{5,6},{6,7},{8,9},{9,10},{10,11},{11... | collective-permute-start | bytes 589832 | tf_op jit(solution)/shard_map/ppermute | solution.py:561
  11.7 3.6 %collective-permute-start.3 = (f32[6,32,256]{2,1,0:T(8,128)}, f32[6,32,256]{2,1,0:T(8,128)S(1)}, u32[]{:S(2)}, u32[]{:S(2)}) collective-permute-start(f32[6,32,256]{2,1,0:T(8,128)} %get-tuple-element.84), channel_id=1, source_target_pairs={{1,0},{2,1},{3,2},{4,3},{5,4},{6,5},{7,6},{9,8},{10,9},{11,10},{12... | collective-permute-start | bytes 589832 | tf_op jit(solution)/shard_map/ppermute | solution.py:562
  15.7 0.8 reshape.113.rest_0_
  17.1 0.6 pad.6.rest_0_
  17.8 1.0 collective-permute-done.3.yhi
  18.8 0.7 copy-done.3
  19.5 4.7 %advance_0_1.1 = (f32[3,32,32,256]{3,2,1,0:T(8,128)}, f32[200,256]{1,0:T(8,128)}, f32[200,256]{1,0:T(8,128)}, f32[200,256]{1,0:T(8,128)}, f32[200,256]{1,0:T(8,128)}) custom-call(s32[1]{0:T(128)} %bitcast.me_ref, f32[3,32,32,256]{3,2,1,0:T(8,128)} %vort.5, f32[3,32,32,256]{3,2,1,0:T(8,128)} %vel.5, f32[6,32,256]{2,1,0:T(8,128)} %copy-done, ...), custom_call_target="tpu_custom_call" | custom-call | tf_op jit(solution)/shard_map/advance_0_1/pallas_call | solution.py:230
  24.2 2.7 %collective-permute-start.7 = (f32[200,256]{1,0:T(8,128)}, f32[200,256]{1,0:T(8,128)S(1)}, u32[]{:S(2)}, u32[]{:S(2)}) collective-permute-start(f32[200,256]{1,0:T(8,128)} %get-tuple-element.91), channel_id=1, source_target_pairs={{0,4},{1,5},{2,6},{3,7},{4,0},{5,1},{6,2},{7,3},{8,12},{9,13},{10,... | collective-permute-start | bytes 614408 | tf_op jit(solution)/shard_map/ppermute | solution.py:539
  26.9 1.5 collective-permute-start.8
  28.4 1.6 collective-permute-start.9
  30.0 4.9 %advance_0_2.1 = (f32[3,32,32,256]{3,2,1,0:T(8,128)}, f32[192,256]{1,0:T(8,128)}, f32[320,256]{1,0:T(8,128)}, f32[320,256]{1,0:T(8,128)}, f32[320,256]{1,0:T(8,128)}) custom-call(s32[1]{0:T(128)} %bitcast.me_ref, f32[3,32,32,256]{3,2,1,0:T(8,128)} %vort.5, f32[3,32,32,256]{3,2,1,0:T(8,128)} %vel.5, ...), custom_call_target="tpu_custom_call", output_to_operand_aliasing={{0}: (8, {})} | custom-call | tf_op jit(solution)/shard_map/advance_0_2/pallas_call | solution.py:230
  34.9 0.6 collective-permute-start.4
  35.5 6.5 %advance_1_1.1 = (f32[3,32,32,256]{3,2,1,0:T(8,128)}, f32[192,256]{1,0:T(8,128)}, f32[192,256]{1,0:T(8,128)}, f32[192,256]{1,0:T(8,128)}, f32[192,256]{1,0:T(8,1...) custom-call(s32[1]{0:T(128)} %bitcast.me_ref, ...), custom_call_target="tpu_custom_call", output_to_operand_aliasing={{0}: (7, {})} | custom-call | tf_op jit(solution)/shard_map/advance_1_1/pallas_call | solution.py:230
  42.0 8.3 %collective-permute-done.7.refs_7_ = f32[200,256]{1,0:T(8,128)S(1)} collective-permute-done((f32[200,256]{1,0:T(8,128)}, f32[200,256]{1,0:T(8,128)S(1)}, u32[]{:S(2)}, u32[]{:S(2)}) %collective-permute-start.7) | collective-permute-done | bytes 204832 | tf_op jit(solution)/shard_map/ppermute | solution.py:539
  50.3 4.4 %collective-permute-done.8.refs_5_ = f32[200,256]{1,0:T(8,128)S(1)} collective-permute-done((f32[200,256]{1,0:T(8,128)}, f32[200,256]{1,0:T(8,128)S(1)}, u32[]{:S(2)}, u32[]{:S(2)}) %collective-permute-start.8) | collective-permute-done | bytes 204832 | tf_op jit(solution)/shard_map/ppermute | solution.py:539
  54.7 4.4 %collective-permute-done.9.refs_3_ = f32[200,256]{1,0:T(8,128)S(1)} collective-permute-done((f32[200,256]{1,0:T(8,128)}, f32[200,256]{1,0:T(8,128)S(1)}, u32[]{:S(2)}, u32[]{:S(2)}) %collective-permute-start.9) | collective-permute-done | bytes 204832 | tf_op jit(solution)/shard_map/ppermute | solution.py:539
  59.1 3.7 %collective-permute-done.10.refs_1_ = f32[200,256]{1,0:T(8,128)S(1)} collective-permute-done((f32[200,256]{1,0:T(8,128)}, f32[200,256]{1,0:T(8,128)S(1)}, u32[]{:S(2)}, u32[]{:S(2)}) %collective-permute-start.10) | collective-permute-done | bytes 204832 | tf_op jit(solution)/shard_map/ppermute | solution.py:539
  62.9 4.2 %collective-permute-start.14 = (f32[192,256]{1,0:T(8,128)}, f32[192,256]{1,0:T(8,128)}, u32[]{:S(2)}, u32[]{:S(2)}) collective-permute-start(f32[192,256]{1,0:T(8,128)} %get-tuple-element.108), channel_id=1, source_target_pairs={{0,2},{1,3},{2,0},{3,1},{4,6},{5,7},{6,4},{7,5},{8,10},{9,11},{10,... | collective-permute-start | bytes 589832 | tf_op jit(solution)/shard_map/ppermute | solution.py:539
  67.2 3.8 %collective-permute-done.6.refs_2_ = f32[320,256]{1,0:T(8,128)S(1)} collective-permute-done((f32[320,256]{1,0:T(8,128)S(1)}, f32[320,256]{1,0:T(8,128)S(1)}, u32[]{:S(2)}, u32[]{:S(2)}) %collective-permute-start.6) | collective-permute-done | bytes 327712 | tf_op jit(solution)/shard_map/ppermute | solution.py:539
  70.9 4.8 %collective-permute-start.15 = (f32[192,256]{1,0:T(8,128)}, f32[192,256]{1,0:T(8,128)}, u32[]{:S(2)}, u32[]{:S(2)}) collective-permute-start(f32[192,256]{1,0:T(8,128)} %get-tuple-element.109), channel_id=1, source_target_pairs={{0,5},{1,4},{2,7},{3,6},{4,1},{5,0},{6,3},{7,2},{8,13},{9,12},{10,... | collective-permute-start | bytes 589832 | tf_op jit(solution)/shard_map/ppermute | solution.py:539
  75.8 0.6 gather_fusion
  76.7 3.5 %convolution_bitcast_fusion = f32[2,256,512]{2,1,0:T(8,128)S(1)} fusion(f32[4,512,64]{2,1,0:T(8,128)S(1)} %gather.11, f32[4,8,2,8,256]{4,3,2,1,0:T(8,128)S(1)} %bitcast.42, pred[4]{0:T(512)(128)(4,1)S(1)} %compare_and_fusion), kind=kOutput, calls=%fused_computation.1 | convolution fusion | flops 805437440 | bytes 2097156 | tf_op jit(solution)/shard_map/kjc,jmc->km/dot_general | solution.py:109
  80.2 1.3 fusion.5
  81.6 1.6 collective-permute-done.12.refs_2_
  83.2 1.9 %convolution_add_fusion.green = f32[256,512]{1,0:T(8,128)} fusion(f32[256,512]{1,0:T(8,128)S(1)} %fusion.5, f32[512,512]{1,0:T(8,128)S(1)} %copy-done.4, f32[2,256,512]{2,1,0:T(8,128)S(1)} %convolution_bitcast_fusion), kind=kOutput, calls=%fused_computation.2 | convolution fusion | flops 805437440 | bytes 2621440 | tf_op jit(solution)/shard_map/dot_general | solution.py:113
  85.1 13.5 %solve_first.1 = (f32[136,256]{1,0:T(8,128)}, f32[136,256]{1,0:T(8,128)}, f32[136,256]{1,0:T(8,128)}, f32[136,256]{1,0:T(8,128)}, f32[136,256]{1,0:T(8,128)}, /*...) custom-call(s32[1]{0:T(128)} %bitcast.me_ref, ...), custom_call_target="tpu_custom_call" | custom-call | tf_op jit(solution)/shard_map/solve_first/pallas_call | solution.py:355
  98.6 3.9 %collective-permute-start.18 = (f32[136,256]{1,0:T(8,128)}, f32[136,256]{1,0:T(8,128)S(1)}, u32[]{:S(2)}, u32[]{:S(2)}) collective-permute-start(f32[136,256]{1,0:T(8,128)} %get-tuple-element.113), channel_id=1, source_target_pairs={{0,7},{1,6},{2,5},{3,4},{4,3},{5,2},{6,1},{7,0},{8,15},{9,14},{10,... | collective-permute-start | bytes 417800 | tf_op jit(solution)/shard_map/ppermute | solution.py:539
  102.5 3.1 %collective-permute-start.19 = (f32[136,256]{1,0:T(8,128)}, f32[136,256]{1,0:T(8,128)S(1)}, u32[]{:S(2)}, u32[]{:S(2)}) collective-permute-start(f32[136,256]{1,0:T(8,128)} %get-tuple-element.114), channel_id=1, source_target_pairs={{0,6},{1,7},{2,4},{3,5},{4,2},{5,3},{6,0},{7,1},{8,14},{9,15},{10,... | collective-permute-start | bytes 417800 | tf_op jit(solution)/shard_map/ppermute | solution.py:539
  105.7 2.0 %collective-permute-start.21 = (f32[136,256]{1,0:T(8,128)}, f32[136,256]{1,0:T(8,128)S(1)}, u32[]{:S(2)}, u32[]{:S(2)}) collective-permute-start(f32[136,256]{1,0:T(8,128)} %get-tuple-element.116), channel_id=1, source_target_pairs={{0,4},{1,5},{2,6},{3,7},{4,0},{5,1},{6,2},{7,3},{8,12},{9,13},{10,... | collective-permute-start | bytes 417800 | tf_op jit(solution)/shard_map/ppermute | solution.py:539
  107.7 13.9 %solve_second.1 = (f32[200,256]{1,0:T(8,128)}, f32[200,256]{1,0:T(8,128)}, f32[200,256]{1,0:T(8,128)}, f32[200,256]{1,0:T(8,128)}, f32[200,256]{1,0:T(8,128)}, /...) custom-call(s32[1]{0:T(128)} %bitcast.me_ref, bf16[512,768]{1,0:T(8,128)(2,1)} %constant.101.clone.fz, ...), custom_call_target="tpu_custom_call" | custom-call | tf_op jit(solution)/shard_map/solve_second/pallas_call | solution.py:355
  121.6 2.3 %collective-permute-start.23 = (f32[136,256]{1,0:T(8,128)S(1)}, f32[136,256]{1,0:T(8,128)S(1)}, u32[]{:S(2)}, u32[]{:S(2)}) collective-permute-start(f32[136,256]{1,0:T(8,128)S(1)} %copy-done.39), channel_id=1, source_target_pairs={{0,2},{1,3},{2,0},{3,1},{4,6},{5,7},{6,4},{7,5},{8,10},{9,11},{10,... | collective-permute-start | bytes 417800 | tf_op jit(solution)/shard_map/ppermute | solution.py:539
  123.9 1.3 collective-permute-start.25
  125.2 1.1 collective-permute-start.28
  126.3 0.9 collective-permute-done.21.refs_4_
  127.6 2.2 %collective-permute-done.23.refs_6_ = f32[136,256]{1,0:T(8,128)S(1)} collective-permute-done((f32[136,256]{1,0:T(8,128)S(1)}, f32[136,256]{1,0:T(8,128)S(1)}, u32[]{:S(2)}, u32[]{:S(2)}) %collective-permute-start.23) | collective-permute-done | bytes 139296 | tf_op jit(solution)/shard_map/ppermute | solution.py:539
  129.9 3.3 %collective-permute-start.30 = (f32[200,256]{1,0:T(8,128)}, f32[200,256]{1,0:T(8,128)S(1)}, u32[]{:S(2)}, u32[]{:S(2)}) collective-permute-start(f32[200,256]{1,0:T(8,128)} %get-tuple-element.143), channel_id=1, source_target_pairs={{0,5},{1,4},{2,7},{3,6},{4,1},{5,0},{6,3},{7,2},{8,13},{9,12},{10,... | collective-permute-start | bytes 614408 | tf_op jit(solution)/shard_map/ppermute | solution.py:539
  133.6 9.5 %collective-permute-done.25.refs_13_ = f32[200,256]{1,0:T(8,128)S(1)} collective-permute-done((f32[200,256]{1,0:T(8,128)}, f32[200,256]{1,0:T(8,128)S(1)}, u32[]{:S(2)}, u32[]{:S(2)}) %collective-permute-start.25) | collective-permute-done | bytes 204832 | tf_op jit(solution)/shard_map/ppermute | solution.py:539
  143.1 2.3 %collective-permute-start.32 = (f32[200,256]{1,0:T(8,128)}, f32[200,256]{1,0:T(8,128)S(1)}, u32[]{:S(2)}, u32[]{:S(2)}) collective-permute-start(f32[200,256]{1,0:T(8,128)} %get-tuple-element.146), channel_id=1, source_target_pairs={{0,2},{1,3},{2,0},{3,1},{4,6},{5,7},{6,4},{7,5},{8,10},{9,11},{10,... | collective-permute-start | bytes 614408 | tf_op jit(solution)/shard_map/ppermute | solution.py:539
  145.5 2.2 %pick.1 = (f32[2,32,256]{2,1,0:T(8,128)}, f32[2,32,256]{2,1,0:T(8,128)}) custom-call(s32[1]{0:T(128)} %bitcast.me_ref, f32[136,256]{1,0:T(8,128)} %get-tuple-element.130.refs_0_, f32[136,256]{1,0:T(8,128)} %copy-done.9, f32[136,256]{1,0:T(8,128)} %copy-done.10, f32[136,256]{1,0:T(8,128)} %copy-done.11, f32[136,256]{1,0:T(8,128)} %copy-done.12, ...), custom_call_target="tpu_custom_call" | custom-call | tf_op jit(solution)/shard_map/pick/pallas_call | solution.py:520
  147.7 6.4 %collective-permute-done.29.refs_10_ = f32[200,256]{1,0:T(8,128)S(1)} collective-permute-done((f32[200,256]{1,0:T(8,128)}, f32[200,256]{1,0:T(8,128)S(1)}, u32[]{:S(2)}, u32[]{:S(2)}) %collective-permute-start.29) | collective-permute-done | bytes 204832 | tf_op jit(solution)/shard_map/ppermute | solution.py:539
  154.1 4.3 %collective-permute-start.26 = (f32[2,32,256]{2,1,0:T(8,128)}, f32[2,32,256]{2,1,0:T(8,128)S(1)}, u32[]{:S(2)}, u32[]{:S(2)}) collective-permute-start(f32[2,32,256]{2,1,0:T(8,128)} %get-tuple-element.138), channel_id=1, source_target_pairs={{0,8},{8,16},{16,24},{1,9},{9,17},{17,25},{2,10},{10,18},{18,26},{... | collective-permute-start | bytes 196616 | tf_op jit(solution)/shard_map/ppermute | solution.py:601
  158.5 1.9 %collective-permute-start.27 = (f32[2,32,256]{2,1,0:T(8,128)}, f32[2,32,256]{2,1,0:T(8,128)S(1)}, u32[]{:S(2)}, u32[]{:S(2)}) collective-permute-start(f32[2,32,256]{2,1,0:T(8,128)} %get-tuple-element.139), channel_id=1, source_target_pairs={{8,0},{16,8},{24,16},{9,1},{17,9},{25,17},{10,2},{18,10},{26,18},{... | collective-permute-start | bytes 196616 | tf_op jit(solution)/shard_map/ppermute | solution.py:602
  160.4 2.0 %collective-permute-done.31.refs_12_ = f32[200,256]{1,0:T(8,128)S(1)} collective-permute-done((f32[200,256]{1,0:T(8,128)}, f32[200,256]{1,0:T(8,128)S(1)}, u32[]{:S(2)}, u32[]{:S(2)}) %collective-permute-start.31) | collective-permute-done | bytes 204832 | tf_op jit(solution)/shard_map/ppermute | solution.py:539
  162.4 3.3 %collective-permute-done.27.xhi = f32[2,32,256]{2,1,0:T(8,128)S(1)} collective-permute-done((f32[2,32,256]{2,1,0:T(8,128)}, f32[2,32,256]{2,1,0:T(8,128)S(1)}, u32[]{:S(2)}, u32[]{:S(2)}) %collective-permute-start.27) | collective-permute-done | bytes 65568 | tf_op jit(solution)/shard_map/ppermute | solution.py:602
  166.4 3.9 %curl.1 = f32[3,32,32,256]{3,2,1,0:T(8,128)} custom-call(s32[1]{0:T(128)} %bitcast.me_ref, f32[2,32,256]{2,1,0:T(8,128)} %copy-done.31, f32[2,32,256]{2,1,0:T(8,128)} %copy-done.32, f32[136,256]{1,0:T(8,128)} %get-tuple-element.130.refs_0_, f32[136,256]{1,0:T(8,128)} %copy-done.9, f32[136,256]{1,0:T(8,128)} %copy-done.10, f32[136,256]{1,0:T(8,128)} %copy-done.11, ...), custom_call_target="tpu_custom_call" | custom-call | tf_op jit(solution)/shard_map/curl/pallas_call | solution.py:449
  (135 shorter events, 3.3 us)
Async XLA Ops:
  0.6 15.8 %copy-start.16 = (f32[2,2,256,256]{2,1,3,0:T(2,128)S(1)}, f32[2,2,256,256]{2,1,3,0:T(2,128)}, u32[]{:S(2)}) copy-start(f32[2,2,256,256]{2,1,3,0:T(2,128)} %constant.105.clone) | copy-start | bytes 3145732
  3.8 13.9 %collective-permute-start = (f32[6,32,256]{2,1,0:T(8,128)}, f32[6,32,256]{2,1,0:T(8,128)S(1)}, u32[]{:S(2)}, u32[]{:S(2)}) collective-permute-start(f32[6,32,256]{2,1,0:T(8,128)} %get-tuple-element.81), channel_id=1, source_target_pairs={{0,8},{8,16},{16,24},{1,9},{9,17},{17,25},{2,10},{10,18},{18,26},{... | collective-permute-start | bytes 589832 | tf_op jit(solution)/shard_map/ppermute | solution.py:557
  7.3 10.5 %collective-permute-start.1 = (f32[6,32,256]{2,1,0:T(8,128)}, f32[6,32,256]{2,1,0:T(8,128)S(1)}, u32[]{:S(2)}, u32[]{:S(2)}) collective-permute-start(f32[6,32,256]{2,1,0:T(8,128)} %get-tuple-element.82), channel_id=1, source_target_pairs={{8,0},{16,8},{24,16},{9,1},{17,9},{25,17},{10,2},{18,10},{26,18},{... | collective-permute-start | bytes 589832 | tf_op jit(solution)/shard_map/ppermute | solution.py:558
  9.8 8.1 %collective-permute-start.2 = (f32[6,32,256]{2,1,0:T(8,128)}, f32[6,32,256]{2,1,0:T(8,128)S(1)}, u32[]{:S(2)}, u32[]{:S(2)}) collective-permute-start(f32[6,32,256]{2,1,0:T(8,128)} %get-tuple-element.83), channel_id=1, source_target_pairs={{0,1},{1,2},{2,3},{3,4},{4,5},{5,6},{6,7},{8,9},{9,10},{10,11},{11... | collective-permute-start | bytes 589832 | tf_op jit(solution)/shard_map/ppermute | solution.py:561
  11.7 7.1 %collective-permute-start.3 = (f32[6,32,256]{2,1,0:T(8,128)}, f32[6,32,256]{2,1,0:T(8,128)S(1)}, u32[]{:S(2)}, u32[]{:S(2)}) collective-permute-start(f32[6,32,256]{2,1,0:T(8,128)} %get-tuple-element.84), channel_id=1, source_target_pairs={{1,0},{2,1},{3,2},{4,3},{5,4},{6,5},{7,6},{9,8},{10,9},{11,10},{12... | collective-permute-start | bytes 589832 | tf_op jit(solution)/shard_map/ppermute | solution.py:562
  24.2 26.0 %collective-permute-start.7 = (f32[200,256]{1,0:T(8,128)}, f32[200,256]{1,0:T(8,128)S(1)}, u32[]{:S(2)}, u32[]{:S(2)}) collective-permute-start(f32[200,256]{1,0:T(8,128)} %get-tuple-element.91), channel_id=1, source_target_pairs={{0,4},{1,5},{2,6},{3,7},{4,0},{5,1},{6,2},{7,3},{8,12},{9,13},{10,... | collective-permute-start | bytes 614408 | tf_op jit(solution)/shard_map/ppermute | solution.py:539
  26.9 27.8 %collective-permute-start.8 = (f32[200,256]{1,0:T(8,128)}, f32[200,256]{1,0:T(8,128)S(1)}, u32[]{:S(2)}, u32[]{:S(2)}) collective-permute-start(f32[200,256]{1,0:T(8,128)} %get-tuple-element.92), channel_id=1, source_target_pairs={{0,5},{1,4},{2,7},{3,6},{4,1},{5,0},{6,3},{7,2},{8,13},{9,12},{10,... | collective-permute-start | bytes 614408 | tf_op jit(solution)/shard_map/ppermute | solution.py:539
  28.4 30.7 %collective-permute-start.9 = (f32[200,256]{1,0:T(8,128)}, f32[200,256]{1,0:T(8,128)S(1)}, u32[]{:S(2)}, u32[]{:S(2)}) collective-permute-start(f32[200,256]{1,0:T(8,128)} %get-tuple-element.93), channel_id=1, source_target_pairs={{0,6},{1,7},{2,4},{3,5},{4,2},{5,3},{6,0},{7,1},{8,14},{9,15},{10,... | collective-permute-start | bytes 614408 | tf_op jit(solution)/shard_map/ppermute | solution.py:539
  30.0 32.8 %collective-permute-start.10 = (f32[200,256]{1,0:T(8,128)}, f32[200,256]{1,0:T(8,128)S(1)}, u32[]{:S(2)}, u32[]{:S(2)}) collective-permute-start(f32[200,256]{1,0:T(8,128)} %get-tuple-element.94), channel_id=1, source_target_pairs={{0,7},{1,6},{2,5},{3,4},{4,3},{5,2},{6,1},{7,0},{8,15},{9,14},{10,... | collective-permute-start | bytes 614408 | tf_op jit(solution)/shard_map/ppermute | solution.py:539
  34.9 27.9 %collective-permute-start.4 = (f32[320,256]{1,0:T(8,128)}, f32[320,256]{1,0:T(8,128)S(1)}, u32[]{:S(2)}, u32[]{:S(2)}) collective-permute-start(f32[320,256]{1,0:T(8,128)} %get-tuple-element.88), channel_id=1, source_target_pairs={{0,1},{1,0},{2,3},{3,2},{4,5},{5,4},{6,7},{7,6},{8,9},{9,8},{10,11... | collective-permute-start | bytes 983048 | tf_op jit(solution)/shard_map/ppermute | solution.py:539
  35.5 14.8 %copy-start.35 = (f32[320,256]{1,0:T(8,128)S(1)}, f32[320,256]{1,0:T(8,128)}, u32[]{:S(2)}) copy-start(f32[320,256]{1,0:T(8,128)} %get-tuple-element.89) | copy-start | bytes 983044
  35.5 19.2 %copy-start.34 = (f32[320,256]{1,0:T(8,128)S(1)}, f32[320,256]{1,0:T(8,128)}, u32[]{:S(2)}) copy-start(f32[320,256]{1,0:T(8,128)} %get-tuple-element.90) | copy-start | bytes 983044
  50.3 12.6 %collective-permute-start.5 = (f32[320,256]{1,0:T(8,128)S(1)}, f32[320,256]{1,0:T(8,128)S(1)}, u32[]{:S(2)}, u32[]{:S(2)}) collective-permute-start(f32[320,256]{1,0:T(8,128)S(1)} %copy-done.35), channel_id=1, source_target_pairs={{0,2},{1,3},{2,0},{3,1},{4,6},{5,7},{6,4},{7,5},{8,10},{9,11},{10,... | collective-permute-start | bytes 983048 | tf_op jit(solution)/shard_map/ppermute | solution.py:539
  54.7 16.2 %collective-permute-start.6 = (f32[320,256]{1,0:T(8,128)S(1)}, f32[320,256]{1,0:T(8,128)S(1)}, u32[]{:S(2)}, u32[]{:S(2)}) collective-permute-start(f32[320,256]{1,0:T(8,128)S(1)} %copy-done.34), channel_id=1, source_target_pairs={{0,3},{1,2},{2,1},{3,0},{4,7},{5,6},{6,5},{7,4},{8,11},{9,10},{10,... | collective-permute-start | bytes 983048 | tf_op jit(solution)/shard_map/ppermute | solution.py:539
  59.1 16.7 %copy-start.19 = (f32[200,256]{1,0:T(8,128)}, f32[200,256]{1,0:T(8,128)S(1)}, u32[]{:S(2)}) copy-start(f32[200,256]{1,0:T(8,128)S(1)} %collective-permute-done.9.refs_3_) | copy-start | bytes 614404
  59.1 22.4 %collective-permute-start.11 = (f32[192,256]{1,0:T(8,128)}, f32[192,256]{1,0:T(8,128)}, u32[]{:S(2)}, u32[]{:S(2)}) collective-permute-start(f32[192,256]{1,0:T(8,128)} %get-tuple-element.105), channel_id=1, source_target_pairs={{0,7},{1,6},{2,5},{3,4},{4,3},{5,2},{6,1},{7,0},{8,15},{9,14},{10,... | collective-permute-start | bytes 589832 | tf_op jit(solution)/shard_map/ppermute | solution.py:539
  62.7 20.4 %collective-permute-start.12 = (f32[192,256]{1,0:T(8,128)}, f32[192,256]{1,0:T(8,128)}, u32[]{:S(2)}, u32[]{:S(2)}) collective-permute-start(f32[192,256]{1,0:T(8,128)} %get-tuple-element.106), channel_id=1, source_target_pairs={{0,3},{1,2},{2,1},{3,0},{4,7},{5,6},{6,5},{7,4},{8,11},{9,10},{10,... | collective-permute-start | bytes 589832 | tf_op jit(solution)/shard_map/ppermute | solution.py:539
  62.8 17.4 %copy-start.6 = (f32[320,256]{1,0:T(8,128)}, f32[320,256]{1,0:T(8,128)S(1)}, u32[]{:S(2)}) copy-start(f32[320,256]{1,0:T(8,128)S(1)} %collective-permute-done.4.refs_6_) | copy-start | bytes 983044
  62.8 35.8 %collective-permute-start.13 = (f32[192,256]{1,0:T(8,128)}, f32[192,256]{1,0:T(8,128)}, u32[]{:S(2)}, u32[]{:S(2)}) collective-permute-start(f32[192,256]{1,0:T(8,128)} %get-tuple-element.107), channel_id=1, source_target_pairs={{0,6},{1,7},{2,4},{3,5},{4,2},{5,3},{6,0},{7,1},{8,14},{9,15},{10,... | collective-permute-start | bytes 589832 | tf_op jit(solution)/shard_map/ppermute | solution.py:539
  62.9 35.6 %collective-permute-start.14 = (f32[192,256]{1,0:T(8,128)}, f32[192,256]{1,0:T(8,128)}, u32[]{:S(2)}, u32[]{:S(2)}) collective-permute-start(f32[192,256]{1,0:T(8,128)} %get-tuple-element.108), channel_id=1, source_target_pairs={{0,2},{1,3},{2,0},{3,1},{4,6},{5,7},{6,4},{7,5},{8,10},{9,11},{10,... | collective-permute-start | bytes 589832 | tf_op jit(solution)/shard_map/ppermute | solution.py:539
  70.9 27.6 %collective-permute-start.15 = (f32[192,256]{1,0:T(8,128)}, f32[192,256]{1,0:T(8,128)}, u32[]{:S(2)}, u32[]{:S(2)}) collective-permute-start(f32[192,256]{1,0:T(8,128)} %get-tuple-element.109), channel_id=1, source_target_pairs={{0,5},{1,4},{2,7},{3,6},{4,1},{5,0},{6,3},{7,2},{8,13},{9,12},{10,... | collective-permute-start | bytes 589832 | tf_op jit(solution)/shard_map/ppermute | solution.py:539
  81.5 17.1 %collective-permute-start.16 = (f32[192,256]{1,0:T(8,128)S(1)}, f32[192,256]{1,0:T(8,128)S(1)}, u32[]{:S(2)}, u32[]{:S(2)}) collective-permute-start(f32[192,256]{1,0:T(8,128)S(1)} %copy-done.37), channel_id=1, source_target_pairs={{0,1},{1,0},{2,3},{3,2},{4,5},{5,4},{6,7},{7,6},{8,9},{9,8},{10,11... | collective-permute-start | bytes 589832 | tf_op jit(solution)/shard_map/ppermute | solution.py:539
  83.2 15.4 %collective-permute-start.17 = (f32[192,256]{1,0:T(8,128)S(1)}, f32[192,256]{1,0:T(8,128)S(1)}, u32[]{:S(2)}, u32[]{:S(2)}) collective-permute-start(f32[192,256]{1,0:T(8,128)S(1)} %copy-done.36), channel_id=1, source_target_pairs={{0,4},{1,5},{2,6},{3,7},{4,0},{5,1},{6,2},{7,3},{8,12},{9,13},{10,... | collective-permute-start | bytes 589832 | tf_op jit(solution)/shard_map/ppermute | solution.py:539
  98.6 23.0 %collective-permute-start.18 = (f32[136,256]{1,0:T(8,128)}, f32[136,256]{1,0:T(8,128)S(1)}, u32[]{:S(2)}, u32[]{:S(2)}) collective-permute-start(f32[136,256]{1,0:T(8,128)} %get-tuple-element.113), channel_id=1, source_target_pairs={{0,7},{1,6},{2,5},{3,4},{4,3},{5,2},{6,1},{7,0},{8,15},{9,14},{10,... | collective-permute-start | bytes 417800 | tf_op jit(solution)/shard_map/ppermute | solution.py:539
  102.5 21.4 %collective-permute-start.19 = (f32[136,256]{1,0:T(8,128)}, f32[136,256]{1,0:T(8,128)S(1)}, u32[]{:S(2)}, u32[]{:S(2)}) collective-permute-start(f32[136,256]{1,0:T(8,128)} %get-tuple-element.114), channel_id=1, source_target_pairs={{0,6},{1,7},{2,4},{3,5},{4,2},{5,3},{6,0},{7,1},{8,14},{9,15},{10,... | collective-permute-start | bytes 417800 | tf_op jit(solution)/shard_map/ppermute | solution.py:539
  105.6 19.7 %collective-permute-start.20 = (f32[136,256]{1,0:T(8,128)}, f32[136,256]{1,0:T(8,128)S(1)}, u32[]{:S(2)}, u32[]{:S(2)}) collective-permute-start(f32[136,256]{1,0:T(8,128)} %get-tuple-element.115), channel_id=1, source_target_pairs={{0,5},{1,4},{2,7},{3,6},{4,1},{5,0},{6,3},{7,2},{8,13},{9,12},{10,... | collective-permute-start | bytes 417800 | tf_op jit(solution)/shard_map/ppermute | solution.py:539
  105.7 21.5 %collective-permute-start.21 = (f32[136,256]{1,0:T(8,128)}, f32[136,256]{1,0:T(8,128)S(1)}, u32[]{:S(2)}, u32[]{:S(2)}) collective-permute-start(f32[136,256]{1,0:T(8,128)} %get-tuple-element.116), channel_id=1, source_target_pairs={{0,4},{1,5},{2,6},{3,7},{4,0},{5,1},{6,2},{7,3},{8,12},{9,13},{10,... | collective-permute-start | bytes 417800 | tf_op jit(solution)/shard_map/ppermute | solution.py:539
  107.7 19.7 %collective-permute-start.22 = (f32[136,256]{1,0:T(8,128)}, f32[136,256]{1,0:T(8,128)S(1)}, u32[]{:S(2)}, u32[]{:S(2)}) collective-permute-start(f32[136,256]{1,0:T(8,128)} %get-tuple-element.117), channel_id=1, source_target_pairs={{0,3},{1,2},{2,1},{3,0},{4,7},{5,6},{6,5},{7,4},{8,11},{9,10},{10,... | collective-permute-start | bytes 417800 | tf_op jit(solution)/shard_map/ppermute | solution.py:539
  107.7 19.5 %copy-start.38 = (f32[136,256]{1,0:T(8,128)S(1)}, f32[136,256]{1,0:T(8,128)}, u32[]{:S(2)}) copy-start(f32[136,256]{1,0:T(8,128)} %get-tuple-element.119) | copy-start | bytes 417796
  121.6 23.8 %copy-start.9 = (f32[136,256]{1,0:T(8,128)}, f32[136,256]{1,0:T(8,128)S(1)}, u32[]{:S(2)}) copy-start(f32[136,256]{1,0:T(8,128)S(1)} %collective-permute-done.18.refs_1_) | copy-start | bytes 417796
  121.6 8.2 %collective-permute-start.23 = (f32[136,256]{1,0:T(8,128)S(1)}, f32[136,256]{1,0:T(8,128)S(1)}, u32[]{:S(2)}, u32[]{:S(2)}) collective-permute-start(f32[136,256]{1,0:T(8,128)S(1)} %copy-done.39), channel_id=1, source_target_pairs={{0,2},{1,3},{2,0},{3,1},{4,6},{5,7},{6,4},{7,5},{8,10},{9,11},{10,... | collective-permute-start | bytes 417800 | tf_op jit(solution)/shard_map/ppermute | solution.py:539
  123.9 21.5 %copy-start.10 = (f32[136,256]{1,0:T(8,128)}, f32[136,256]{1,0:T(8,128)S(1)}, u32[]{:S(2)}) copy-start(f32[136,256]{1,0:T(8,128)S(1)} %collective-permute-done.19.refs_2_) | copy-start | bytes 417796
  123.9 19.2 %collective-permute-start.25 = (f32[200,256]{1,0:T(8,128)}, f32[200,256]{1,0:T(8,128)S(1)}, u32[]{:S(2)}, u32[]{:S(2)}) collective-permute-start(f32[200,256]{1,0:T(8,128)} %get-tuple-element.129), channel_id=1, source_target_pairs={{0,3},{1,2},{2,1},{3,0},{4,7},{5,6},{6,5},{7,4},{8,11},{9,10},{10,... | collective-permute-start | bytes 614408 | tf_op jit(solution)/shard_map/ppermute | solution.py:539
  125.2 20.2 %copy-start.11 = (f32[136,256]{1,0:T(8,128)}, f32[136,256]{1,0:T(8,128)S(1)}, u32[]{:S(2)}) copy-start(f32[136,256]{1,0:T(8,128)S(1)} %collective-permute-done.20.refs_3_) | copy-start | bytes 417796
  125.2 20.1 %collective-permute-start.28 = (f32[200,256]{1,0:T(8,128)}, f32[200,256]{1,0:T(8,128)S(1)}, u32[]{:S(2)}, u32[]{:S(2)}) collective-permute-start(f32[200,256]{1,0:T(8,128)} %get-tuple-element.141), channel_id=1, source_target_pairs={{0,7},{1,6},{2,5},{3,4},{4,3},{5,2},{6,1},{7,0},{8,15},{9,14},{10,... | collective-permute-start | bytes 614408 | tf_op jit(solution)/shard_map/ppermute | solution.py:539
  127.2 18.2 %copy-start.12 = (f32[136,256]{1,0:T(8,128)}, f32[136,256]{1,0:T(8,128)S(1)}, u32[]{:S(2)}) copy-start(f32[136,256]{1,0:T(8,128)S(1)} %collective-permute-done.21.refs_4_) | copy-start | bytes 417796
  127.2 6.0 %collective-permute-start.24 = (f32[136,256]{1,0:T(8,128)S(1)}, f32[136,256]{1,0:T(8,128)S(1)}, u32[]{:S(2)}, u32[]{:S(2)}) collective-permute-start(f32[136,256]{1,0:T(8,128)S(1)} %copy-done.38), channel_id=1, source_target_pairs={{0,1},{1,0},{2,3},{3,2},{4,5},{5,4},{6,7},{7,6},{8,9},{9,8},{10,11... | collective-permute-start | bytes 417800 | tf_op jit(solution)/shard_map/ppermute | solution.py:539
  127.4 18.0 %copy-start.13 = (f32[136,256]{1,0:T(8,128)}, f32[136,256]{1,0:T(8,128)S(1)}, u32[]{:S(2)}) copy-start(f32[136,256]{1,0:T(8,128)S(1)} %collective-permute-done.22.refs_5_) | copy-start | bytes 417796
  127.4 26.7 %collective-permute-start.29 = (f32[200,256]{1,0:T(8,128)}, f32[200,256]{1,0:T(8,128)S(1)}, u32[]{:S(2)}, u32[]{:S(2)}) collective-permute-start(f32[200,256]{1,0:T(8,128)} %get-tuple-element.142), channel_id=1, source_target_pairs={{0,6},{1,7},{2,4},{3,5},{4,2},{5,3},{6,0},{7,1},{8,14},{9,15},{10,... | collective-permute-start | bytes 614408 | tf_op jit(solution)/shard_map/ppermute | solution.py:539
  129.9 15.6 %copy-start.14 = (f32[136,256]{1,0:T(8,128)}, f32[136,256]{1,0:T(8,128)S(1)}, u32[]{:S(2)}) copy-start(f32[136,256]{1,0:T(8,128)S(1)} %collective-permute-done.23.refs_6_) | copy-start | bytes 417796
  129.9 28.6 %collective-permute-start.30 = (f32[200,256]{1,0:T(8,128)}, f32[200,256]{1,0:T(8,128)S(1)}, u32[]{:S(2)}, u32[]{:S(2)}) collective-permute-start(f32[200,256]{1,0:T(8,128)} %get-tuple-element.143), channel_id=1, source_target_pairs={{0,5},{1,4},{2,7},{3,6},{4,1},{5,0},{6,3},{7,2},{8,13},{9,12},{10,... | collective-permute-start | bytes 614408 | tf_op jit(solution)/shard_map/ppermute | solution.py:539
  133.2 29.2 %collective-permute-start.31 = (f32[200,256]{1,0:T(8,128)}, f32[200,256]{1,0:T(8,128)S(1)}, u32[]{:S(2)}, u32[]{:S(2)}) collective-permute-start(f32[200,256]{1,0:T(8,128)} %get-tuple-element.144), channel_id=1, source_target_pairs={{0,4},{1,5},{2,6},{3,7},{4,0},{5,1},{6,2},{7,3},{8,12},{9,13},{10,... | collective-permute-start | bytes 614408 | tf_op jit(solution)/shard_map/ppermute | solution.py:539
  143.1 22.7 %copy-start.21 = (f32[200,256]{1,0:T(8,128)}, f32[200,256]{1,0:T(8,128)S(1)}, u32[]{:S(2)}) copy-start(f32[200,256]{1,0:T(8,128)S(1)} %collective-permute-done.25.refs_13_) | copy-start | bytes 614404
  143.1 19.3 %collective-permute-start.32 = (f32[200,256]{1,0:T(8,128)}, f32[200,256]{1,0:T(8,128)S(1)}, u32[]{:S(2)}, u32[]{:S(2)}) collective-permute-start(f32[200,256]{1,0:T(8,128)} %get-tuple-element.146), channel_id=1, source_target_pairs={{0,2},{1,3},{2,0},{3,1},{4,6},{5,7},{6,4},{7,5},{8,10},{9,11},{10,... | collective-permute-start | bytes 614408 | tf_op jit(solution)/shard_map/ppermute | solution.py:539
  145.4 20.4 %copy-start.22 = (f32[200,256]{1,0:T(8,128)}, f32[200,256]{1,0:T(8,128)S(1)}, u32[]{:S(2)}) copy-start(f32[200,256]{1,0:T(8,128)S(1)} %collective-permute-done.28.refs_9_) | copy-start | bytes 614404
  145.4 17.0 %collective-permute-start.33 = (f32[200,256]{1,0:T(8,128)}, f32[200,256]{1,0:T(8,128)S(1)}, u32[]{:S(2)}, u32[]{:S(2)}) collective-permute-start(f32[200,256]{1,0:T(8,128)} %get-tuple-element.147), channel_id=1, source_target_pairs={{0,1},{1,0},{2,3},{3,2},{4,5},{5,4},{6,7},{7,6},{8,9},{9,8},{10,11... | collective-permute-start | bytes 614408 | tf_op jit(solution)/shard_map/ppermute | solution.py:539
  154.1 8.3 %collective-permute-start.26 = (f32[2,32,256]{2,1,0:T(8,128)}, f32[2,32,256]{2,1,0:T(8,128)S(1)}, u32[]{:S(2)}, u32[]{:S(2)}) collective-permute-start(f32[2,32,256]{2,1,0:T(8,128)} %get-tuple-element.138), channel_id=1, source_target_pairs={{0,8},{8,16},{16,24},{1,9},{9,17},{17,25},{2,10},{10,18},{18,26},{... | collective-permute-start | bytes 196616 | tf_op jit(solution)/shard_map/ppermute | solution.py:601
  158.5 7.3 %collective-permute-start.27 = (f32[2,32,256]{2,1,0:T(8,128)}, f32[2,32,256]{2,1,0:T(8,128)S(1)}, u32[]{:S(2)}, u32[]{:S(2)}) collective-permute-start(f32[2,32,256]{2,1,0:T(8,128)} %get-tuple-element.139), channel_id=1, source_target_pairs={{8,0},{16,8},{24,16},{9,1},{17,9},{25,17},{10,2},{18,10},{26,18},{... | collective-permute-start | bytes 196616 | tf_op jit(solution)/shard_map/ppermute | solution.py:602
  (26 other events, 175.2 us)

commit v4 on v3

--- a/solution.py
+++ b/solution.py
@@ -593,7 +593,7 @@
     base = width * band * (0 if gauge else 1)
     early = returned[0]
     if chunks == 2:
-        late = groups // 2 - 1
+        late = 1
         early, returned[1][late] = lax.optimization_barrier((arranged(early, True), returned[1][late]))
         early = by_step(early, True)
     low, high = pick(me_array, (base, base + width * band), band, early)

time: 173 us -> 172 us (level)
  waiting for transfers between devices: 51.6 us -> 53.8 us
    ppermute x28, starting transfers between devices: 35.6 us -> 33.9 us  [swap(): lax.ppermute(blocks[d], 'gy', [(i, i ^ d) for i in range(groups)])]
  transfers between devices with their start and end apart: 34 -> 34, of which waited for: 15 -> 14; matrix products, arithmetic and copies ran while one was open for 6% -> 6% of each run, Pallas kernels for 24% -> 24%
where the time goes in v4:
time: 172 us; the launch traced here: 171 us
  waiting for transfers between devices  53.8 us (31%)
  Pallas kernels  52.7 us (31%)
  starting transfers between devices  51.6 us (30%)
  matrix products  6.71 us (4%)
  local copies, waits for them, and re-layouts  4.47 us (3%)
    ppermute x28, waiting for transfers between devices, swap(): lax.ppermute(blocks[d], 'gy', [(i, i ^ d) for i in range(groups)])  48.9 us
    ppermute x28, starting transfers between devices, swap(): lax.ppermute(blocks[d], 'gy', [(i, i ^ d) for i in range(groups)])  33.9 us
    pallas_call x2, Pallas kernels, solve(): pl.pallas_call(functools.partial(solve_kernel, groups, stage, width, band...  27.4 us
    pallas_call x3, Pallas kernels, advance(): pl.pallas_call(functools.partial(advance_kernel, steps, chunk, chunks), o...  16.1 us
    ppermute x1, starting transfers between devices, on_device(): lax.ppermute(high, 'gx', pairs(across_x, 1))  4.27 us
    pallas_call x1, Pallas kernels, curl(): pl.pallas_call(functools.partial(curl_kernel, groups, gauge, total // chu...  3.9 us
    ppermute x1, waiting for transfers between devices, on_device(): lax.ppermute(low, 'gx', pairs(across_x, -1))  3.87 us
    ppermute x1, starting transfers between devices, on_device(): lax.ppermute(first_rows, 'gy', pairs(groups, -1))  3.64 us
  transfers between devices with their start and end apart: 34, of which 14 were waited for; matrix products, arithmetic and copies ran while one was open for 6% of the time, Pallas kernels for 24%

profile of v4, /device:TPU:10, one launch (start us, length us, event | category | flops | bytes accessed | tf_op | source)
XLA Modules:
  0.0 170.9 jit_solution(13144316682222936118)
XLA Ops:
  0.7 3.1 %outline.1 = (f32[6,32,256]{2,1,0:T(8,128)}, f32[6,32,256]{2,1,0:T(8,128)}, f32[6,32,256]{2,1,0:T(8,128)}, f32[6,32,256]{2,1,0:T(8,128)}) custom-call(f32[3,32,32,256]{3,2,1,0:T(8,128)} %vort.5, f32[3,32,32,256]{3,2,1,0:T(8,128)} %vel.5, f32[3,32,32,256]{3,2,1,0:T(8,128)} %vort.5, f32[3,32,32,256]{3,2,1,0:T(8,128)} %vel.5, f32[3,32,32,256]{3,2,1,0:T(8,128)} %vort.5, ...), custom_call_target="tpu_custom_call" | custom-call | tf_op jit(solution)/shard_map/outline/pallas_call | solution.py:488
  3.8 3.5 %collective-permute-start = (f32[6,32,256]{2,1,0:T(8,128)}, f32[6,32,256]{2,1,0:T(8,128)S(1)}, u32[]{:S(2)}, u32[]{:S(2)}) collective-permute-start(f32[6,32,256]{2,1,0:T(8,128)} %get-tuple-element.81), channel_id=1, source_target_pairs={{0,8},{8,16},{16,24},{1,9},{9,17},{17,25},{2,10},{10,18},{18,26},{... | collective-permute-start | bytes 589832 | tf_op jit(solution)/shard_map/ppermute | solution.py:557
  7.3 2.5 %collective-permute-start.1 = (f32[6,32,256]{2,1,0:T(8,128)}, f32[6,32,256]{2,1,0:T(8,128)S(1)}, u32[]{:S(2)}, u32[]{:S(2)}) collective-permute-start(f32[6,32,256]{2,1,0:T(8,128)} %get-tuple-element.82), channel_id=1, source_target_pairs={{8,0},{16,8},{24,16},{9,1},{17,9},{25,17},{10,2},{18,10},{26,18},{... | collective-permute-start | bytes 589832 | tf_op jit(solution)/shard_map/ppermute | solution.py:558
  9.8 1.9 %collective-permute-start.2 = (f32[6,32,256]{2,1,0:T(8,128)}, f32[6,32,256]{2,1,0:T(8,128)S(1)}, u32[]{:S(2)}, u32[]{:S(2)}) collective-permute-start(f32[6,32,256]{2,1,0:T(8,128)} %get-tuple-element.83), channel_id=1, source_target_pairs={{0,1},{1,2},{2,3},{3,4},{4,5},{5,6},{6,7},{8,9},{9,10},{10,11},{11... | collective-permute-start | bytes 589832 | tf_op jit(solution)/shard_map/ppermute | solution.py:561
  11.7 3.6 %collective-permute-start.3 = (f32[6,32,256]{2,1,0:T(8,128)}, f32[6,32,256]{2,1,0:T(8,128)S(1)}, u32[]{:S(2)}, u32[]{:S(2)}) collective-permute-start(f32[6,32,256]{2,1,0:T(8,128)} %get-tuple-element.84), channel_id=1, source_target_pairs={{1,0},{2,1},{3,2},{4,3},{5,4},{6,5},{7,6},{9,8},{10,9},{11,10},{12... | collective-permute-start | bytes 589832 | tf_op jit(solution)/shard_map/ppermute | solution.py:562
  15.7 0.8 reshape.113.rest_0_
  17.1 0.6 pad.6.rest_0_
  17.8 1.0 collective-permute-done.3.yhi
  18.8 0.7 copy-done.3
  19.5 4.7 %advance_0_1.1 = (f32[3,32,32,256]{3,2,1,0:T(8,128)}, f32[200,256]{1,0:T(8,128)}, f32[200,256]{1,0:T(8,128)}, f32[200,256]{1,0:T(8,128)}, f32[200,256]{1,0:T(8,128)}) custom-call(s32[1]{0:T(128)} %bitcast.me_ref, f32[3,32,32,256]{3,2,1,0:T(8,128)} %vort.5, f32[3,32,32,256]{3,2,1,0:T(8,128)} %vel.5, f32[6,32,256]{2,1,0:T(8,128)} %copy-done, ...), custom_call_target="tpu_custom_call" | custom-call | tf_op jit(solution)/shard_map/advance_0_1/pallas_call | solution.py:230
  24.2 2.7 %collective-permute-start.7 = (f32[200,256]{1,0:T(8,128)}, f32[200,256]{1,0:T(8,128)S(1)}, u32[]{:S(2)}, u32[]{:S(2)}) collective-permute-start(f32[200,256]{1,0:T(8,128)} %get-tuple-element.91), channel_id=1, source_target_pairs={{0,4},{1,5},{2,6},{3,7},{4,0},{5,1},{6,2},{7,3},{8,12},{9,13},{10,... | collective-permute-start | bytes 614408 | tf_op jit(solution)/shard_map/ppermute | solution.py:539
  26.9 1.5 collective-permute-start.8
  28.4 1.6 collective-permute-start.9
  30.0 4.9 %advance_0_2.1 = (f32[3,32,32,256]{3,2,1,0:T(8,128)}, f32[192,256]{1,0:T(8,128)}, f32[320,256]{1,0:T(8,128)}, f32[320,256]{1,0:T(8,128)}, f32[320,256]{1,0:T(8,128)}) custom-call(s32[1]{0:T(128)} %bitcast.me_ref, f32[3,32,32,256]{3,2,1,0:T(8,128)} %vort.5, f32[3,32,32,256]{3,2,1,0:T(8,128)} %vel.5, ...), custom_call_target="tpu_custom_call", output_to_operand_aliasing={{0}: (8, {})} | custom-call | tf_op jit(solution)/shard_map/advance_0_2/pallas_call | solution.py:230
  34.9 0.6 collective-permute-start.4
  35.5 6.5 %advance_1_1.1 = (f32[3,32,32,256]{3,2,1,0:T(8,128)}, f32[192,256]{1,0:T(8,128)}, f32[192,256]{1,0:T(8,128)}, f32[192,256]{1,0:T(8,128)}, f32[192,256]{1,0:T(8,1...) custom-call(s32[1]{0:T(128)} %bitcast.me_ref, ...), custom_call_target="tpu_custom_call", output_to_operand_aliasing={{0}: (7, {})} | custom-call | tf_op jit(solution)/shard_map/advance_1_1/pallas_call | solution.py:230
  42.0 8.3 %collective-permute-done.7.refs_7_ = f32[200,256]{1,0:T(8,128)S(1)} collective-permute-done((f32[200,256]{1,0:T(8,128)}, f32[200,256]{1,0:T(8,128)S(1)}, u32[]{:S(2)}, u32[]{:S(2)}) %collective-permute-start.7) | collective-permute-done | bytes 204832 | tf_op jit(solution)/shard_map/ppermute | solution.py:539
  50.3 4.4 %collective-permute-done.8.refs_5_ = f32[200,256]{1,0:T(8,128)S(1)} collective-permute-done((f32[200,256]{1,0:T(8,128)}, f32[200,256]{1,0:T(8,128)S(1)}, u32[]{:S(2)}, u32[]{:S(2)}) %collective-permute-start.8) | collective-permute-done | bytes 204832 | tf_op jit(solution)/shard_map/ppermute | solution.py:539
  54.7 4.4 %collective-permute-done.9.refs_3_ = f32[200,256]{1,0:T(8,128)S(1)} collective-permute-done((f32[200,256]{1,0:T(8,128)}, f32[200,256]{1,0:T(8,128)S(1)}, u32[]{:S(2)}, u32[]{:S(2)}) %collective-permute-start.9) | collective-permute-done | bytes 204832 | tf_op jit(solution)/shard_map/ppermute | solution.py:539
  59.1 3.7 %collective-permute-done.10.refs_1_ = f32[200,256]{1,0:T(8,128)S(1)} collective-permute-done((f32[200,256]{1,0:T(8,128)}, f32[200,256]{1,0:T(8,128)S(1)}, u32[]{:S(2)}, u32[]{:S(2)}) %collective-permute-start.10) | collective-permute-done | bytes 204832 | tf_op jit(solution)/shard_map/ppermute | solution.py:539
  62.9 4.2 %collective-permute-start.14 = (f32[192,256]{1,0:T(8,128)}, f32[192,256]{1,0:T(8,128)}, u32[]{:S(2)}, u32[]{:S(2)}) collective-permute-start(f32[192,256]{1,0:T(8,128)} %get-tuple-element.108), channel_id=1, source_target_pairs={{0,2},{1,3},{2,0},{3,1},{4,6},{5,7},{6,4},{7,5},{8,10},{9,11},{10,... | collective-permute-start | bytes 589832 | tf_op jit(solution)/shard_map/ppermute | solution.py:539
  67.2 3.8 %collective-permute-done.6.refs_2_ = f32[320,256]{1,0:T(8,128)S(1)} collective-permute-done((f32[320,256]{1,0:T(8,128)S(1)}, f32[320,256]{1,0:T(8,128)S(1)}, u32[]{:S(2)}, u32[]{:S(2)}) %collective-permute-start.6) | collective-permute-done | bytes 327712 | tf_op jit(solution)/shard_map/ppermute | solution.py:539
  70.9 4.8 %collective-permute-start.15 = (f32[192,256]{1,0:T(8,128)}, f32[192,256]{1,0:T(8,128)}, u32[]{:S(2)}, u32[]{:S(2)}) collective-permute-start(f32[192,256]{1,0:T(8,128)} %get-tuple-element.109), channel_id=1, source_target_pairs={{0,5},{1,4},{2,7},{3,6},{4,1},{5,0},{6,3},{7,2},{8,13},{9,12},{10,... | collective-permute-start | bytes 589832 | tf_op jit(solution)/shard_map/ppermute | solution.py:539
  75.8 0.6 gather_fusion
  76.7 3.5 %convolution_bitcast_fusion = f32[2,256,512]{2,1,0:T(8,128)S(1)} fusion(f32[4,512,64]{2,1,0:T(8,128)S(1)} %gather.11, f32[4,8,2,8,256]{4,3,2,1,0:T(8,128)S(1)} %bitcast.42, pred[4]{0:T(512)(128)(4,1)S(1)} %compare_and_fusion), kind=kOutput, calls=%fused_computation.1 | convolution fusion | flops 805437440 | bytes 2097156 | tf_op jit(solution)/shard_map/kjc,jmc->km/dot_general | solution.py:109
  80.2 1.3 fusion.5
  81.6 1.6 collective-permute-done.12.refs_2_
  83.2 1.9 %convolution_add_fusion.green = f32[256,512]{1,0:T(8,128)} fusion(f32[256,512]{1,0:T(8,128)S(1)} %fusion.5, f32[512,512]{1,0:T(8,128)S(1)} %copy-done.4, f32[2,256,512]{2,1,0:T(8,128)S(1)} %convolution_bitcast_fusion), kind=kOutput, calls=%fused_computation.2 | convolution fusion | flops 805437440 | bytes 2621440 | tf_op jit(solution)/shard_map/dot_general | solution.py:113
  85.1 13.5 %solve_first.1 = (f32[136,256]{1,0:T(8,128)}, f32[136,256]{1,0:T(8,128)}, f32[136,256]{1,0:T(8,128)}, f32[136,256]{1,0:T(8,128)}, f32[136,256]{1,0:T(8,128)}, /*...) custom-call(s32[1]{0:T(128)} %bitcast.me_ref, ...), custom_call_target="tpu_custom_call" | custom-call | tf_op jit(solution)/shard_map/solve_first/pallas_call | solution.py:355
  98.6 3.9 %collective-permute-start.18 = (f32[136,256]{1,0:T(8,128)}, f32[136,256]{1,0:T(8,128)S(1)}, u32[]{:S(2)}, u32[]{:S(2)}) collective-permute-start(f32[136,256]{1,0:T(8,128)} %get-tuple-element.113), channel_id=1, source_target_pairs={{0,7},{1,6},{2,5},{3,4},{4,3},{5,2},{6,1},{7,0},{8,15},{9,14},{10,... | collective-permute-start | bytes 417800 | tf_op jit(solution)/shard_map/ppermute | solution.py:539
  102.5 3.1 %collective-permute-start.19 = (f32[136,256]{1,0:T(8,128)}, f32[136,256]{1,0:T(8,128)S(1)}, u32[]{:S(2)}, u32[]{:S(2)}) collective-permute-start(f32[136,256]{1,0:T(8,128)} %get-tuple-element.114), channel_id=1, source_target_pairs={{0,6},{1,7},{2,4},{3,5},{4,2},{5,3},{6,0},{7,1},{8,14},{9,15},{10,... | collective-permute-start | bytes 417800 | tf_op jit(solution)/shard_map/ppermute | solution.py:539
  105.7 2.0 %collective-permute-start.21 = (f32[136,256]{1,0:T(8,128)}, f32[136,256]{1,0:T(8,128)S(1)}, u32[]{:S(2)}, u32[]{:S(2)}) collective-permute-start(f32[136,256]{1,0:T(8,128)} %get-tuple-element.116), channel_id=1, source_target_pairs={{0,4},{1,5},{2,6},{3,7},{4,0},{5,1},{6,2},{7,3},{8,12},{9,13},{10,... | collective-permute-start | bytes 417800 | tf_op jit(solution)/shard_map/ppermute | solution.py:539
  107.7 13.9 %solve_second.1 = (f32[200,256]{1,0:T(8,128)}, f32[200,256]{1,0:T(8,128)}, f32[200,256]{1,0:T(8,128)}, f32[200,256]{1,0:T(8,128)}, f32[200,256]{1,0:T(8,128)}, /...) custom-call(s32[1]{0:T(128)} %bitcast.me_ref, bf16[512,768]{1,0:T(8,128)(2,1)} %constant.101.clone.fz, ...), custom_call_target="tpu_custom_call" | custom-call | tf_op jit(solution)/shard_map/solve_second/pallas_call | solution.py:355
  121.6 2.3 %collective-permute-start.23 = (f32[136,256]{1,0:T(8,128)S(1)}, f32[136,256]{1,0:T(8,128)S(1)}, u32[]{:S(2)}, u32[]{:S(2)}) collective-permute-start(f32[136,256]{1,0:T(8,128)S(1)} %copy-done.39), channel_id=1, source_target_pairs={{0,2},{1,3},{2,0},{3,1},{4,6},{5,7},{6,4},{7,5},{8,10},{9,11},{10,... | collective-permute-start | bytes 417800 | tf_op jit(solution)/shard_map/ppermute | solution.py:539
  124.2 0.6 collective-permute-start.28
  124.8 2.4 %collective-permute-done.21.refs_4_ = f32[136,256]{1,0:T(8,128)S(1)} collective-permute-done((f32[136,256]{1,0:T(8,128)}, f32[136,256]{1,0:T(8,128)S(1)}, u32[]{:S(2)}, u32[]{:S(2)}) %collective-permute-start.21) | collective-permute-done | bytes 139296 | tf_op jit(solution)/shard_map/ppermute | solution.py:539
  127.5 0.6 collective-permute-start.29
  128.1 10.5 %collective-permute-done.23.refs_6_ = f32[136,256]{1,0:T(8,128)S(1)} collective-permute-done((f32[136,256]{1,0:T(8,128)S(1)}, f32[136,256]{1,0:T(8,128)S(1)}, u32[]{:S(2)}, u32[]{:S(2)}) %collective-permute-start.23) | collective-permute-done | bytes 139296 | tf_op jit(solution)/shard_map/ppermute | solution.py:539
  138.6 3.4 %collective-permute-start.30 = (f32[200,256]{1,0:T(8,128)}, f32[200,256]{1,0:T(8,128)S(1)}, u32[]{:S(2)}, u32[]{:S(2)}) collective-permute-start(f32[200,256]{1,0:T(8,128)} %get-tuple-element.143), channel_id=1, source_target_pairs={{0,5},{1,4},{2,7},{3,6},{4,1},{5,0},{6,3},{7,2},{8,13},{9,12},{10,... | collective-permute-start | bytes 614408 | tf_op jit(solution)/shard_map/ppermute | solution.py:539
  142.3 1.1 collective-permute-start.32
  143.4 0.7 collective-permute-start.33
  144.2 2.2 %pick.1 = (f32[2,32,256]{2,1,0:T(8,128)}, f32[2,32,256]{2,1,0:T(8,128)}) custom-call(s32[1]{0:T(128)} %bitcast.me_ref, f32[136,256]{1,0:T(8,128)} %get-tuple-element.130.refs_0_, f32[136,256]{1,0:T(8,128)} %copy-done.9, f32[136,256]{1,0:T(8,128)} %copy-done.10, f32[136,256]{1,0:T(8,128)} %copy-done.11, f32[136,256]{1,0:T(8,128)} %copy-done.12, ...), custom_call_target="tpu_custom_call" | custom-call | tf_op jit(solution)/shard_map/pick/pallas_call | solution.py:520
  146.4 8.2 %collective-permute-done.29.refs_10_ = f32[200,256]{1,0:T(8,128)S(1)} collective-permute-done((f32[200,256]{1,0:T(8,128)}, f32[200,256]{1,0:T(8,128)S(1)}, u32[]{:S(2)}, u32[]{:S(2)}) %collective-permute-start.29) | collective-permute-done | bytes 204832 | tf_op jit(solution)/shard_map/ppermute | solution.py:539
  154.6 4.3 %collective-permute-start.26 = (f32[2,32,256]{2,1,0:T(8,128)}, f32[2,32,256]{2,1,0:T(8,128)S(1)}, u32[]{:S(2)}, u32[]{:S(2)}) collective-permute-start(f32[2,32,256]{2,1,0:T(8,128)} %get-tuple-element.138), channel_id=1, source_target_pairs={{0,8},{8,16},{16,24},{1,9},{9,17},{17,25},{2,10},{10,18},{18,26},{... | collective-permute-start | bytes 196616 | tf_op jit(solution)/shard_map/ppermute | solution.py:601
  158.9 1.9 %collective-permute-start.27 = (f32[2,32,256]{2,1,0:T(8,128)}, f32[2,32,256]{2,1,0:T(8,128)S(1)}, u32[]{:S(2)}, u32[]{:S(2)}) collective-permute-start(f32[2,32,256]{2,1,0:T(8,128)} %get-tuple-element.139), channel_id=1, source_target_pairs={{8,0},{16,8},{24,16},{9,1},{17,9},{25,17},{10,2},{18,10},{26,18},{... | collective-permute-start | bytes 196616 | tf_op jit(solution)/shard_map/ppermute | solution.py:602
  160.9 1.4 collective-permute-done.31.refs_12_
  162.3 3.9 %collective-permute-done.27.xhi = f32[2,32,256]{2,1,0:T(8,128)S(1)} collective-permute-done((f32[2,32,256]{2,1,0:T(8,128)}, f32[2,32,256]{2,1,0:T(8,128)S(1)}, u32[]{:S(2)}, u32[]{:S(2)}) %collective-permute-start.27) | collective-permute-done | bytes 65568 | tf_op jit(solution)/shard_map/ppermute | solution.py:602
  166.8 3.9 %curl.1 = f32[3,32,32,256]{3,2,1,0:T(8,128)} custom-call(s32[1]{0:T(128)} %bitcast.me_ref, f32[2,32,256]{2,1,0:T(8,128)} %copy-done.31, f32[2,32,256]{2,1,0:T(8,128)} %copy-done.32, f32[136,256]{1,0:T(8,128)} %get-tuple-element.130.refs_0_, f32[136,256]{1,0:T(8,128)} %copy-done.9, f32[136,256]{1,0:T(8,128)} %copy-done.10, f32[136,256]{1,0:T(8,128)} %copy-done.11, ...), custom_call_target="tpu_custom_call" | custom-call | tf_op jit(solution)/shard_map/curl/pallas_call | solution.py:449
  (135 shorter events, 3.3 us)
Async XLA Ops:
  0.6 15.8 %copy-start.16 = (f32[2,2,256,256]{2,1,3,0:T(2,128)S(1)}, f32[2,2,256,256]{2,1,3,0:T(2,128)}, u32[]{:S(2)}) copy-start(f32[2,2,256,256]{2,1,3,0:T(2,128)} %constant.105.clone) | copy-start | bytes 3145732
  0.6 14.7 %copy-start.30 = (f32[512,64]{0,1:T(8,128)S(1)}, f32[512,64]{0,1:T(8,128)}, u32[]{:S(2)}) copy-start(f32[512,64]{0,1:T(8,128)} %param.14) | copy-start | bytes 393220
  3.8 13.9 %collective-permute-start = (f32[6,32,256]{2,1,0:T(8,128)}, f32[6,32,256]{2,1,0:T(8,128)S(1)}, u32[]{:S(2)}, u32[]{:S(2)}) collective-permute-start(f32[6,32,256]{2,1,0:T(8,128)} %get-tuple-element.81), channel_id=1, source_target_pairs={{0,8},{8,16},{16,24},{1,9},{9,17},{17,25},{2,10},{10,18},{18,26},{... | collective-permute-start | bytes 589832 | tf_op jit(solution)/shard_map/ppermute | solution.py:557
  7.3 10.5 %collective-permute-start.1 = (f32[6,32,256]{2,1,0:T(8,128)}, f32[6,32,256]{2,1,0:T(8,128)S(1)}, u32[]{:S(2)}, u32[]{:S(2)}) collective-permute-start(f32[6,32,256]{2,1,0:T(8,128)} %get-tuple-element.82), channel_id=1, source_target_pairs={{8,0},{16,8},{24,16},{9,1},{17,9},{25,17},{10,2},{18,10},{26,18},{... | collective-permute-start | bytes 589832 | tf_op jit(solution)/shard_map/ppermute | solution.py:558
  9.8 8.1 %collective-permute-start.2 = (f32[6,32,256]{2,1,0:T(8,128)}, f32[6,32,256]{2,1,0:T(8,128)S(1)}, u32[]{:S(2)}, u32[]{:S(2)}) collective-permute-start(f32[6,32,256]{2,1,0:T(8,128)} %get-tuple-element.83), channel_id=1, source_target_pairs={{0,1},{1,2},{2,3},{3,4},{4,5},{5,6},{6,7},{8,9},{9,10},{10,11},{11... | collective-permute-start | bytes 589832 | tf_op jit(solution)/shard_map/ppermute | solution.py:561
  11.7 7.1 %collective-permute-start.3 = (f32[6,32,256]{2,1,0:T(8,128)}, f32[6,32,256]{2,1,0:T(8,128)S(1)}, u32[]{:S(2)}, u32[]{:S(2)}) collective-permute-start(f32[6,32,256]{2,1,0:T(8,128)} %get-tuple-element.84), channel_id=1, source_target_pairs={{1,0},{2,1},{3,2},{4,3},{5,4},{6,5},{7,6},{9,8},{10,9},{11,10},{12... | collective-permute-start | bytes 589832 | tf_op jit(solution)/shard_map/ppermute | solution.py:562
  24.2 26.0 %collective-permute-start.7 = (f32[200,256]{1,0:T(8,128)}, f32[200,256]{1,0:T(8,128)S(1)}, u32[]{:S(2)}, u32[]{:S(2)}) collective-permute-start(f32[200,256]{1,0:T(8,128)} %get-tuple-element.91), channel_id=1, source_target_pairs={{0,4},{1,5},{2,6},{3,7},{4,0},{5,1},{6,2},{7,3},{8,12},{9,13},{10,... | collective-permute-start | bytes 614408 | tf_op jit(solution)/shard_map/ppermute | solution.py:539
  26.9 27.8 %collective-permute-start.8 = (f32[200,256]{1,0:T(8,128)}, f32[200,256]{1,0:T(8,128)S(1)}, u32[]{:S(2)}, u32[]{:S(2)}) collective-permute-start(f32[200,256]{1,0:T(8,128)} %get-tuple-element.92), channel_id=1, source_target_pairs={{0,5},{1,4},{2,7},{3,6},{4,1},{5,0},{6,3},{7,2},{8,13},{9,12},{10,... | collective-permute-start | bytes 614408 | tf_op jit(solution)/shard_map/ppermute | solution.py:539
  28.4 30.7 %collective-permute-start.9 = (f32[200,256]{1,0:T(8,128)}, f32[200,256]{1,0:T(8,128)S(1)}, u32[]{:S(2)}, u32[]{:S(2)}) collective-permute-start(f32[200,256]{1,0:T(8,128)} %get-tuple-element.93), channel_id=1, source_target_pairs={{0,6},{1,7},{2,4},{3,5},{4,2},{5,3},{6,0},{7,1},{8,14},{9,15},{10,... | collective-permute-start | bytes 614408 | tf_op jit(solution)/shard_map/ppermute | solution.py:539
  30.0 32.8 %collective-permute-start.10 = (f32[200,256]{1,0:T(8,128)}, f32[200,256]{1,0:T(8,128)S(1)}, u32[]{:S(2)}, u32[]{:S(2)}) collective-permute-start(f32[200,256]{1,0:T(8,128)} %get-tuple-element.94), channel_id=1, source_target_pairs={{0,7},{1,6},{2,5},{3,4},{4,3},{5,2},{6,1},{7,0},{8,15},{9,14},{10,... | collective-permute-start | bytes 614408 | tf_op jit(solution)/shard_map/ppermute | solution.py:539
  34.9 27.9 %collective-permute-start.4 = (f32[320,256]{1,0:T(8,128)}, f32[320,256]{1,0:T(8,128)S(1)}, u32[]{:S(2)}, u32[]{:S(2)}) collective-permute-start(f32[320,256]{1,0:T(8,128)} %get-tuple-element.88), channel_id=1, source_target_pairs={{0,1},{1,0},{2,3},{3,2},{4,5},{5,4},{6,7},{7,6},{8,9},{9,8},{10,11... | collective-permute-start | bytes 983048 | tf_op jit(solution)/shard_map/ppermute | solution.py:539
  35.5 14.8 %copy-start.35 = (f32[320,256]{1,0:T(8,128)S(1)}, f32[320,256]{1,0:T(8,128)}, u32[]{:S(2)}) copy-start(f32[320,256]{1,0:T(8,128)} %get-tuple-element.89) | copy-start | bytes 983044
  35.5 19.2 %copy-start.34 = (f32[320,256]{1,0:T(8,128)S(1)}, f32[320,256]{1,0:T(8,128)}, u32[]{:S(2)}) copy-start(f32[320,256]{1,0:T(8,128)} %get-tuple-element.90) | copy-start | bytes 983044
  50.3 12.6 %collective-permute-start.5 = (f32[320,256]{1,0:T(8,128)S(1)}, f32[320,256]{1,0:T(8,128)S(1)}, u32[]{:S(2)}, u32[]{:S(2)}) collective-permute-start(f32[320,256]{1,0:T(8,128)S(1)} %copy-done.35), channel_id=1, source_target_pairs={{0,2},{1,3},{2,0},{3,1},{4,6},{5,7},{6,4},{7,5},{8,10},{9,11},{10,... | collective-permute-start | bytes 983048 | tf_op jit(solution)/shard_map/ppermute | solution.py:539
  54.7 16.2 %collective-permute-start.6 = (f32[320,256]{1,0:T(8,128)S(1)}, f32[320,256]{1,0:T(8,128)S(1)}, u32[]{:S(2)}, u32[]{:S(2)}) collective-permute-start(f32[320,256]{1,0:T(8,128)S(1)} %copy-done.34), channel_id=1, source_target_pairs={{0,3},{1,2},{2,1},{3,0},{4,7},{5,6},{6,5},{7,4},{8,11},{9,10},{10,... | collective-permute-start | bytes 983048 | tf_op jit(solution)/shard_map/ppermute | solution.py:539
  59.1 16.7 %copy-start.19 = (f32[200,256]{1,0:T(8,128)}, f32[200,256]{1,0:T(8,128)S(1)}, u32[]{:S(2)}) copy-start(f32[200,256]{1,0:T(8,128)S(1)} %collective-permute-done.9.refs_3_) | copy-start | bytes 614404
  59.1 22.4 %collective-permute-start.11 = (f32[192,256]{1,0:T(8,128)}, f32[192,256]{1,0:T(8,128)}, u32[]{:S(2)}, u32[]{:S(2)}) collective-permute-start(f32[192,256]{1,0:T(8,128)} %get-tuple-element.105), channel_id=1, source_target_pairs={{0,7},{1,6},{2,5},{3,4},{4,3},{5,2},{6,1},{7,0},{8,15},{9,14},{10,... | collective-permute-start | bytes 589832 | tf_op jit(solution)/shard_map/ppermute | solution.py:539
  62.7 20.4 %collective-permute-start.12 = (f32[192,256]{1,0:T(8,128)}, f32[192,256]{1,0:T(8,128)}, u32[]{:S(2)}, u32[]{:S(2)}) collective-permute-start(f32[192,256]{1,0:T(8,128)} %get-tuple-element.106), channel_id=1, source_target_pairs={{0,3},{1,2},{2,1},{3,0},{4,7},{5,6},{6,5},{7,4},{8,11},{9,10},{10,... | collective-permute-start | bytes 589832 | tf_op jit(solution)/shard_map/ppermute | solution.py:539
  62.8 17.4 %copy-start.6 = (f32[320,256]{1,0:T(8,128)}, f32[320,256]{1,0:T(8,128)S(1)}, u32[]{:S(2)}) copy-start(f32[320,256]{1,0:T(8,128)S(1)} %collective-permute-done.4.refs_6_) | copy-start | bytes 983044
  62.8 35.8 %collective-permute-start.13 = (f32[192,256]{1,0:T(8,128)}, f32[192,256]{1,0:T(8,128)}, u32[]{:S(2)}, u32[]{:S(2)}) collective-permute-start(f32[192,256]{1,0:T(8,128)} %get-tuple-element.107), channel_id=1, source_target_pairs={{0,6},{1,7},{2,4},{3,5},{4,2},{5,3},{6,0},{7,1},{8,14},{9,15},{10,... | collective-permute-start | bytes 589832 | tf_op jit(solution)/shard_map/ppermute | solution.py:539
  62.9 35.6 %collective-permute-start.14 = (f32[192,256]{1,0:T(8,128)}, f32[192,256]{1,0:T(8,128)}, u32[]{:S(2)}, u32[]{:S(2)}) collective-permute-start(f32[192,256]{1,0:T(8,128)} %get-tuple-element.108), channel_id=1, source_target_pairs={{0,2},{1,3},{2,0},{3,1},{4,6},{5,7},{6,4},{7,5},{8,10},{9,11},{10,... | collective-permute-start | bytes 589832 | tf_op jit(solution)/shard_map/ppermute | solution.py:539
  70.9 27.6 %collective-permute-start.15 = (f32[192,256]{1,0:T(8,128)}, f32[192,256]{1,0:T(8,128)}, u32[]{:S(2)}, u32[]{:S(2)}) collective-permute-start(f32[192,256]{1,0:T(8,128)} %get-tuple-element.109), channel_id=1, source_target_pairs={{0,5},{1,4},{2,7},{3,6},{4,1},{5,0},{6,3},{7,2},{8,13},{9,12},{10,... | collective-permute-start | bytes 589832 | tf_op jit(solution)/shard_map/ppermute | solution.py:539
  81.5 17.1 %collective-permute-start.16 = (f32[192,256]{1,0:T(8,128)S(1)}, f32[192,256]{1,0:T(8,128)S(1)}, u32[]{:S(2)}, u32[]{:S(2)}) collective-permute-start(f32[192,256]{1,0:T(8,128)S(1)} %copy-done.37), channel_id=1, source_target_pairs={{0,1},{1,0},{2,3},{3,2},{4,5},{5,4},{6,7},{7,6},{8,9},{9,8},{10,11... | collective-permute-start | bytes 589832 | tf_op jit(solution)/shard_map/ppermute | solution.py:539
  83.2 15.4 %collective-permute-start.17 = (f32[192,256]{1,0:T(8,128)S(1)}, f32[192,256]{1,0:T(8,128)S(1)}, u32[]{:S(2)}, u32[]{:S(2)}) collective-permute-start(f32[192,256]{1,0:T(8,128)S(1)} %copy-done.36), channel_id=1, source_target_pairs={{0,4},{1,5},{2,6},{3,7},{4,0},{5,1},{6,2},{7,3},{8,12},{9,13},{10,... | collective-permute-start | bytes 589832 | tf_op jit(solution)/shard_map/ppermute | solution.py:539
  98.6 23.0 %collective-permute-start.18 = (f32[136,256]{1,0:T(8,128)}, f32[136,256]{1,0:T(8,128)S(1)}, u32[]{:S(2)}, u32[]{:S(2)}) collective-permute-start(f32[136,256]{1,0:T(8,128)} %get-tuple-element.113), channel_id=1, source_target_pairs={{0,7},{1,6},{2,5},{3,4},{4,3},{5,2},{6,1},{7,0},{8,15},{9,14},{10,... | collective-permute-start | bytes 417800 | tf_op jit(solution)/shard_map/ppermute | solution.py:539
  102.5 21.4 %collective-permute-start.19 = (f32[136,256]{1,0:T(8,128)}, f32[136,256]{1,0:T(8,128)S(1)}, u32[]{:S(2)}, u32[]{:S(2)}) collective-permute-start(f32[136,256]{1,0:T(8,128)} %get-tuple-element.114), channel_id=1, source_target_pairs={{0,6},{1,7},{2,4},{3,5},{4,2},{5,3},{6,0},{7,1},{8,14},{9,15},{10,... | collective-permute-start | bytes 417800 | tf_op jit(solution)/shard_map/ppermute | solution.py:539
  105.6 18.6 %collective-permute-start.20 = (f32[136,256]{1,0:T(8,128)}, f32[136,256]{1,0:T(8,128)S(1)}, u32[]{:S(2)}, u32[]{:S(2)}) collective-permute-start(f32[136,256]{1,0:T(8,128)} %get-tuple-element.115), channel_id=1, source_target_pairs={{0,5},{1,4},{2,7},{3,6},{4,1},{5,0},{6,3},{7,2},{8,13},{9,12},{10,... | collective-permute-start | bytes 417800 | tf_op jit(solution)/shard_map/ppermute | solution.py:539
  105.7 21.5 %collective-permute-start.21 = (f32[136,256]{1,0:T(8,128)}, f32[136,256]{1,0:T(8,128)S(1)}, u32[]{:S(2)}, u32[]{:S(2)}) collective-permute-start(f32[136,256]{1,0:T(8,128)} %get-tuple-element.116), channel_id=1, source_target_pairs={{0,4},{1,5},{2,6},{3,7},{4,0},{5,1},{6,2},{7,3},{8,12},{9,13},{10,... | collective-permute-start | bytes 417800 | tf_op jit(solution)/shard_map/ppermute | solution.py:539
  107.7 19.8 %collective-permute-start.22 = (f32[136,256]{1,0:T(8,128)}, f32[136,256]{1,0:T(8,128)S(1)}, u32[]{:S(2)}, u32[]{:S(2)}) collective-permute-start(f32[136,256]{1,0:T(8,128)} %get-tuple-element.117), channel_id=1, source_target_pairs={{0,3},{1,2},{2,1},{3,0},{4,7},{5,6},{6,5},{7,4},{8,11},{9,10},{10,... | collective-permute-start | bytes 417800 | tf_op jit(solution)/shard_map/ppermute | solution.py:539
  107.7 19.5 %copy-start.38 = (f32[136,256]{1,0:T(8,128)S(1)}, f32[136,256]{1,0:T(8,128)}, u32[]{:S(2)}) copy-start(f32[136,256]{1,0:T(8,128)} %get-tuple-element.119) | copy-start | bytes 417796
  121.6 22.5 %copy-start.9 = (f32[136,256]{1,0:T(8,128)}, f32[136,256]{1,0:T(8,128)S(1)}, u32[]{:S(2)}) copy-start(f32[136,256]{1,0:T(8,128)S(1)} %collective-permute-done.18.refs_1_) | copy-start | bytes 417796
  121.6 16.9 %collective-permute-start.23 = (f32[136,256]{1,0:T(8,128)S(1)}, f32[136,256]{1,0:T(8,128)S(1)}, u32[]{:S(2)}, u32[]{:S(2)}) collective-permute-start(f32[136,256]{1,0:T(8,128)S(1)} %copy-done.39), channel_id=1, source_target_pairs={{0,2},{1,3},{2,0},{3,1},{4,6},{5,7},{6,4},{7,5},{8,10},{9,11},{10,... | collective-permute-start | bytes 417800 | tf_op jit(solution)/shard_map/ppermute | solution.py:539
  123.9 20.2 %copy-start.10 = (f32[136,256]{1,0:T(8,128)}, f32[136,256]{1,0:T(8,128)S(1)}, u32[]{:S(2)}) copy-start(f32[136,256]{1,0:T(8,128)S(1)} %collective-permute-done.19.refs_2_) | copy-start | bytes 417796
  123.9 18.4 %collective-permute-start.25 = (f32[200,256]{1,0:T(8,128)}, f32[200,256]{1,0:T(8,128)S(1)}, u32[]{:S(2)}, u32[]{:S(2)}) collective-permute-start(f32[200,256]{1,0:T(8,128)} %get-tuple-element.129), channel_id=1, source_target_pairs={{0,1},{1,0},{2,3},{3,2},{4,5},{5,4},{6,7},{7,6},{8,9},{9,8},{10,11... | collective-permute-start | bytes 614408 | tf_op jit(solution)/shard_map/ppermute | solution.py:539
  124.2 20.0 %copy-start.11 = (f32[136,256]{1,0:T(8,128)}, f32[136,256]{1,0:T(8,128)S(1)}, u32[]{:S(2)}) copy-start(f32[136,256]{1,0:T(8,128)S(1)} %collective-permute-done.20.refs_3_) | copy-start | bytes 417796
  124.2 19.3 %collective-permute-start.28 = (f32[200,256]{1,0:T(8,128)}, f32[200,256]{1,0:T(8,128)S(1)}, u32[]{:S(2)}, u32[]{:S(2)}) collective-permute-start(f32[200,256]{1,0:T(8,128)} %get-tuple-element.141), channel_id=1, source_target_pairs={{0,7},{1,6},{2,5},{3,4},{4,3},{5,2},{6,1},{7,0},{8,15},{9,14},{10,... | collective-permute-start | bytes 614408 | tf_op jit(solution)/shard_map/ppermute | solution.py:539
  127.2 17.0 %copy-start.12 = (f32[136,256]{1,0:T(8,128)}, f32[136,256]{1,0:T(8,128)S(1)}, u32[]{:S(2)}) copy-start(f32[136,256]{1,0:T(8,128)S(1)} %collective-permute-done.21.refs_4_) | copy-start | bytes 417796
  127.2 14.7 %collective-permute-start.24 = (f32[136,256]{1,0:T(8,128)S(1)}, f32[136,256]{1,0:T(8,128)S(1)}, u32[]{:S(2)}, u32[]{:S(2)}) collective-permute-start(f32[136,256]{1,0:T(8,128)S(1)} %copy-done.38), channel_id=1, source_target_pairs={{0,1},{1,0},{2,3},{3,2},{4,5},{5,4},{6,7},{7,6},{8,9},{9,8},{10,11... | collective-permute-start | bytes 417800 | tf_op jit(solution)/shard_map/ppermute | solution.py:539
  127.4 16.7 %copy-start.13 = (f32[136,256]{1,0:T(8,128)}, f32[136,256]{1,0:T(8,128)S(1)}, u32[]{:S(2)}) copy-start(f32[136,256]{1,0:T(8,128)S(1)} %collective-permute-done.22.refs_5_) | copy-start | bytes 417796
  127.5 27.2 %collective-permute-start.29 = (f32[200,256]{1,0:T(8,128)}, f32[200,256]{1,0:T(8,128)S(1)}, u32[]{:S(2)}, u32[]{:S(2)}) collective-permute-start(f32[200,256]{1,0:T(8,128)} %get-tuple-element.142), channel_id=1, source_target_pairs={{0,6},{1,7},{2,4},{3,5},{4,2},{5,3},{6,0},{7,1},{8,14},{9,15},{10,... | collective-permute-start | bytes 614408 | tf_op jit(solution)/shard_map/ppermute | solution.py:539
  138.6 20.4 %collective-permute-start.30 = (f32[200,256]{1,0:T(8,128)}, f32[200,256]{1,0:T(8,128)S(1)}, u32[]{:S(2)}, u32[]{:S(2)}) collective-permute-start(f32[200,256]{1,0:T(8,128)} %get-tuple-element.143), channel_id=1, source_target_pairs={{0,5},{1,4},{2,7},{3,6},{4,1},{5,0},{6,3},{7,2},{8,13},{9,12},{10,... | collective-permute-start | bytes 614408 | tf_op jit(solution)/shard_map/ppermute | solution.py:539
  141.9 20.4 %collective-permute-start.31 = (f32[200,256]{1,0:T(8,128)}, f32[200,256]{1,0:T(8,128)S(1)}, u32[]{:S(2)}, u32[]{:S(2)}) collective-permute-start(f32[200,256]{1,0:T(8,128)} %get-tuple-element.144), channel_id=1, source_target_pairs={{0,4},{1,5},{2,6},{3,7},{4,0},{5,1},{6,2},{7,3},{8,12},{9,13},{10,... | collective-permute-start | bytes 614408 | tf_op jit(solution)/shard_map/ppermute | solution.py:539
  142.3 23.9 %copy-start.21 = (f32[200,256]{1,0:T(8,128)}, f32[200,256]{1,0:T(8,128)S(1)}, u32[]{:S(2)}) copy-start(f32[200,256]{1,0:T(8,128)S(1)} %collective-permute-done.25.refs_15_) | copy-start | bytes 614404
  142.3 20.0 %collective-permute-start.32 = (f32[200,256]{1,0:T(8,128)}, f32[200,256]{1,0:T(8,128)S(1)}, u32[]{:S(2)}, u32[]{:S(2)}) collective-permute-start(f32[200,256]{1,0:T(8,128)} %get-tuple-element.145), channel_id=1, source_target_pairs={{0,3},{1,2},{2,1},{3,0},{4,7},{5,6},{6,5},{7,4},{8,11},{9,10},{10,... | collective-permute-start | bytes 614408 | tf_op jit(solution)/shard_map/ppermute | solution.py:539
  143.4 22.8 %copy-start.22 = (f32[200,256]{1,0:T(8,128)}, f32[200,256]{1,0:T(8,128)S(1)}, u32[]{:S(2)}) copy-start(f32[200,256]{1,0:T(8,128)S(1)} %collective-permute-done.28.refs_9_) | copy-start | bytes 614404
  143.4 18.9 %collective-permute-start.33 = (f32[200,256]{1,0:T(8,128)}, f32[200,256]{1,0:T(8,128)S(1)}, u32[]{:S(2)}, u32[]{:S(2)}) collective-permute-start(f32[200,256]{1,0:T(8,128)} %get-tuple-element.146), channel_id=1, source_target_pairs={{0,2},{1,3},{2,0},{3,1},{4,6},{5,7},{6,4},{7,5},{8,10},{9,11},{10,... | collective-permute-start | bytes 614408 | tf_op jit(solution)/shard_map/ppermute | solution.py:539
  154.6 7.7 %collective-permute-start.26 = (f32[2,32,256]{2,1,0:T(8,128)}, f32[2,32,256]{2,1,0:T(8,128)S(1)}, u32[]{:S(2)}, u32[]{:S(2)}) collective-permute-start(f32[2,32,256]{2,1,0:T(8,128)} %get-tuple-element.138), channel_id=1, source_target_pairs={{0,8},{8,16},{16,24},{1,9},{9,17},{17,25},{2,10},{10,18},{18,26},{... | collective-permute-start | bytes 196616 | tf_op jit(solution)/shard_map/ppermute | solution.py:601
  158.9 7.3 %collective-permute-start.27 = (f32[2,32,256]{2,1,0:T(8,128)}, f32[2,32,256]{2,1,0:T(8,128)S(1)}, u32[]{:S(2)}, u32[]{:S(2)}) collective-permute-start(f32[2,32,256]{2,1,0:T(8,128)} %get-tuple-element.139), channel_id=1, source_target_pairs={{8,0},{16,8},{24,16},{9,1},{17,9},{25,17},{10,2},{18,10},{26,18},{... | collective-permute-start | bytes 196616 | tf_op jit(solution)/shard_map/ppermute | solution.py:602
  (26 other events, 158.1 us)
